TPU v7x, 32 devices: a whole 2x2x4 slice. The times are simulated.
32 devices in a mesh: seq: 8 (over y, x, core), tp: 4 (over z).
Axes of the slice: x: 2, y: 2, z: 4, core: 2. Of those that a mesh axis runs over, the one named last changes fastest.
Arguments:
- tokens: bfloat16 [8192, 2048], P(('seq', 'tp')), may hold values from -6 to 6
- lengths: int32 [7], replicated, may hold values from 1 to 7296, as said below
- cotangent: bfloat16 [8192, 2048], P(('seq', 'tp')), may hold values from -6 to 6
- first_gain: float32 [2048], replicated, may hold values from 0.5 to 1.5
- query_weight: bfloat16 [2048, 2048], P(None, 'tp'), may hold values from -0.125 to 0.125
- forget_weight: bfloat16 [2048, 2048], P(None, 'tp'), may hold values from -0.125 to 0.125
- input_weight: bfloat16 [2048, 2048], P(None, 'tp'), may hold values from -0.125 to 0.125
- swish_weight: bfloat16 [2048, 2048], P(None, 'tp'), may hold values from -0.125 to 0.125
- bound_logit: float32 [16, 128], P('tp'), as said below
- group_gain: float32 [16, 128], P('tp'), may hold values from 0.5 to 1.5
- out_weight: bfloat16 [2048, 2048], P('tp'), may hold values from -0.125 to 0.125
- second_gain: float32 [2048], replicated, may hold values from 0.5 to 1.5
- gate_weight: bfloat16 [2048, 5632], P(None, 'tp'), may hold values from -0.125 to 0.125
- up_weight: bfloat16 [2048, 5632], P(None, 'tp'), may hold values from -0.125 to 0.125
- down_weight: bfloat16 [5632, 2048], P('tp'), may hold values from -0.078125 to 0.078125
Outputs:
- output: bfloat16 [8192, 2048], P(('seq', 'tp'))
- tokens_grad: float32 [8192, 2048], P(('seq', 'tp'))
- first_gain_grad: float32 [2048], P(('seq', 'tp'))
- query_grad: float32 [2048, 2048], P('seq', 'tp')
- forget_grad: float32 [2048, 2048], P('seq', 'tp')
- input_grad: float32 [2048, 2048], P('seq', 'tp')
- swish_grad: float32 [2048, 2048], P('seq', 'tp')
- bound_grad: float32 [16, 128], P('tp', 'seq')
- group_gain_grad: float32 [16, 128], P('tp', 'seq')
- out_grad: float32 [2048, 2048], P('tp', 'seq')
- second_gain_grad: float32 [2048], P(('seq', 'tp'))
- gate_grad: float32 [2048, 5632], P('seq', 'tp')
- up_grad: float32 [2048, 5632], P('seq', 'tp')
- down_grad: float32 [5632, 2048], P('tp', 'seq')
Inputs may be any that keep to these rules, and one draw needn't show every extreme that they name: lengths of the packed sequences in order; the fourth is the longest, their sum is under 8192, and rows from the sum on are padding. `bound_logit`: logits of the lower bounds, each at least 0 and under ln(16384).
All inputs are finite; a program needn't handle non-finite values.
Results may differ from a plain program's by a relative error of at most 0.014.
Values may be sent and summed in bfloat16 or wider, within the bound.
A program may use at most 256 MiB of HBM per device.

v0:
```python
from functools import partial

import jax
import jax.numpy as jnp
from jax import lax
from jax.sharding import PartitionSpec as P

BLOCK = 64


epsilon = 1e-05
highest = lax.Precision.HIGHEST


def entering(value, axis, combine, identity):
    size, here = (lax.axis_size(axis), lax.axis_index(axis))
    everything = jax.tree.map(lambda part: lax.all_gather(part, axis), value)
    start = jax.tree.map(
        lambda part, zero: jnp.broadcast_to(jnp.asarray(zero, part.dtype), part.shape),
        value,
        identity,
    )

    def lap(k, before):
        reached = k < here
        new = combine(before, jax.tree.map(lambda part: part[k], everything))
        return jax.tree.map(lambda a, b: jnp.where(reached, a, b), new, before)

    return lax.fori_loop(0, size, lap, start)


def entering_2(value, axis, combine, identity):
    size, here = (lax.axis_size(axis), lax.axis_index(axis))
    everything = jax.tree.map(
        lambda part, kind: lax.all_gather(part.astype(kind), axis),
        value,
        jax.tree.map(lambda a: jnp.bfloat16 if a.dtype == jnp.float32 else a.dtype, value),
    )
    start = jax.tree.map(
        lambda part, zero: jnp.broadcast_to(jnp.asarray(zero, part.dtype), part.shape),
        value,
        identity,
    )

    def lap(k, before):
        at = size - 1 - k
        reached = at > here
        new = combine(
            before, jax.tree.map(lambda part, own: part[at].astype(own.dtype), everything, value)
        )
        return jax.tree.map(lambda a, b: jnp.where(reached, a, b), new, before)

    return lax.fori_loop(0, size, lap, start)


def doc_layout(positions, lengths):
    seq_ends = jnp.cumsum(lengths)
    doc_ids = jnp.sum((positions[:, None] >= seq_ends[None, :]).astype(jnp.int32), axis=1)
    shifted = positions - 1
    earlier_ids = jnp.sum((shifted[:, None] >= seq_ends[None, :]).astype(jnp.int32), axis=1)
    prev_ids = jnp.where(shifted >= 0, earlier_ids, -1)
    valid_rows = (positions < seq_ends[-1]).astype(jnp.float32)
    return (doc_ids, prev_ids, valid_rows)


def rms_norm(rows_in, gain_vector):
    inv_scale = lax.rsqrt(jnp.mean(rows_in * rows_in, axis=-1, keepdims=True) + epsilon)
    return rows_in * inv_scale * gain_vector


def gate_values(query_pre, forget_pre, input_pre, bound_logit):
    lower_bound = jax.nn.sigmoid(bound_logit).reshape(-1)
    forget = lower_bound + (1.0 - lower_bound) * jax.nn.sigmoid(forget_pre)
    return (jax.nn.silu(query_pre), jnp.log(forget), 1.0 - forget, input_pre)


def group_out(valid_rows, recurrent_out, swish_pre, group_gain):
    head_count, head_width = group_gain.shape
    split_heads = recurrent_out.reshape(recurrent_out.shape[0], head_count, head_width)
    inv_scale = lax.rsqrt(jnp.mean(split_heads * split_heads, axis=-1, keepdims=True) + epsilon)
    normed = (split_heads * inv_scale * group_gain).reshape(recurrent_out.shape)
    return normed * jax.nn.silu(swish_pre) * valid_rows[:, None]


def swiglu_mix(gate_up):
    gate_rows, up_rows = jnp.split(gate_up, 2, axis=1)
    return jax.nn.silu(gate_rows) * up_rows


def block_run(queries, log_forget, key_rows, values, doc_ids, prev_ids, carried):
    head_count, head_width = (carried.shape[0], carried.shape[1])
    blocks = queries.shape[0] // BLOCK
    layout = (blocks, BLOCK, head_count, head_width)
    query_blocks = queries.reshape(layout)
    key_blocks = key_rows.reshape(layout)
    value_blocks = values.reshape(layout)
    cum_log = jnp.cumsum(log_forget.reshape(layout), axis=1)
    last_log = cum_log[:, -1]
    block_ids = doc_ids.reshape(blocks, BLOCK)
    before = prev_ids.reshape(blocks, BLOCK)[:, 0]
    query_decay = query_blocks * jnp.exp(cum_log)
    key_decay = key_blocks * jnp.exp(-cum_log)
    lower_mask = jnp.tril(jnp.ones((BLOCK, BLOCK), jnp.float32))
    same_doc = (block_ids[:, :, None] == block_ids[:, None, :]).astype(jnp.float32) * lower_mask
    scores = (
        jnp.einsum("nthd,nshd->nhts", query_decay, key_decay, precision=highest) * same_doc[:, None]
    )
    within = jnp.einsum("nhts,nshe->nthe", scores, value_blocks, precision=highest)
    carry_in = (block_ids == before[:, None]).astype(jnp.float32)
    tail_keep = (block_ids == block_ids[:, -1:]).astype(jnp.float32)
    key_tail = key_blocks * jnp.exp(last_log[:, None] - cum_log) * tail_keep[:, :, None, None]
    state_adds = jnp.einsum("nshd,nshe->nhde", key_tail, value_blocks, precision=highest)
    decays = jnp.exp(last_log) * carry_in[:, -1][:, None, None]

    def advance(state_now, pieces):
        return (pieces[0][:, :, None] * state_now + pieces[1], state_now)

    closing, starts = lax.scan(advance, carried, (decays, state_adds))
    across = jnp.einsum(
        "nthd,nhde->nthe", query_decay * carry_in[:, :, None, None], starts, precision=highest
    )
    return ((within + across).reshape(queries.shape), closing)


def reach_rows(queries, log_forget, doc_ids, first_prev):
    blocks = queries.shape[0] // BLOCK
    cum_log = jnp.cumsum(log_forget.reshape(blocks, BLOCK, -1), axis=1)
    totals = cum_log[:, -1]
    before = jnp.concatenate([jnp.zeros_like(totals[:1]), jnp.cumsum(totals, axis=0)[:-1]], axis=0)
    factor = jnp.exp(cum_log + before[:, None]).reshape(queries.shape)
    kept = (doc_ids == first_prev).astype(jnp.float32)
    return queries * factor * kept[:, None]


def mixer_local(doc_ids, prev_ids, query_pre, forget_pre, input_pre, bound_logit):
    queries, log_forget, key_rows, values = gate_values(
        query_pre, forget_pre, input_pre, bound_logit
    )
    head_count, head_width = bound_logit.shape
    empty_state = jnp.zeros((head_count, head_width, head_width), jnp.float32)
    own_part, state_adds = block_run(
        queries, log_forget, key_rows, values, doc_ids, prev_ids, empty_state
    )
    whole_doc = jnp.all(doc_ids == prev_ids[0]).astype(jnp.float32)
    decays = jnp.exp(jnp.sum(log_forget, axis=0)).reshape(head_count, head_width) * whole_doc
    entry_rows = reach_rows(queries, log_forget, doc_ids, prev_ids[0])
    return (own_part, state_adds, decays, entry_rows)


def combine_maps(earlier, latter):
    return (earlier[0] * latter[0], latter[0][:, :, None] * earlier[1] + latter[1])


def per_device(
    tokens,
    lengths,
    cotangent,
    first_gain,
    query_weight,
    forget_weight,
    input_weight,
    swish_weight,
    bound_logit,
    group_gain,
    out_weight,
    second_gain,
    gate_weight,
    up_weight,
    down_weight,
):
    input_rows = tokens.astype(jnp.float32)
    first_norm, first_back = jax.vjp(rms_norm, input_rows, first_gain)
    gathered = lax.all_gather(first_norm.astype(jnp.bfloat16), "tp", axis=0, tiled=True)
    group_rows = gathered.shape[0]
    positions = lax.axis_index("seq") * group_rows + jnp.arange(group_rows, dtype=jnp.int32)
    doc_ids, prev_ids, valid_rows = doc_layout(positions, lengths)
    mix_weights = jnp.concatenate([query_weight, forget_weight, input_weight, swish_weight], axis=1)
    projected = jnp.dot(gathered, mix_weights, preferred_element_type=jnp.float32)
    query_pre, forget_pre, input_pre, swish_pre = jnp.split(projected, 4, axis=1)
    pieces, mixer_back = jax.vjp(
        partial(mixer_local, doc_ids, prev_ids), query_pre, forget_pre, input_pre, bound_logit
    )
    own_part, state_adds, decays, entry_rows = pieces
    identity = (jnp.ones_like(decays), jnp.zeros_like(state_adds))
    arrived = entering((decays, state_adds), "seq", combine_maps, identity)[1]
    head_count, head_width = bound_logit.shape
    entry_heads = entry_rows.reshape(group_rows, head_count, head_width)
    carried_out = jnp.einsum("thd,hde->the", entry_heads, arrived, precision=highest)
    recurrent_out = own_part + carried_out.reshape(own_part.shape)
    gated, group_back = jax.vjp(
        partial(group_out, valid_rows), recurrent_out, swish_pre, group_gain
    )
    gated_low = gated.astype(jnp.bfloat16)
    piece = gated_low
    residual = input_rows + lax.psum_scatter(
        jnp.dot(piece, out_weight, preferred_element_type=jnp.float32),
        "tp",
        scatter_dimension=0,
        tiled=True,
    )
    second_norm, second_back = jax.vjp(rms_norm, residual, second_gain)
    ffn_rows = lax.all_gather(second_norm.astype(jnp.bfloat16), "tp", axis=0, tiled=True)
    glu_weights = jnp.concatenate([gate_weight, up_weight], axis=1)
    gate_up = jnp.dot(ffn_rows, glu_weights, preferred_element_type=jnp.float32)
    hidden, glu_back = jax.vjp(swiglu_mix, gate_up)
    hidden_low = hidden.astype(jnp.bfloat16)
    piece = hidden_low
    result = residual + lax.psum_scatter(
        jnp.dot(piece, down_weight, preferred_element_type=jnp.float32).astype(jnp.bfloat16),
        "tp",
        scatter_dimension=0,
        tiled=True,
    ).astype(jnp.float32)
    output = result.astype(jnp.bfloat16)
    cot_rows = lax.all_gather(cotangent, "tp", axis=0, tiled=True)
    down_grad = jnp.dot(hidden_low.T, cot_rows, preferred_element_type=jnp.float32)
    hidden_grad = jnp.dot(cot_rows, down_weight.T, preferred_element_type=jnp.float32)
    gate_up_grad = glu_back(hidden_grad)[0].astype(jnp.bfloat16)
    glu_grad = jnp.dot(ffn_rows.T, gate_up_grad, preferred_element_type=jnp.float32)
    gate_grad, up_grad = jnp.split(glu_grad, 2, axis=1)
    piece = gate_up_grad
    second_norm_grad = lax.psum_scatter(
        jnp.dot(piece, glu_weights.T, preferred_element_type=jnp.float32),
        "tp",
        scatter_dimension=0,
        tiled=True,
    )
    residual_norm_grad, second_gain_grad = second_back(second_norm_grad)
    residual_grad = cotangent.astype(jnp.float32) + residual_norm_grad
    branch_rows = lax.all_gather(residual_grad.astype(jnp.bfloat16), "tp", axis=0, tiled=True)
    out_grad = jnp.dot(gated_low.T, branch_rows, preferred_element_type=jnp.float32)
    gated_grad = jnp.dot(branch_rows, out_weight.T, preferred_element_type=jnp.float32)
    recurrent_grad, swish_back, group_gain_grad = group_back(gated_grad)
    recurrent_heads = recurrent_grad.reshape(group_rows, head_count, head_width)
    pulled = jnp.einsum("thd,the->hde", entry_heads, recurrent_heads, precision=highest)
    later_grad = entering_2((decays, pulled), "seq", combine_maps, identity)[1]
    entry_grad = jnp.einsum("the,hde->thd", recurrent_heads, arrived, precision=highest).reshape(
        entry_rows.shape
    )
    decay_grad = jnp.sum(later_grad * arrived, axis=-1)
    query_back, forget_back, input_back, bound_grad = mixer_back(
        (recurrent_grad, later_grad, decay_grad, entry_grad)
    )
    pre_grad = jnp.concatenate([query_back, forget_back, input_back, swish_back], axis=1).astype(
        jnp.bfloat16
    )
    mix_grad = jnp.dot(gathered.T, pre_grad, preferred_element_type=jnp.float32)
    piece = pre_grad
    first_norm_grad = lax.psum_scatter(
        jnp.dot(piece, mix_weights.T, preferred_element_type=jnp.float32).astype(jnp.bfloat16),
        "tp",
        scatter_dimension=0,
        tiled=True,
    ).astype(jnp.float32)
    input_norm_grad, first_gain_grad = first_back(first_norm_grad)
    tokens_grad = residual_grad + input_norm_grad
    query_grad, forget_grad, input_grad, swish_grad = jnp.split(mix_grad, 4, axis=1)
    (
        query_grad,
        forget_grad,
        input_grad,
        swish_grad,
        bound_grad,
        group_gain_grad,
        out_grad,
        gate_grad,
        up_grad,
        down_grad,
    ) = (
        lax.psum_scatter(query_grad, "seq", scatter_dimension=0, tiled=True),
        lax.psum_scatter(forget_grad, "seq", scatter_dimension=0, tiled=True),
        lax.psum_scatter(input_grad, "seq", scatter_dimension=0, tiled=True),
        lax.psum_scatter(swish_grad, "seq", scatter_dimension=0, tiled=True),
        lax.psum_scatter(bound_grad, "seq", scatter_dimension=1, tiled=True),
        lax.psum_scatter(group_gain_grad, "seq", scatter_dimension=1, tiled=True),
        lax.psum_scatter(out_grad, "seq", scatter_dimension=1, tiled=True),
        lax.psum_scatter(gate_grad, "seq", scatter_dimension=0, tiled=True),
        lax.psum_scatter(up_grad, "seq", scatter_dimension=0, tiled=True),
        lax.psum_scatter(down_grad, "seq", scatter_dimension=1, tiled=True),
    )
    first_gain_grad, second_gain_grad = (
        lax.psum_scatter(first_gain_grad, ("seq", "tp"), scatter_dimension=0, tiled=True),
        lax.psum_scatter(second_gain_grad, ("seq", "tp"), scatter_dimension=0, tiled=True),
    )
    return (
        output,
        tokens_grad,
        first_gain_grad,
        query_grad,
        forget_grad,
        input_grad,
        swish_grad,
        bound_grad,
        group_gain_grad,
        out_grad,
        second_gain_grad,
        gate_grad,
        up_grad,
        down_grad,
    )


def solution(mesh):
    in_specs = (
        P(("seq", "tp"), None),
        P(),
        P(("seq", "tp"), None),
        P(),
        P(None, "tp"),
        P(None, "tp"),
        P(None, "tp"),
        P(None, "tp"),
        P("tp", None),
        P("tp", None),
        P("tp", None),
        P(),
        P(None, "tp"),
        P(None, "tp"),
        P("tp", None),
    )
    out_specs = (
        P(("seq", "tp"), None),
        P(("seq", "tp"), None),
        P(("seq", "tp")),
        P("seq", "tp"),
        P("seq", "tp"),
        P("seq", "tp"),
        P("seq", "tp"),
        P("tp", "seq"),
        P("tp", "seq"),
        P("tp", "seq"),
        P(("seq", "tp")),
        P("seq", "tp"),
        P("seq", "tp"),
        P("tp", "seq"),
    )
    return jax.shard_map(
        per_device, mesh=mesh, in_specs=in_specs, out_specs=out_specs, check_vma=False
    )
```

profile of v0, /device:TPU:0, one launch (start us, length us, event | category | flops | bytes accessed | tf_op | source)
XLA Modules:
  0.0 1733.6 jit_solution(177883630952219363)
XLA Ops:
  14.9 3.2 constant_dynamic-update-slice_fusion.3
  24.5 71.7 %all-gather.9.cloned.1.call-done = bf16[1024,2048]{1,0:T(8,128)(2,1)} async-done(((bf16[256,2048]{1,0:T(8,128)(2,1)}), bf16[1024,2048]{1,0:T(8,128)(2,1)}) %all-gather.9.cloned.1.call-update) | async-done | bytes 4194320 | tf_op jit(solution)/shard_map/all_gather | solution.py:173
  96.2 12.5 fusion.119
  108.7 3.3 copy-done.27
  127.0 6.3 fusion.39
  139.3 12.2 fusion.72
  154.1 30.2 %while.64 = (s32[]{:T(128)}, f32[4,128,128]{2,1,0:T(8,128)S(1)}, f32[16,4,128,128]{3,2,1,0:T(8,128)}, f32[16,4,128,1]{2,1,3,0:T(4,128)S(1)}, f32[16,4,128]{2,1,0...) while((s32[]{:T(128)}, f32[4,128,128]{2,1,0:T(8,128)S(1)}, ...), condition=%wide.region_6.7_spmd.clone, body=%wide.region_5.6_spmd.clone.sunk | while | flops 262147 | bytes 1321080 | solution.py:118
  187.8 3.1 reshape.316
  190.9 3.3 copy_multiply_fusion.1
  194.5 4.2 fusion.93
  198.7 4.0 fusion.57
  206.6 3.3 copy.220
  212.9 8.9 all_gather.33
  221.8 9.5 while.65
  231.3 4.3 multiply_reduce_fusion.6
  237.7 3.1 copy.255
  244.6 5.7 fusion.120
  250.3 142.4 %reduce-scatter.19.cloned.1.call-done = f32[256,2048]{1,0:T(8,128)} async-done(((f32[1024,2048]{1,0:T(8,128)}), f32[256,2048]{1,0:T(8,128)}) %reduce-scatter.19.cloned.1.call-update) | async-done | bytes 2097168 | tf_op jit(solution)/shard_map/reduce_scatter | solution.py:195
  397.8 5.5 constant_dynamic-update-slice_fusion.5
  403.3 6.1 constant_dynamic-update-slice_fusion.4
  409.4 69.4 %all-gather.11.cloned.1.call-done = bf16[1024,2048]{1,0:T(8,128)(2,1)} async-done(((bf16[256,2048]{1,0:T(8,128)(2,1)}), bf16[1024,2048]{1,0:T(8,128)(2,1)}) %all-gather.11.cloned.1.call-update) | async-done | bytes 4194320 | tf_op jit(solution)/shard_map/all_gather | solution.py:202
  478.8 18.9 %fusion.121 = f32[1024,2816]{1,0:T(8,128)} fusion(bf16[1024,2048]{1,0:T(8,128)(2,1)} %all-gather.11.cloned.1.call-done, bf16[2048,2816]{1,0:T(8,128)(2,1)} %constant_dynamic-update-slice_fusion.4), kind=kOutput, calls=%fused_computation.226 | convolution fusion | flops 11811160064 | bytes 27262976 | tf_op jit(solution)/shard_map/dot_general | solution.py:204
  497.7 61.8 %all-gather.13.cloned.1.call-done = bf16[1024,2048]{1,0:T(8,128)(2,1)} async-done(((bf16[256,2048]{1,0:T(8,128)(2,1)}), bf16[1024,2048]{1,0:T(8,128)(2,1)}) %all-gather.13.cloned.1.call-update) | async-done | bytes 4194320 | tf_op jit(solution)/shard_map/all_gather | solution.py:215
  559.5 16.3 fusion.5
  578.4 16.9 fusion.8
  595.4 143.1 %reduce-scatter.23.cloned.1.call-done = f32[256,2048]{1,0:T(8,128)} async-done(((f32[1024,2048]{1,0:T(8,128)}), f32[256,2048]{1,0:T(8,128)}) %reduce-scatter.23.cloned.1.call-update) | async-done | bytes 2097168 | tf_op jit(solution)/shard_map/reduce_scatter | solution.py:222
  738.5 3.5 multiply_reduce_fusion
  744.4 9.1 all_gather.39
  753.5 72.5 %all-gather.15.cloned.1.call-done = bf16[1024,2048]{1,0:T(8,128)(2,1)} async-done(((bf16[256,2048]{1,0:T(8,128)(2,1)}), bf16[1024,2048]{1,0:T(8,128)(2,1)}) %all-gather.15.cloned.1.call-update) | async-done | bytes 4194320 | tf_op jit(solution)/shard_map/all_gather | solution.py:230
  826.0 8.2 multiply_multiply_fusion.2
  834.2 3.1 copy.261
  845.0 5.1 convolution_convert_fusion.2
  850.2 6.5 fusion.65
  856.7 3.3 fusion.122
  860.0 3.5 copy.256
  864.2 6.6 fusion.59
  870.8 8.5 fusion.55
  882.3 9.6 multiply_add_fusion
  892.0 9.5 while.66
  904.2 32.9 %while.63 = (s32[]{:T(128)}, f32[4,128,128]{2,1,0:T(8,128)S(1)}, f32[16,4,128]{2,1,0:T(4,128)S(1)}, f32[16,4,128,128]{3,2,1,0:T(8,128)}, f32[16,4,128,128]{3,2,1...) while((s32[]{:T(128)}, f32[4,128,128]{2,1,0:T(8,128)S(1)}, ...), condition=%wide.region_24.25_spmd, body=%wide.region_22.24_spmd.sunk | while | flops 261635 | bytes 1585281 | solution.py:118
  937.2 13.3 fusion.84
  950.6 5.7 fusion.83
  956.4 7.9 fusion.31
  975.0 3.4 fusion.46
  985.3 13.2 convolution_convert_fusion
  998.7 11.0 convolution_convert_fusion.1
  1009.7 20.3 %fusion.7 = f32[2048,2816]{1,0:T(8,128)} fusion(bf16[1024,2048]{1,0:T(8,128)(2,1)} %all-gather.11.cloned.1.call-done, bf16[1024,1408]{1,0:T(8,128)(2,1)} %copy-done.87, bf16[1024,1408]{1,0:T(8,128)(2,1)} %copy-done.86), kind=kOutput, calls=%fused_computation.33 | convolution fusion | flops 11822694400 | bytes 33030144 | tf_op jit(solution)/shard_map/dot_general | solution.py:219
  1030.0 17.0 fusion.116
  1047.6 11.4 fusion.124
  1060.2 6.6 fusion.123
  1068.1 11.5 fusion.92
  1079.5 6.1 fusion.117
  1090.4 5.9 reduce-scatter.25.cloned.1.call-done
  1098.6 46.2 %all-reduce.5 = (f32[2048]{0:T(1024)S(1)}, f32[2048]{0:T(1024)S(1)}) all-reduce(f32[2048]{0:T(1024)S(1)} %get-tuple-element.486, f32[2048]{0:T(1024)S(1)} %copy-done.67), channel_id=8, replica_groups=mesh['seq'=8,'tp'=4] {'seq','tp'}, use_global_device_ids=true, to_apply=%region_34.35.clone | all-reduce | flops 4096 | bytes 32768
  1146.0 30.9 %reduce-scatter.21.cloned.1.call-done = bf16[256,2048]{1,0:T(8,128)(2,1)} async-done(((bf16[1024,2048]{1,0:T(8,128)(2,1)}), bf16[256,2048]{1,0:T(8,128)(2,1)}) %reduce-scatter.21.cloned.1.call-update) | async-done | bytes 1048592 | tf_op jit(solution)/shard_map/reduce_scatter | solution.py:208
  1176.9 6.0 fusion.22
  1183.0 85.4 %reduce-scatter.37.cloned.1.call-done = f32[256,1408]{1,0:T(8,128)} async-done(((f32[2048,1408]{1,0:T(8,128)}), f32[256,1408]{1,0:T(8,128)}) %reduce-scatter.37.cloned.1.call-update) | async-done | bytes 1441808 | tf_op jit(solution)/shard_map/reduce_scatter | solution.py:277
  1268.3 90.8 %reduce-scatter.39.cloned.1.call-done = f32[256,1408]{1,0:T(8,128)} async-done(((f32[2048,1408]{1,0:T(8,128)}), f32[256,1408]{1,0:T(8,128)}) %reduce-scatter.39.cloned.1.call-update) | async-done | bytes 1441808 | tf_op jit(solution)/shard_map/reduce_scatter | solution.py:278
  1359.1 90.7 %reduce-scatter.41.cloned.1.call-done = f32[1408,256]{1,0:T(8,128)} async-done(((f32[1408,2048]{1,0:T(8,128)}), f32[1408,256]{1,0:T(8,128)}) %reduce-scatter.41.cloned.1.call-update) | async-done | bytes 1441808 | tf_op jit(solution)/shard_map/reduce_scatter | solution.py:279
  1449.8 55.1 %reduce-scatter.35.cloned.1.call-done = f32[512,256]{1,0:T(8,128)} async-done(((f32[512,2048]{1,0:T(8,128)}), f32[512,256]{1,0:T(8,128)}) %reduce-scatter.35.cloned.1.call-update) | async-done | bytes 524304 | tf_op jit(solution)/shard_map/reduce_scatter | solution.py:276
  1504.9 55.5 %reduce-scatter.27.cloned.1.call-done = f32[256,512]{1,0:T(8,128)} async-done(((f32[2048,512]{1,0:T(8,128)}), f32[256,512]{1,0:T(8,128)}) %reduce-scatter.27.cloned.1.call-update) | async-done | bytes 524304 | tf_op jit(solution)/shard_map/reduce_scatter | solution.py:270
  1560.5 55.1 %reduce-scatter.29.cloned.1.call-done = f32[256,512]{1,0:T(8,128)} async-done(((f32[2048,512]{1,0:T(8,128)}), f32[256,512]{1,0:T(8,128)}) %reduce-scatter.29.cloned.1.call-update) | async-done | bytes 524304 | tf_op jit(solution)/shard_map/reduce_scatter | solution.py:271
  1615.6 55.7 %reduce-scatter.31.cloned.1.call-done = f32[256,512]{1,0:T(8,128)} async-done(((f32[2048,512]{1,0:T(8,128)}), f32[256,512]{1,0:T(8,128)}) %reduce-scatter.31.cloned.1.call-update) | async-done | bytes 524304 | tf_op jit(solution)/shard_map/reduce_scatter | solution.py:272
  1671.3 55.1 %reduce-scatter.33.cloned.1.call-done = f32[256,512]{1,0:T(8,128)} async-done(((f32[2048,512]{1,0:T(8,128)}), f32[256,512]{1,0:T(8,128)}) %reduce-scatter.33.cloned.1.call-update) | async-done | bytes 524304 | tf_op jit(solution)/shard_map/reduce_scatter | solution.py:273
  (474 shorter events, 186.7 us)
Async XLA Ops:
  7.2 237.4 %copy-start = (bf16[512,2048]{1,0:T(8,128)(2,1)S(1)}, bf16[512,2048]{1,0:T(8,128)(2,1)}, u32[]{:S(2)}) copy-start(bf16[512,2048]{1,0:T(8,128)(2,1)} %param.33) | copy-start | bytes 6291460
  7.2 5.4 copy-start.85
  7.2 7.0 copy-start.75
  7.2 89.0 %all-gather.9.cloned.1.call-start = ((), (), s32[]{:S(2)}) async-start(), calls=%async_computation.14 | async-start | bytes 5242880 | tf_op jit(solution)/shard_map/all_gather | solution.py:173
  12.6 209.2 %all-gather.17.cloned.1.call-start = ((), (), s32[]{:S(2)}) async-start(), calls=%async_computation.30 | async-start | bytes 2359296 | tf_op jit(solution)/shard_map/all_gather | solution.py:17
  14.0 125.3 %copy-start.58 = (f32[16,64]{1,0:T(8,128)}, f32[16,64]{1,0:T(8,128)S(1)}, u32[]{:S(2)}) copy-start(f32[16,64]{1,0:T(8,128)S(1)} %get-tuple-element.571) | copy-start | bytes 12292
  14.2 105.7 %copy-start.83 = (f32[16]{0:T(128)}, f32[16]{0:T(128)S(1)}, u32[]{:S(2)}) copy-start(f32[16]{0:T(128)S(1)} %slice_reduce_fusion.1) | copy-start | bytes 196
  14.2 94.5 %copy-start.65 = (f32[512]{0:T(512)}, f32[512]{0:T(512)S(1)}, u32[]{:S(2)}) copy-start(f32[512]{0:T(512)S(1)} %broadcast_subtract_fusion) | copy-start | bytes 6148
  14.2 94.5 %copy-start.70 = (f32[512]{0:T(512)}, f32[512]{0:T(512)S(1)}, u32[]{:S(2)}) copy-start(f32[512]{0:T(512)S(1)} %fusion.109) | copy-start | bytes 6148
  14.9 112.1 %copy-start.63 = (f32[1024]{0:T(1024)}, f32[1024]{0:T(1024)S(1)}, u32[]{:S(2)}) copy-start(f32[1024]{0:T(1024)S(1)} %get-tuple-element.543) | copy-start | bytes 12292
  114.9 98.0 %copy-start.72 = (f32[512]{0:T(512)}, f32[512]{0:T(512)S(1)}, u32[]{:S(2)}) copy-start(f32[512]{0:T(512)S(1)} %get-tuple-element.545) | copy-start | bytes 6148
  119.8 19.5 %copy-start.52 = (f32[16,1,4,128]{3,2,0,1:T(4,128)}, f32[16,1,4,128]{3,2,0,1:T(4,128)S(1)}, u32[]{:S(2)}) copy-start(f32[16,1,4,128]{3,2,0,1:T(4,128)S(1)} %copy.359) | copy-start | bytes 98308
  127.0 6.3 copy-start.38
  185.0 207.7 %reduce-scatter.19.cloned.1.call-start = ((), (), s32[]{:S(2)}) async-start(), calls=%async_computation.15 | async-start | bytes 10485760 | tf_op jit(solution)/shard_map/reduce_scatter | solution.py:195
  187.8 15.0 copy-start.40
  250.2 142.4 %copy-start.25 = (bf16[256,2048]{1,0:T(8,128)(2,1)S(1)}, bf16[256,2048]{1,0:T(8,128)(2,1)}, u32[]{:S(2)}) copy-start(bf16[256,2048]{1,0:T(8,128)(2,1)} %param.23) | copy-start | bytes 3145732
  250.2 145.7 %copy-start.60 = (f32[2048]{0:T(1024)S(1)}, f32[2048]{0:T(1024)}, u32[]{:S(2)}) copy-start(f32[2048]{0:T(1024)} %param.34) | copy-start | bytes 24580
  250.3 228.5 %all-gather.11.cloned.1.call-start = ((), (), s32[]{:S(2)}) async-start(), calls=%async_computation.16 | async-start | bytes 5242880 | tf_op jit(solution)/shard_map/all_gather | solution.py:202
  394.6 347.4 %copy-start.68 = (f32[256]{0:T(256)}, f32[256]{0:T(256)S(1)}, u32[]{:S(2)}) copy-start(f32[256]{0:T(256)S(1)} %fusion.103) | copy-start | bytes 3076
  397.1 162.4 %all-gather.13.cloned.1.call-start = ((), (), s32[]{:S(2)}) async-start(), calls=%async_computation.18 | async-start | bytes 5242880 | tf_op jit(solution)/shard_map/all_gather | solution.py:215
  397.7 340.8 %reduce-scatter.23.cloned.1.call-start = ((), (), s32[]{:S(2)}) async-start(), calls=%async_computation.19 | async-start | bytes 10485760 | tf_op jit(solution)/shard_map/reduce_scatter | solution.py:222
  595.3 147.3 %copy-start.42 = (bf16[256,2048]{1,0:T(8,128)(2,1)S(1)}, bf16[256,2048]{1,0:T(8,128)(2,1)}, u32[]{:S(2)}) copy-start(bf16[256,2048]{1,0:T(8,128)(2,1)} %param.25) | copy-start | bytes 3145732
  595.4 230.7 %all-gather.15.cloned.1.call-start = ((), (), s32[]{:S(2)}) async-start(), calls=%async_computation.20 | async-start | bytes 5242880 | tf_op jit(solution)/shard_map/all_gather | solution.py:230
  744.4 147.6 %all-gather.19.cloned.1.call-start = ((), (), s32[]{:S(2)}) async-start(), calls=%async_computation.31 | async-start | bytes 1179648 | tf_op jit(solution)/shard_map/all_gather | solution.py:35
  850.1 237.5 %reduce-scatter.45.cloned.1.call-start = ((), (), s32[]{:S(2)}) async-start(), calls=%async_computation.33 | async-start | bytes 73728
  850.2 6.5 copy-start.22
  864.2 6.6 copy-start.9
  864.2 6.6 copy-start.14
  870.7 8.6 copy-start.4
  870.7 8.6 copy-start.6
  870.7 8.6 copy-start.30
  891.9 197.1 %reduce-scatter.43.cloned.1.call-start = ((), (), s32[]{:S(2)}) async-start(), calls=%async_computation.32 | async-start | bytes 73728
  904.2 33.0 %copy-start.53 = (f32[16,1,4,128]{3,2,0,1:T(4,128)S(1)}, f32[16,1,4,128]{3,2,0,1:T(4,128)}, u32[]{:S(2)}) copy-start(f32[16,1,4,128]{3,2,0,1:T(4,128)} %copy-done.52) | copy-start | bytes 98308
  904.2 33.0 %copy-start.59 = (f32[16,64]{1,0:T(8,128)S(1)}, f32[16,64]{1,0:T(8,128)}, u32[]{:S(2)}) copy-start(f32[16,64]{1,0:T(8,128)} %copy-done.58) | copy-start | bytes 12292
  937.2 13.3 copy-start.7
  937.2 13.3 copy-start.19
  937.2 13.3 copy-start.43
  950.5 5.7 copy-start.55
  950.5 5.7 copy-start.84
  950.5 5.8 copy-start.10
  950.6 5.8 copy-start.31
  950.6 5.8 copy-start.32
  950.6 19.6 %slice-start = ((s8[8388608]{0:T(1024)(128)(4,1)}), s8[4194304]{0:T(1024)(128)(4,1)S(1)}, s32[]{:S(2)}) async-start(s8[8388608]{0:T(1024)(128)(4,1)} %bitcast.219), calls=%async_computation.34 | async-start | bytes 8388608
  956.4 13.8 slice-start.1
  964.3 5.8 copy-start.64
  985.3 111.0 %reduce-scatter.25.cloned.1.call-start = ((), (), s32[]{:S(2)}) async-start(), calls=%async_computation.21 | async-start | bytes 5242880 | tf_op jit(solution)/shard_map/reduce_scatter | solution.py:249
  998.6 178.3 %reduce-scatter.21.cloned.1.call-start = ((), (), s32[]{:S(2)}) async-start(), calls=%async_computation.17 | async-start | bytes 5242880 | tf_op jit(solution)/shard_map/reduce_scatter | solution.py:208
  1009.7 258.7 %reduce-scatter.37.cloned.1.call-start = ((), (), s32[]{:S(2)}) async-start(), calls=%async_computation.27 | async-start | bytes 12976128 | tf_op jit(solution)/shard_map/reduce_scatter | solution.py:277
  1047.0 312.1 %reduce-scatter.39.cloned.1.call-start = ((), (), s32[]{:S(2)}) async-start(), calls=%async_computation.28 | async-start | bytes 12976128 | tf_op jit(solution)/shard_map/reduce_scatter | solution.py:278
  1047.6 402.3 %reduce-scatter.41.cloned.1.call-start = ((), (), s32[]{:S(2)}) async-start(), calls=%async_computation.29 | async-start | bytes 12976128 | tf_op jit(solution)/shard_map/reduce_scatter | solution.py:279
  1059.0 445.9 %reduce-scatter.35.cloned.1.call-start = ((), (), s32[]{:S(2)}) async-start(), calls=%async_computation.26 | async-start | bytes 4718592 | tf_op jit(solution)/shard_map/reduce_scatter | solution.py:276
  1066.9 493.6 %reduce-scatter.27.cloned.1.call-start = ((), (), s32[]{:S(2)}) async-start(), calls=%async_computation.22 | async-start | bytes 4718592 | tf_op jit(solution)/shard_map/reduce_scatter | solution.py:270
  1085.7 529.9 %reduce-scatter.29.cloned.1.call-start = ((), (), s32[]{:S(2)}) async-start(), calls=%async_computation.23 | async-start | bytes 4718592 | tf_op jit(solution)/shard_map/reduce_scatter | solution.py:271
  1086.2 585.0 %reduce-scatter.31.cloned.1.call-start = ((), (), s32[]{:S(2)}) async-start(), calls=%async_computation.24 | async-start | bytes 4718592 | tf_op jit(solution)/shard_map/reduce_scatter | solution.py:272
  1087.0 639.4 %reduce-scatter.33.cloned.1.call-start = ((), (), s32[]{:S(2)}) async-start(), calls=%async_computation.25 | async-start | bytes 4718592 | tf_op jit(solution)/shard_map/reduce_scatter | solution.py:273
  1087.0 9.3 copy-start.26
  1087.1 9.3 copy-start.62
  1087.1 9.2 copy-start.78
  1087.6 11.0 copy-start.67
  1087.6 58.4 %copy-start.80 = (f32[256]{0:T(256)S(1)}, f32[256]{0:T(256)}, u32[]{:S(2)}) copy-start(f32[256]{0:T(256)} %copy-done.79) | copy-start | bytes 3076
  1087.6 89.3 %copy-start.61 = (f32[2048]{0:T(1024)S(1)}, f32[2048]{0:T(1024)}, u32[]{:S(2)}) copy-start(f32[2048]{0:T(1024)} %param.34) | copy-start | bytes 24580
  1087.6 89.3 %copy-start.69 = (f32[256]{0:T(256)S(1)}, f32[256]{0:T(256)}, u32[]{:S(2)}) copy-start(f32[256]{0:T(256)} %copy-done.68) | copy-start | bytes 3076
  1087.6 89.3 %copy-start.82 = (f32[256]{0:T(256)S(1)}, f32[256]{0:T(256)}, u32[]{:S(2)}) copy-start(f32[256]{0:T(256)} %copy-done.81) | copy-start | bytes 3076
  1176.9 549.5 %copy-start.1 = (bf16[512,2048]{1,0:T(8,128)(2,1)S(1)}, bf16[512,2048]{1,0:T(8,128)(2,1)}, u32[]{:S(2)}) copy-start(bf16[512,2048]{1,0:T(8,128)(2,1)} %param.33) | copy-start | bytes 6291460
  (46 other events, 111.6 us)
Sparse Core Ops, SparseCore 0:
  12.7 83.4 all-gather.8
  185.1 26.4 all-gather.16
  250.4 142.2 reduce-scatter.18
  397.3 81.4 all-gather.10
  480.2 79.2 all-gather.12
  595.5 142.9 reduce-scatter.22
  744.5 81.4 all-gather.14
  850.2 22.0 all-gather.18
  892.0 31.7 reduce-scatter.44
  985.4 31.7 reduce-scatter.42
  1019.5 76.7 reduce-scatter.24
  1098.6 78.2 reduce-scatter.20
  1181.0 87.3 reduce-scatter.36
  1272.2 86.7 reduce-scatter.38
  1363.0 86.7 reduce-scatter.40
  1453.6 51.2 reduce-scatter.34
  1509.1 51.3 reduce-scatter.26
  1564.3 51.2 reduce-scatter.28
  1619.9 51.3 reduce-scatter.30
  1675.0 51.2 reduce-scatter.32
where the time goes:
time: 1740 us; the launch traced here: 1730 us
  waiting for transfers between devices  1140 us (66%)
  matrix products  249 us (14%)
  other arithmetic  131 us (8%)
  local copies, waits for them, and re-layouts  126 us (7%)
  blocking collectives  64.2 us (4%)
    reduce_scatter x1, waiting for transfers between devices, per_device(): lax.psum_scatter(jnp.dot(piece, glu_weights.T, preferred_element_type=jnp...  143 us
    reduce_scatter x1, waiting for transfers between devices, per_device(): lax.psum_scatter(jnp.dot(piece, out_weight, preferred_element_type=jnp.fl...  142 us
    reduce_scatter x1, waiting for transfers between devices, per_device(): lax.psum_scatter(up_grad, 'seq', scatter_dimension=0, tiled=True)  90.8 us
    reduce_scatter x1, waiting for transfers between devices, per_device(): lax.psum_scatter(down_grad, 'seq', scatter_dimension=1, tiled=True)  90.7 us
    reduce_scatter x1, waiting for transfers between devices, per_device(): lax.psum_scatter(gate_grad, 'seq', scatter_dimension=0, tiled=True)  85.4 us
    all_gather x1, waiting for transfers between devices, per_device(): lax.all_gather(residual_grad.astype(jnp.bfloat16), 'tp', axis=0, tiled=True)  72.5 us
    all_gather x1, waiting for transfers between devices, per_device(): lax.all_gather(first_norm.astype(jnp.bfloat16), 'tp', axis=0, tiled=True)  71.7 us
    all_gather x1, waiting for transfers between devices, per_device(): lax.all_gather(second_norm.astype(jnp.bfloat16), 'tp', axis=0, tiled=True)  69.4 us
  transfers between devices with their start and end apart: 20, of which 16 were waited for; matrix products, arithmetic and copies ran while one was open for 18% of the time, Pallas kernels for 0%

commit v1 on v0

--- a/solution.py
+++ b/solution.py
@@ -51,6 +51,12 @@
         return jax.tree.map(lambda a, b: jnp.where(reached, a, b), new, before)
 
     return lax.fori_loop(0, size, lap, start)
+
+
+def sum_groups(part, dimension):
+    low = part.astype(jnp.bfloat16)
+    total = lax.psum_scatter(low, "seq", scatter_dimension=dimension, tiled=True)
+    return total.astype(jnp.float32)
 
 
 def doc_layout(positions, lengths):
@@ -193,11 +199,11 @@
     gated_low = gated.astype(jnp.bfloat16)
     piece = gated_low
     residual = input_rows + lax.psum_scatter(
-        jnp.dot(piece, out_weight, preferred_element_type=jnp.float32),
+        jnp.dot(piece, out_weight, preferred_element_type=jnp.float32).astype(jnp.bfloat16),
         "tp",
         scatter_dimension=0,
         tiled=True,
-    )
+    ).astype(jnp.float32)
     second_norm, second_back = jax.vjp(rms_norm, residual, second_gain)
     ffn_rows = lax.all_gather(second_norm.astype(jnp.bfloat16), "tp", axis=0, tiled=True)
     glu_weights = jnp.concatenate([gate_weight, up_weight], axis=1)
@@ -220,11 +226,11 @@
     gate_grad, up_grad = jnp.split(glu_grad, 2, axis=1)
     piece = gate_up_grad
     second_norm_grad = lax.psum_scatter(
-        jnp.dot(piece, glu_weights.T, preferred_element_type=jnp.float32),
+        jnp.dot(piece, glu_weights.T, preferred_element_type=jnp.float32).astype(jnp.bfloat16),
         "tp",
         scatter_dimension=0,
         tiled=True,
-    )
+    ).astype(jnp.float32)
     residual_norm_grad, second_gain_grad = second_back(second_norm_grad)
     residual_grad = cotangent.astype(jnp.float32) + residual_norm_grad
     branch_rows = lax.all_gather(residual_grad.astype(jnp.bfloat16), "tp", axis=0, tiled=True)
@@ -267,16 +273,16 @@
         up_grad,
         down_grad,
     ) = (
-        lax.psum_scatter(query_grad, "seq", scatter_dimension=0, tiled=True),
-        lax.psum_scatter(forget_grad, "seq", scatter_dimension=0, tiled=True),
-        lax.psum_scatter(input_grad, "seq", scatter_dimension=0, tiled=True),
-        lax.psum_scatter(swish_grad, "seq", scatter_dimension=0, tiled=True),
+        sum_groups(query_grad, 0),
+        sum_groups(forget_grad, 0),
+        sum_groups(input_grad, 0),
+        sum_groups(swish_grad, 0),
         lax.psum_scatter(bound_grad, "seq", scatter_dimension=1, tiled=True),
         lax.psum_scatter(group_gain_grad, "seq", scatter_dimension=1, tiled=True),
-        lax.psum_scatter(out_grad, "seq", scatter_dimension=1, tiled=True),
-        lax.psum_scatter(gate_grad, "seq", scatter_dimension=0, tiled=True),
-        lax.psum_scatter(up_grad, "seq", scatter_dimension=0, tiled=True),
-        lax.psum_scatter(down_grad, "seq", scatter_dimension=1, tiled=True),
+        sum_groups(out_grad, 1),
+        sum_groups(gate_grad, 0),
+        sum_groups(up_grad, 0),
+        sum_groups(down_grad, 1),
     )
     first_gain_grad, second_gain_grad = (
         lax.psum_scatter(first_gain_grad, ("seq", "tp"), scatter_dimension=0, tiled=True),

time: 1740 us -> 1400 us (0.80)
  waiting for transfers between devices: 1140 us -> 784 us
  other arithmetic: 131 us -> 150 us
    reduce_scatter x8, waiting for transfers between devices: 543 us -> 215 us  [sum_groups(): lax.psum_scatter(low, 'seq', scatter_dimension=dimension, tiled=True)]
    reduce_scatter x1, waiting for transfers between devices: 5.94 us -> 77.3 us  [per_device(): lax.psum_scatter(jnp.dot(piece, mix_weights.T, preferred_element_type=jnp...]
    reduce_scatter x1, waiting for transfers between devices: 143 us -> 75.2 us  [per_device(): lax.psum_scatter(jnp.dot(piece, glu_weights.T, preferred_element_type=jnp...]
    reduce_scatter x1, waiting for transfers between devices: 142 us -> 74.6 us  [per_device(): lax.psum_scatter(jnp.dot(piece, out_weight, preferred_element_type=jnp.fl...]
    unnamed x22, waiting for transfers between devices: 3.04 us -> 26.9 us
  transfers between devices with their start and end apart: 20 -> 20, of which waited for: 16 -> 14; matrix products, arithmetic and copies ran while one was open for 18% -> 23% of each run, Pallas kernels for 0% -> 0%
where the time goes in v1:
time: 1400 us; the launch traced here: 1390 us
  waiting for transfers between devices  784 us (56%)
  matrix products  244 us (17%)
  other arithmetic  150 us (11%)
  local copies, waits for them, and re-layouts  130 us (9%)
  blocking collectives  64.5 us (5%)
  between operations  16.7 us (1%)
    reduce_scatter x8, waiting for transfers between devices, sum_groups(): lax.psum_scatter(low, 'seq', scatter_dimension=dimension, tiled=True)  215 us
    all_gather x1, waiting for transfers between devices, per_device(): lax.all_gather(residual_grad.astype(jnp.bfloat16), 'tp', axis=0, tiled=True)  81.4 us
    reduce_scatter x1, waiting for transfers between devices, per_device(): lax.psum_scatter(jnp.dot(piece, mix_weights.T, preferred_element_type=jnp...  77.3 us
    reduce_scatter x1, waiting for transfers between devices, per_device(): lax.psum_scatter(jnp.dot(piece, glu_weights.T, preferred_element_type=jnp...  75.2 us
    reduce_scatter x1, waiting for transfers between devices, per_device(): lax.psum_scatter(jnp.dot(piece, out_weight, preferred_element_type=jnp.fl...  74.6 us
    all_gather x1, waiting for transfers between devices, per_device(): lax.all_gather(first_norm.astype(jnp.bfloat16), 'tp', axis=0, tiled=True)  71.5 us
    all_gather x1, waiting for transfers between devices, per_device(): lax.all_gather(second_norm.astype(jnp.bfloat16), 'tp', axis=0, tiled=True)  69.1 us
    all_gather x1, waiting for transfers between devices, per_device(): cot_rows = lax.all_gather(cotangent, 'tp', axis=0, tiled=True)  61.9 us
  transfers between devices with their start and end apart: 20, of which 14 were waited for; matrix products, arithmetic and copies ran while one was open for 23% of the time, Pallas kernels for 0%

profile of v1, /device:TPU:0, one launch (start us, length us, event | category | flops | bytes accessed | tf_op | source)
XLA Modules:
  0.0 1392.2 jit_solution(2136669355758981277)
XLA Ops:
  13.8 3.4 constant_dynamic-update-slice_fusion.3
  23.6 71.5 %all-gather.9.cloned.1.call-done = bf16[1024,2048]{1,0:T(8,128)(2,1)} async-done(((bf16[256,2048]{1,0:T(8,128)(2,1)}), bf16[1024,2048]{1,0:T(8,128)(2,1)}) %all-gather.9.cloned.1.call-update) | async-done | bytes 4194320 | tf_op jit(solution)/shard_map/all_gather | solution.py:179
  95.1 12.5 fusion.120
  107.6 3.3 copy-done.25
  124.8 6.3 fusion.41
  131.1 2.9 reshape.315
  134.1 3.1 reshape.318
  137.2 12.2 fusion.74
  151.8 39.1 %while.64 = (s32[]{:T(128)}, f32[4,128,128]{2,1,0:T(8,128)S(1)}, f32[16,4,128,128]{3,2,1,0:T(8,128)}, f32[16,4,128,1]{2,1,3,0:T(4,128)}, f32[16,4,128]{2,1,0:T(4...) while((s32[]{:T(128)}, f32[4,128,128]{2,1,0:T(8,128)S(1)}, ...), condition=%wide.region_6.7_spmd.clone, body=%wide.region_5.6_spmd.clone.sunk | while | flops 262147 | bytes 1321080 | solution.py:124
  194.5 3.2 reshape.316
  197.6 3.3 copy_multiply_fusion.1
  201.2 4.2 fusion.94
  205.4 4.0 fusion.59
  213.3 3.3 copy.220
  219.5 8.9 all_gather.33
  228.5 9.5 while.65
  238.0 4.4 multiply_reduce_fusion.4
  250.2 4.4 convolution_convert_fusion.6
  254.7 74.6 %reduce-scatter.19.cloned.1.call-done = bf16[256,2048]{1,0:T(8,128)(2,1)} async-done(((bf16[1024,2048]{1,0:T(8,128)(2,1)}), bf16[256,2048]{1,0:T(8,128)(2,1)}) %reduce-scatter.19.cloned.1.call-update) | async-done | bytes 1048592 | tf_op jit(solution)/shard_map/reduce_scatter | solution.py:201
  333.3 5.6 constant_dynamic-update-slice_fusion.5
  338.8 6.1 constant_dynamic-update-slice_fusion.4
  345.0 69.1 %all-gather.11.cloned.1.call-done = bf16[1024,2048]{1,0:T(8,128)(2,1)} async-done(((bf16[256,2048]{1,0:T(8,128)(2,1)}), bf16[1024,2048]{1,0:T(8,128)(2,1)}) %all-gather.11.cloned.1.call-update) | async-done | bytes 4194320 | tf_op jit(solution)/shard_map/all_gather | solution.py:208
  414.1 18.9 %fusion.121 = f32[1024,2816]{1,0:T(8,128)} fusion(bf16[1024,2048]{1,0:T(8,128)(2,1)} %all-gather.11.cloned.1.call-done, bf16[2048,2816]{1,0:T(8,128)(2,1)} %constant_dynamic-update-slice_fusion.4), kind=kOutput, calls=%fused_computation.232 | convolution fusion | flops 11811160064 | bytes 27262976 | tf_op jit(solution)/shard_map/dot_general | solution.py:210
  433.0 61.9 %all-gather.13.cloned.1.call-done = bf16[1024,2048]{1,0:T(8,128)(2,1)} async-done(((bf16[256,2048]{1,0:T(8,128)(2,1)}), bf16[1024,2048]{1,0:T(8,128)(2,1)}) %all-gather.13.cloned.1.call-update) | async-done | bytes 4194320 | tf_op jit(solution)/shard_map/all_gather | solution.py:221
  494.9 16.3 %fusion.5 = (bf16[1024,1408]{1,0:T(8,128)(2,1)S(1)}, bf16[1024,1408]{1,0:T(8,128)(2,1)S(1)}, bf16[1024,1408]{1,0:T(8,128)(2,1)}) fusion(f32[1024,2816]{1,0:T(8,128)} %fusion.121, bf16[1024,2048]{1,0:T(8,128)(2,1)} %all-gather.13.cloned.1.call-done, bf16[1408,2048]{1,0:T(8,128)(2,1)} %param.37), kind=kOutput, calls=%fused_computation.22 | convolution fusion | flops 5928648704 | bytes 30146560 | tf_op jit(solution)/shard_map/dot_general | solution.py:223
  513.7 16.3 %convolution_convert_fusion.3 = bf16[1024,2048]{1,0:T(8,128)(2,1)} fusion(bf16[2048,2816]{1,0:T(8,128)(2,1)} %constant_dynamic-update-slice_fusion.4, bf16[1024,1408]{1,0:T(8,128)(2,1)S(1)} %get-tuple-element.548, bf16[1024,1408]{1,0:T(8,128)(2,1)S(1)} %get-tuple-element.547), kind=kOutput, calls=%fused_computation.34 | convolution fusion | flops 11824791552 | bytes 21495808 | tf_op jit(solution)/shard_map/dot_general | solution.py:229
  530.4 75.2 %reduce-scatter.23.cloned.1.call-done = bf16[256,2048]{1,0:T(8,128)(2,1)} async-done(((bf16[1024,2048]{1,0:T(8,128)(2,1)}), bf16[256,2048]{1,0:T(8,128)(2,1)}) %reduce-scatter.23.cloned.1.call-update) | async-done | bytes 1048592 | tf_op jit(solution)/shard_map/reduce_scatter | solution.py:228
  610.4 81.4 %all-gather.15.cloned.1.call-done = bf16[1024,2048]{1,0:T(8,128)(2,1)} async-done(((bf16[256,2048]{1,0:T(8,128)(2,1)}), bf16[1024,2048]{1,0:T(8,128)(2,1)}) %all-gather.15.cloned.1.call-update) | async-done | bytes 4194320 | tf_op jit(solution)/shard_map/all_gather | solution.py:236
  691.7 8.2 multiply_multiply_fusion.2
  699.9 3.0 copy.261
  702.9 2.9 multiply_reduce_fusion
  711.0 18.3 %convolution_convert_fusion = bf16[2048,2816]{1,0:T(8,128)(2,1)} fusion(bf16[1024,2048]{1,0:T(8,128)(2,1)} %all-gather.11.cloned.1.call-done, bf16[1024,1408]{1,0:T(8,128)(2,1)} %copy-done.86, bf16[1024,1408]{1,0:T(8,128)(2,1)} %copy-done.85), kind=kOutput, calls=%fused_computation.16 | convolution fusion | flops 11828461568 | bytes 21495808 | tf_op jit(solution)/shard_map/dot_general | solution.py:225
  729.3 9.5 fusion.117
  739.5 10.5 convolution_convert_fusion.1
  750.1 9.3 all_gather.39
  761.2 4.3 fusion.122
  765.5 3.0 copy.256
  769.3 5.1 fusion.67
  774.5 8.6 fusion.57
  783.1 2.9 fusion.55
  786.1 9.6 multiply_add_fusion
  795.7 6.3 convolution_convert_fusion.7
  802.0 9.8 while.66
  815.6 43.9 %while.63 = (s32[]{:T(128)}, f32[4,128,128]{2,1,0:T(8,128)S(1)}, f32[16,4,128]{2,1,0:T(4,128)S(1)}, f32[16,4,128,128]{3,2,1,0:T(8,128)}, f32[16,4,128,128]{3,2,1...) while((s32[]{:T(128)}, f32[4,128,128]{2,1,0:T(8,128)S(1)}, ...), condition=%wide.region_24.25_spmd, body=%wide.region_22.24_spmd.sunk | while | flops 261635 | bytes 1585281 | solution.py:124
  859.6 13.3 fusion.86
  873.0 7.8 fusion.33
  880.8 3.2 fusion.42
  892.5 3.2 fusion.48
  901.9 7.1 fusion.61
  909.1 8.6 fusion.85
  922.7 10.7 convolution_convert_fusion.2
  933.4 3.5 fusion.118
  939.0 13.2 convolution_convert_fusion.4
  952.3 10.9 convolution_convert_fusion.5
  971.6 24.0 %reduce-scatter.43.cloned.1.call-done = f32[16,4]{1,0:T(8,128)} async-done(((f32[128,4]{1,0:T(8,128)}), f32[16,4]{1,0:T(8,128)}) %reduce-scatter.43.cloned.1.call-update) | async-done | bytes 272
  997.0 43.4 %reduce-scatter.35.cloned.1.call-done = bf16[512,256]{1,0:T(8,128)(2,1)} async-done(((bf16[512,2048]{1,0:T(8,128)(2,1)}), bf16[512,256]{1,0:T(8,128)(2,1)}) %reduce-scatter.35.cloned.1.call-update) | async-done | bytes 262160 | tf_op jit(solution)/shard_map/reduce_scatter | solution.py:58
  1042.2 42.6 %reduce-scatter.27.cloned.1.call-done = bf16[256,512]{1,0:T(8,128)(2,1)} async-done(((bf16[2048,512]{1,0:T(8,128)(2,1)}), bf16[256,512]{1,0:T(8,128)(2,1)}) %reduce-scatter.27.cloned.1.call-update) | async-done | bytes 262160 | tf_op jit(solution)/shard_map/reduce_scatter | solution.py:58
  1086.6 43.0 %reduce-scatter.29.cloned.1.call-done = bf16[256,512]{1,0:T(8,128)(2,1)} async-done(((bf16[2048,512]{1,0:T(8,128)(2,1)}), bf16[256,512]{1,0:T(8,128)(2,1)}) %reduce-scatter.29.cloned.1.call-update) | async-done | bytes 262160 | tf_op jit(solution)/shard_map/reduce_scatter | solution.py:58
  1131.4 42.6 %reduce-scatter.31.cloned.1.call-done = bf16[256,512]{1,0:T(8,128)(2,1)} async-done(((bf16[2048,512]{1,0:T(8,128)(2,1)}), bf16[256,512]{1,0:T(8,128)(2,1)}) %reduce-scatter.31.cloned.1.call-update) | async-done | bytes 262160 | tf_op jit(solution)/shard_map/reduce_scatter | solution.py:58
  1175.8 43.5 %reduce-scatter.33.cloned.1.call-done = bf16[256,512]{1,0:T(8,128)(2,1)} async-done(((bf16[2048,512]{1,0:T(8,128)(2,1)}), bf16[256,512]{1,0:T(8,128)(2,1)}) %reduce-scatter.33.cloned.1.call-update) | async-done | bytes 262160 | tf_op jit(solution)/shard_map/reduce_scatter | solution.py:58
  1221.1 77.3 %reduce-scatter.25.cloned.1.call-done = bf16[256,2048]{1,0:T(8,128)(2,1)} async-done(((bf16[1024,2048]{1,0:T(8,128)(2,1)}), bf16[256,2048]{1,0:T(8,128)(2,1)}) %reduce-scatter.25.cloned.1.call-update) | async-done | bytes 1048592 | tf_op jit(solution)/shard_map/reduce_scatter | solution.py:255
  1300.7 46.2 %all-reduce.5 = (f32[2048]{0:T(1024)S(1)}, f32[2048]{0:T(1024)S(1)}) all-reduce(f32[2048]{0:T(1024)S(1)} %get-tuple-element.486, f32[2048]{0:T(1024)S(1)} %get-tuple-element.480), channel_id=8, replica_groups=mesh['seq'=8,'tp'=4] {'seq','tp'}, use_global_device_ids=true, to_apply=%region_34.35.clone | all-reduce | flops 4096 | bytes 32768
  1348.1 30.9 %reduce-scatter.21.cloned.1.call-done = bf16[256,2048]{1,0:T(8,128)(2,1)} async-done(((bf16[1024,2048]{1,0:T(8,128)(2,1)}), bf16[256,2048]{1,0:T(8,128)(2,1)}) %reduce-scatter.21.cloned.1.call-update) | async-done | bytes 1048592 | tf_op jit(solution)/shard_map/reduce_scatter | solution.py:214
  1379.0 5.9 fusion.24
  (482 shorter events, 215.0 us)
Async XLA Ops:
  7.2 243.0 %copy-start = (bf16[512,2048]{1,0:T(8,128)(2,1)S(1)}, bf16[512,2048]{1,0:T(8,128)(2,1)}, u32[]{:S(2)}) copy-start(bf16[512,2048]{1,0:T(8,128)(2,1)} %param.33) | copy-start | bytes 6291460
  7.2 4.4 copy-start.84
  7.2 5.9 copy-start.75
  7.2 87.9 %all-gather.9.cloned.1.call-start = ((), (), s32[]{:S(2)}) async-start(), calls=%async_computation.14 | async-start | bytes 5242880 | tf_op jit(solution)/shard_map/all_gather | solution.py:179
  11.5 217.0 %all-gather.17.cloned.1.call-start = ((), (), s32[]{:S(2)}) async-start(), calls=%async_computation.30 | async-start | bytes 2359296 | tf_op jit(solution)/shard_map/all_gather | solution.py:17
  12.9 124.2 %copy-start.60 = (f32[16,64]{1,0:T(8,128)}, f32[16,64]{1,0:T(8,128)S(1)}, u32[]{:S(2)}) copy-start(f32[16,64]{1,0:T(8,128)S(1)} %get-tuple-element.569) | copy-start | bytes 12292
  12.9 192.5 %copy-start.62 = (f32[16,64]{1,0:T(8,128)}, f32[16,64]{1,0:T(8,128)S(1)}, u32[]{:S(2)}) copy-start(f32[16,64]{1,0:T(8,128)S(1)} %get-tuple-element.570) | copy-start | bytes 12292
  13.1 105.6 %copy-start.81 = (f32[16]{0:T(128)}, f32[16]{0:T(128)S(1)}, u32[]{:S(2)}) copy-start(f32[16]{0:T(128)S(1)} %slice_reduce_fusion.1) | copy-start | bytes 196
  13.1 94.5 %copy-start.68 = (f32[512]{0:T(512)}, f32[512]{0:T(512)S(1)}, u32[]{:S(2)}) copy-start(f32[512]{0:T(512)S(1)} %broadcast_subtract_fusion) | copy-start | bytes 6148
  13.1 94.4 %copy-start.70 = (f32[512]{0:T(512)}, f32[512]{0:T(512)S(1)}, u32[]{:S(2)}) copy-start(f32[512]{0:T(512)S(1)} %fusion.110) | copy-start | bytes 6148
  13.8 111.0 %copy-start.66 = (f32[1024]{0:T(1024)}, f32[1024]{0:T(1024)S(1)}, u32[]{:S(2)}) copy-start(f32[1024]{0:T(1024)S(1)} %get-tuple-element.541) | copy-start | bytes 12292
  113.8 105.7 %copy-start.72 = (f32[512]{0:T(512)}, f32[512]{0:T(512)S(1)}, u32[]{:S(2)}) copy-start(f32[512]{0:T(512)S(1)} %get-tuple-element.543) | copy-start | bytes 6148
  118.7 18.4 %copy-start.54 = (f32[16,1,4,128]{3,2,0,1:T(4,128)}, f32[16,1,4,128]{3,2,0,1:T(4,128)S(1)}, u32[]{:S(2)}) copy-start(f32[16,1,4,128]{3,2,0,1:T(4,128)S(1)} %copy.359) | copy-start | bytes 98308
  124.8 6.3 copy-start.36
  191.7 137.7 %reduce-scatter.19.cloned.1.call-start = ((), (), s32[]{:S(2)}) async-start(), calls=%async_computation.15 | async-start | bytes 5242880 | tf_op jit(solution)/shard_map/reduce_scatter | solution.py:201
  194.5 15.0 %copy-start.39 = (f32[16,64,64]{2,1,0:T(8,128)}, f32[16,64,64]{2,1,0:T(8,128)S(1)}, u32[]{:S(2)}) copy-start(f32[16,64,64]{2,1,0:T(8,128)S(1)} %compare_select_fusion) | copy-start | bytes 786436
  201.2 4.2 copy-start.9
  201.2 4.2 copy-start.15
  238.0 4.4 copy-start.38
  238.0 4.5 copy-start.74
  250.2 4.4 copy-start.52
  254.6 74.7 %copy-start.8 = (bf16[256,2048]{1,0:T(8,128)(2,1)S(1)}, bf16[256,2048]{1,0:T(8,128)(2,1)}, u32[]{:S(2)}) copy-start(bf16[256,2048]{1,0:T(8,128)(2,1)} %param.23) | copy-start | bytes 3145732
  254.7 76.4 %copy-start.64 = (f32[2048]{0:T(1024)S(1)}, f32[2048]{0:T(1024)}, u32[]{:S(2)}) copy-start(f32[2048]{0:T(1024)} %param.34) | copy-start | bytes 24580
  254.7 159.4 %all-gather.11.cloned.1.call-start = ((), (), s32[]{:S(2)}) async-start(), calls=%async_computation.16 | async-start | bytes 5242880 | tf_op jit(solution)/shard_map/all_gather | solution.py:208
  332.6 162.3 %all-gather.13.cloned.1.call-start = ((), (), s32[]{:S(2)}) async-start(), calls=%async_computation.18 | async-start | bytes 5242880 | tf_op jit(solution)/shard_map/all_gather | solution.py:221
  333.2 272.3 %reduce-scatter.23.cloned.1.call-start = ((), (), s32[]{:S(2)}) async-start(), calls=%async_computation.19 | async-start | bytes 5242880 | tf_op jit(solution)/shard_map/reduce_scatter | solution.py:228
  530.1 161.6 %all-gather.15.cloned.1.call-start = ((), (), s32[]{:S(2)}) async-start(), calls=%async_computation.20 | async-start | bytes 5242880 | tf_op jit(solution)/shard_map/all_gather | solution.py:236
  610.3 191.7 %all-gather.19.cloned.1.call-start = ((), (), s32[]{:S(2)}) async-start(), calls=%async_computation.31 | async-start | bytes 1179648 | tf_op jit(solution)/shard_map/all_gather | solution.py:35
  710.5 252.7 %reduce-scatter.37.cloned.1.call-start = ((), (), s32[]{:S(2)}) async-start(), calls=%async_computation.27 | async-start | bytes 6488064 | tf_op jit(solution)/shard_map/reduce_scatter | solution.py:58
  738.8 226.8 %reduce-scatter.39.cloned.1.call-start = ((), (), s32[]{:S(2)}) async-start(), calls=%async_computation.28 | async-start | bytes 6488064 | tf_op jit(solution)/shard_map/reduce_scatter | solution.py:58
  739.4 228.5 %reduce-scatter.41.cloned.1.call-start = ((), (), s32[]{:S(2)}) async-start(), calls=%async_computation.29 | async-start | bytes 6488064 | tf_op jit(solution)/shard_map/reduce_scatter | solution.py:58
  750.0 9.4 copy-start.20
  750.0 220.2 %reduce-scatter.45.cloned.1.call-start = ((), (), s32[]{:S(2)}) async-start(), calls=%async_computation.33 | async-start | bytes 73728
  769.3 5.1 copy-start.10
  769.3 5.1 copy-start.14
  769.3 5.2 copy-start.63
  774.4 8.7 copy-start.28
  774.4 8.7 copy-start.4
  774.5 8.7 copy-start.6
  774.5 8.7 copy-start.40
  795.7 199.9 %reduce-scatter.43.cloned.1.call-start = ((), (), s32[]{:S(2)}) async-start(), calls=%async_computation.32 | async-start | bytes 73728
  815.6 43.9 %copy-start.55 = (f32[16,1,4,128]{3,2,0,1:T(4,128)S(1)}, f32[16,1,4,128]{3,2,0,1:T(4,128)}, u32[]{:S(2)}) copy-start(f32[16,1,4,128]{3,2,0,1:T(4,128)} %copy-done.54) | copy-start | bytes 98308
  815.6 43.9 %copy-start.61 = (f32[16,64]{1,0:T(8,128)S(1)}, f32[16,64]{1,0:T(8,128)}, u32[]{:S(2)}) copy-start(f32[16,64]{1,0:T(8,128)} %copy-done.60) | copy-start | bytes 12292
  859.5 13.4 copy-start.57
  859.5 13.4 copy-start.82
  859.5 13.5 copy-start.7
  859.5 13.5 copy-start.11
  859.5 13.5 copy-start.29
  859.5 13.5 copy-start.30
  859.5 27.3 %slice-start = ((s8[8388608]{0:T(1024)(128)(4,1)}), s8[4194304]{0:T(1024)(128)(4,1)S(1)}, s32[]{:S(2)}) async-start(s8[8388608]{0:T(1024)(128)(4,1)} %bitcast.219), calls=%async_computation.34 | async-start | bytes 8388608
  873.0 13.8 slice-start.1
  880.8 6.0 copy-start.67
  901.6 138.8 %reduce-scatter.35.cloned.1.call-start = ((), (), s32[]{:S(2)}) async-start(), calls=%async_computation.26 | async-start | bytes 2359296 | tf_op jit(solution)/shard_map/reduce_scatter | solution.py:58
  909.1 175.8 %reduce-scatter.27.cloned.1.call-start = ((), (), s32[]{:S(2)}) async-start(), calls=%async_computation.22 | async-start | bytes 2359296 | tf_op jit(solution)/shard_map/reduce_scatter | solution.py:58
  921.8 11.5 copy-start.48
  936.8 192.7 %reduce-scatter.29.cloned.1.call-start = ((), (), s32[]{:S(2)}) async-start(), calls=%async_computation.23 | async-start | bytes 2359296 | tf_op jit(solution)/shard_map/reduce_scatter | solution.py:58
  937.4 236.6 %reduce-scatter.31.cloned.1.call-start = ((), (), s32[]{:S(2)}) async-start(), calls=%async_computation.24 | async-start | bytes 2359296 | tf_op jit(solution)/shard_map/reduce_scatter | solution.py:58
  938.0 281.3 %reduce-scatter.33.cloned.1.call-start = ((), (), s32[]{:S(2)}) async-start(), calls=%async_computation.25 | async-start | bytes 2359296 | tf_op jit(solution)/shard_map/reduce_scatter | solution.py:58
  938.6 359.8 %reduce-scatter.25.cloned.1.call-start = ((), (), s32[]{:S(2)}) async-start(), calls=%async_computation.21 | async-start | bytes 5242880 | tf_op jit(solution)/shard_map/reduce_scatter | solution.py:255
  952.3 426.7 %reduce-scatter.21.cloned.1.call-start = ((), (), s32[]{:S(2)}) async-start(), calls=%async_computation.17 | async-start | bytes 5242880 | tf_op jit(solution)/shard_map/reduce_scatter | solution.py:214
  970.2 328.2 %copy-start.65 = (f32[2048]{0:T(1024)S(1)}, f32[2048]{0:T(1024)}, u32[]{:S(2)}) copy-start(f32[2048]{0:T(1024)} %param.26) | copy-start | bytes 24580
  970.2 328.2 %copy-start.78 = (f32[256]{0:T(256)S(1)}, f32[256]{0:T(256)}, u32[]{:S(2)}) copy-start(f32[256]{0:T(256)} %copy-done.77) | copy-start | bytes 3076
  1086.6 261.5 %copy-start.80 = (f32[256]{0:T(256)S(1)}, f32[256]{0:T(256)}, u32[]{:S(2)}) copy-start(f32[256]{0:T(256)} %copy-done.79) | copy-start | bytes 3076
  1379.0 5.9 copy-start.1
  (46 other events, 109.5 us)
Sparse Core Ops, SparseCore 0:
  11.6 83.4 all-gather.8
  191.8 26.4 all-gather.16
  254.8 74.5 reduce-scatter.18
  332.7 81.2 all-gather.10
  415.6 79.2 all-gather.12
  530.2 75.2 reduce-scatter.22
  610.4 81.2 all-gather.14
  710.7 22.0 all-gather.18
  738.9 57.5 reduce-scatter.36
  800.2 59.0 reduce-scatter.38
  862.8 59.0 reduce-scatter.40
  925.6 33.2 reduce-scatter.44
  962.4 33.2 reduce-scatter.42
  999.1 41.2 reduce-scatter.34
  1043.5 41.2 reduce-scatter.26
  1088.3 41.2 reduce-scatter.28
  1132.7 41.2 reduce-scatter.30
  1178.0 41.2 reduce-scatter.32
  1221.6 76.7 reduce-scatter.24
  1300.7 78.2 reduce-scatter.20

commit v2 on v0

v2 whole, which is shorter than its diff:
```python
from functools import partial

import jax
import jax.numpy as jnp
from jax import lax
from jax.experimental import pallas as pl
from jax.experimental.pallas import tpu as pltpu
from jax.sharding import PartitionSpec as P

WIDTH = 128
ROUNDS = 4
MIB = 1 << 20
epsilon = 1e-05

f32 = jnp.float32
bf16 = jnp.bfloat16
NN = (((1,), (0,)), ((), ()))
NT = (((1,), (1,)), ((), ()))
TN = (((0,), (0,)), ((), ()))
VM = pltpu.VMEM
DMA = pltpu.SemaphoreType.DMA
MESH = pl.DeviceIdType.MESH


def mul(left, right, dims):
    return lax.dot_general(left, right, dims, preferred_element_type=f32)


def silu_slope(value):
    gate = jax.nn.sigmoid(value)
    return gate * (1.0 + value * (1.0 - gate))


def remote(src, dst, send, recv, axis, peer):
    return pltpu.make_async_remote_copy(
        src_ref=src,
        dst_ref=dst,
        send_sem=send,
        recv_sem=recv,
        device_id={axis: peer},
        device_id_type=MESH,
    )


def greet(peers, count):
    barrier = pltpu.get_barrier_semaphore()
    for axis, peer, wanted in peers:

        @pl.when(wanted)
        def _():
            pl.semaphore_signal(barrier, inc=1, device_id={axis: peer}, device_id_type=MESH)

    pl.semaphore_wait(barrier, count)


def line_peers(size):
    me = lax.axis_index("tp")
    peers = [("tp", lax.rem(me + 1, size), me < size - 1), ("tp", lax.rem(me + size - 1, size), me > 0)]
    return peers, jnp.where(me < size - 1, 1, 0) + jnp.where(me > 0, 1, 0)


def group_peers(size, axis):
    me = lax.axis_index(axis)
    return [(axis, lax.rem(me + k, size), True) for k in range(1, size)], size - 1


class Line:
    def __init__(self, size, send, recv):
        self.size = size
        self.me = lax.axis_index("tp")
        self.right = lax.rem(self.me + 1, size)
        self.left = lax.rem(self.me + size - 1, size)
        self.send, self.recv = send, recv

    def hop(self, way, src, dst, j, at):
        peer = self.right if way == 0 else self.left
        return remote(src, dst, self.send.at[way, j, at], self.recv.at[way, j, at], "tp", peer)


class Scatter(Line):
    def __init__(self, size, send, recv, part, land, total):
        super().__init__(size, send, recv)
        self.part, self.land, self.total = part, land, total

    def copy(self, way, j, to):
        return self.hop(way, self.part.at[j, to], self.land.at[way, j, to], j, to)

    def start(self, j):
        last = self.size - 1

        @pl.when(self.me == 0)
        def _():
            for to in range(last, 0, -1):
                self.copy(0, j, to).start()

        @pl.when(self.me == last)
        def _():
            for to in range(last):
                self.copy(1, j, to).start()

    def step(self, j, t):
        last = self.size - 1
        for way in (0, 1):
            place = self.me if way == 0 else last - self.me
            to = last - t + place
            to = to if way == 0 else last - to

            @pl.when((place >= 1) & (place <= t))
            def _():
                copy = self.copy(way, j, to)
                copy.wait_recv()
                self.add(self.part.at[j, to], self.land.at[way, j, to])
                copy.start()

    def add(self, into, more):
        rows = into.shape[0]

        @pl.loop(0, rows // 16)
        def _(g):
            r = pl.ds(pl.multiple_of(g * 16, 16), 16)
            into[r, :] = (into[r, :].astype(f32) + more[r, :].astype(f32)).astype(bf16)

    def finish(self, j):
        me, last = self.me, self.size - 1
        rows = self.total.shape[0]

        def over(body):
            @pl.loop(0, rows // 16)
            def _(g):
                body(pl.ds(pl.multiple_of(g * 16, 16), 16))

        def first(r):
            self.total[r, :] = self.part[j, me, r, :].astype(f32)

        over(first)
        for way, there in ((0, me >= 1), (1, me < last)):

            @pl.when(there)
            def _():
                self.copy(way, j, me).wait_recv()

                def more(r):
                    self.total[r, :] = self.total[r, :] + self.land[way, j, me, r, :].astype(f32)

                over(more)

    def drain(self, j):
        for to in range(self.size):

            @pl.when(self.me < to)
            def _():
                self.copy(0, j, to).wait_send()

            @pl.when(self.me > to)
            def _():
                self.copy(1, j, to).wait_send()


class Gather(Line):
    def __init__(self, size, send, recv, whole):
        super().__init__(size, send, recv)
        self.whole = whole

    def copy(self, way, j, source):
        block = self.whole.at[source, j]
        return self.hop(way, block, block, j, source)

    def start(self, j):
        @pl.when(self.me < self.size - 1)
        def _():
            self.copy(0, j, self.me).start()

        @pl.when(self.me > 0)
        def _():
            self.copy(1, j, self.me).start()

    def step(self, j, t):
        last = self.size - 1

        @pl.when(self.me >= t)
        def _():
            copy = self.copy(0, j, self.me - t)
            copy.wait_recv()

            @pl.when(self.me < last)
            def _():
                copy.start()

        @pl.when(self.me + t <= last)
        def _():
            copy = self.copy(1, j, self.me + t)
            copy.wait_recv()

            @pl.when(self.me > 0)
            def _():
                copy.start()

    def drain(self, j):
        last = self.size - 1
        for source in range(self.size):

            @pl.when((self.me >= source) & (self.me < last))
            def _():
                self.copy(0, j, source).wait_send()

            @pl.when((self.me <= source) & (self.me > 0))
            def _():
                self.copy(1, j, source).wait_send()


class GroupSum:
    def __init__(self, size, grad, own, got, land, out, sems):
        self.half = size // 2
        here = lax.axis_index("seq")
        self.side = lax.rem(here, 2)
        self.mine = here // 2
        self.sibling = here + 1 - 2 * self.side
        self.grad, self.own, self.got, self.land, self.out = grad, own, got, land, out
        self.pair_sems, self.send, self.recv = sems

    def near(self):
        return remote(
            self.grad.at[:, 1 - self.side], self.got, self.pair_sems.at[0], self.pair_sems.at[1], "seq", self.sibling
        )

    def load(self):
        return pltpu.make_async_copy(self.grad.at[:, self.side], self.own, self.pair_sems.at[2])

    def far(self, k):
        return remote(
            self.own.at[k], self.land.at[self.mine], self.send.at[k], self.recv.at[self.mine], "seq", 2 * k + self.side
        )

    def arrival(self, k):
        return remote(
            self.own.at[k], self.land.at[k], self.send.at[k], self.recv.at[k], "seq", 2 * k + self.side
        )

    def start(self):
        self.near().start()
        self.load().start()

    def over(self, body):
        rows = self.own.shape[1]

        @pl.loop(0, rows // 16)
        def _(g):
            body(pl.ds(pl.multiple_of(g * 16, 16), 16))

    def middle(self):
        self.load().wait()
        self.near().wait_recv()
        for k in range(self.half):

            def both(r):
                self.own[k, r, :] = (self.own[k, r, :].astype(f32) + self.got[k, r, :].astype(f32)).astype(bf16)

            self.over(both)

            @pl.when(k != self.mine)
            def _():
                self.far(k).start()

    def finish(self):
        def first(r):
            self.out[r, :] = self.own[self.mine, r, :].astype(f32)

        self.over(first)
        for k in range(self.half):

            @pl.when(k != self.mine)
            def _():
                self.arrival(k).wait_recv()

                def more(r):
                    self.out[r, :] = self.out[r, :] + self.land[k, r, :].astype(f32)

                self.over(more)

    def drain(self):
        self.near().wait_send()
        for k in range(self.half):

            @pl.when(k != self.mine)
            def _():
                self.far(k).wait_send()


def group_sums(size, grads, outs, take):
    sums = []
    for grad, out in zip(grads, outs):
        own, got, land, *sems = take(6)
        sums.append(GroupSum(size, grad, own, got, land, out, sems))
    return sums


def group_sums_scratch(grads):
    scratch = []
    for grad in grads:
        half = grad.shape[0] // 2
        shape = (half,) + grad.shape[1:]
        scratch += [VM(shape, bf16), VM(shape, bf16), VM(shape, bf16), DMA((3,)), DMA((half,)), DMA((half,))]
    return scratch


def in_pairs(grad):
    return grad.reshape((grad.shape[0] // 2, 2) + grad.shape[1:])


def taker(refs):
    refs = list(refs)

    def take(count):
        taken, refs[:count] = refs[:count], []
        return taken

    return take


def project_kernel(size, rounds, x_ref, gain_ref, wq, wf, wi, ws, a_ref, q_ref, f_ref, i_ref, s_ref, send, recv):
    greet(*line_peers(size))
    line = Gather(size, send, recv, a_ref)
    gain = gain_ref[...]
    m, d = x_ref.shape[1:]

    @pl.loop(0, rounds)
    def _(j):
        @pl.loop(0, m // 16)
        def _(g):
            r = pl.ds(pl.multiple_of(g * 16, 16), 16)
            x = x_ref[j, r, :].astype(f32)
            scale = lax.rsqrt(jnp.mean(x * x, axis=-1, keepdims=True) + epsilon)
            a_ref[line.me, j, r, :] = (x * scale * gain).astype(bf16)

        line.start(j)

    def products(j):
        rows = a_ref[:, j].reshape(size * m, d)
        for weight, out in ((wq, q_ref), (wf, f_ref), (wi, i_ref), (ws, s_ref)):
            out[:, j] = mul(rows, weight[...], NN).reshape(size, m, weight.shape[1])

    @pl.loop(0, rounds)
    def _(j):
        for t in range(1, size):
            line.step(j, t)
        products(j)

    @pl.loop(0, rounds)
    def _(j):
        line.drain(j)


def project(size, rounds, tokens, first_gain, wq, wf, wi, ws):
    rows, d = tokens.shape
    m = rows // rounds
    c = wq.shape[1]
    shape = (size, rounds, m)
    out = pl.pallas_call(
        partial(project_kernel, size, rounds),
        out_shape=[jax.ShapeDtypeStruct(shape + (d,), bf16)] + [jax.ShapeDtypeStruct(shape + (c,), f32)] * 4,
        in_specs=[pl.BlockSpec(memory_space=VM)] * 6,
        out_specs=[pl.BlockSpec(memory_space=VM)] * 5,
        scratch_shapes=[DMA((2, rounds, size)), DMA((2, rounds, size))],
        compiler_params=pltpu.CompilerParams(collective_id=0, has_side_effects=True, vmem_limit_bytes=48 * MIB),
        cost_estimate=pl.CostEstimate(flops=8 * size * rows * d * c, bytes_accessed=32 * MIB, transcendentals=0),
        name="project",
    )(tokens.reshape(rounds, m, d), first_gain.reshape(1, d), wq, wf, wi, ws)
    total = size * rows
    return [out[0].reshape(total, d)] + [part.reshape(total, c) for part in out[1:]]


def document(rows, ends_ref):
    total = jnp.where(rows >= ends_ref[0], 1, 0)
    for k in range(1, ends_ref.shape[0]):
        total = total + jnp.where(rows >= ends_ref[k], 1, 0)
    return total


def block_masks(first, ends_ref):
    shape = (WIDTH, WIDTH)
    down = lax.broadcasted_iota(jnp.int32, shape, 0)
    along = lax.broadcasted_iota(jnp.int32, shape, 1)
    docs = document(first + down, ends_ref)
    same = (docs == document(first + along, ends_ref)) & (down >= along)
    before = jnp.where(first > 0, document(first - 1, ends_ref), -1)
    final = document(first + WIDTH - 1, ends_ref)
    carry = jnp.where(docs == before, 1.0, 0.0)
    tail = jnp.where(docs == final, 1.0, 0.0)
    keep = jnp.where(final == before, 1.0, 0.0)
    return same, carry, tail, keep


def running(log_forget):
    shape = (WIDTH, WIDTH)
    lower = lax.broadcasted_iota(jnp.int32, shape, 0) >= lax.broadcasted_iota(jnp.int32, shape, 1)
    ones = jnp.where(lower, 1.0, 0.0).astype(bf16)
    high = log_forget.astype(bf16)
    low = (log_forget - high.astype(f32)).astype(bf16)
    return mul(ones, high, NN) + mul(ones, low, NN)


def decay_parts(forget_pre, bound):
    away = jax.nn.sigmoid(-forget_pre)
    key = jax.nn.sigmoid(-bound) * away
    return key, running(jnp.log(1.0 - key)), away


class States:
    def __init__(self, size, out_state, out_decay, land_state, land_decay, sems):
        self.size = size
        self.here = lax.axis_index("seq")
        self.out_state, self.out_decay = out_state, out_decay
        self.land_state, self.land_decay = land_state, land_decay
        self.sems = sems

    def pair(self, slot, peer):
        s = self.sems
        return (
            remote(self.out_state, self.land_state.at[slot], s.at[0, peer], s.at[1, slot], "seq", peer),
            remote(self.out_decay, self.land_decay.at[slot], s.at[2, peer], s.at[3, slot], "seq", peer),
        )

    def sends(self, later):
        for k in range(self.size):
            yield k, (self.here < k if later else self.here > k)

    def start(self, later):
        for k, wanted in self.sends(later):

            @pl.when(wanted)
            def _():
                for copy in self.pair(self.here, k):
                    copy.start()

    def compose(self, later, state):
        state[...] = jnp.zeros_like(state)
        order = range(self.size) if later else range(self.size - 1, -1, -1)
        for k in order:

            @pl.when(self.here > k if later else self.here < k)
            def _():
                for copy in self.pair(k, k):
                    copy.wait_recv()
                for h in range(state.shape[0]):
                    decay = self.land_decay[k, h : h + 1, :]
                    state[h] = decay * state[h] + self.land_state[k, h].astype(f32)

    def drain(self, later):
        for k, wanted in self.sends(later):

            @pl.when(wanted)
            def _():
                for copy in self.pair(self.here, k):
                    copy.wait_send()


def states_scratch(size, heads):
    return [
        VM((heads, WIDTH, WIDTH), f32),
        VM((heads, WIDTH, WIDTH), bf16),
        VM((8, WIDTH), f32),
        VM((size, heads, WIDTH, WIDTH), bf16),
        VM((size, 8, WIDTH), f32),
        DMA((4, size)),
    ]


def scan_kernel(
    size,
    ends_ref,
    q_ref,
    f_ref,
    i_ref,
    s_ref,
    bound_ref,
    gain_ref,
    o_ref,
    u_ref,
    starts_ref,
    qd_ref,
    kd_ref,
    qe_ref,
    adds,
    decays,
    state,
    out_state,
    out_decay,
    land_state,
    land_decay,
    sems,
):
    greet(*group_peers(size, "seq"))
    rows, c = q_ref.shape
    blocks, heads = rows // WIDTH, c // WIDTH
    base = lax.axis_index("seq") * rows
    states = States(size, out_state, out_decay, land_state, land_decay, sems)
    state[...] = jnp.zeros_like(state)
    out_decay[...] = jnp.ones_like(out_decay)

    @pl.loop(0, blocks)
    def _(b):
        r = pl.ds(pl.multiple_of(b * WIDTH, WIDTH), WIDTH)
        same, carry, tail, keep = block_masks(base + b * WIDTH, ends_ref)
        for h in range(heads):
            cols = slice(h * WIDTH, (h + 1) * WIDTH)
            q = q_ref[r, cols]
            q = q * jax.nn.sigmoid(q)
            key, run, _ = decay_parts(f_ref[r, cols], bound_ref[:, cols])
            middle, last = run[WIDTH // 2 - 1 : WIDTH // 2, :], run[WIDTH - 1 :, :]
            qd_ref[r, cols] = (q * jnp.exp(run - middle)).astype(bf16)
            kd_ref[r, cols] = (key * jnp.exp(middle - run)).astype(bf16)
            qe_ref[r, cols] = (q * jnp.exp(run) * carry).astype(bf16)
            key_tail = (key * jnp.exp(last - run) * tail).astype(bf16)
            add = mul(i_ref[r, cols].astype(bf16), key_tail, TN)
            decay = jnp.exp(last) * keep
            adds[b, h] = add
            decays[b, h : h + 1, :] = decay
            state[h] = decay * state[h] + add
            out_decay[h : h + 1, :] = out_decay[h : h + 1, :] * decay

    out_state[...] = state[...].astype(bf16)
    states.start(True)

    @pl.loop(0, blocks)
    def _(b):
        r = pl.ds(pl.multiple_of(b * WIDTH, WIDTH), WIDTH)
        same, carry, tail, keep = block_masks(base + b * WIDTH, ends_ref)
        for h in range(heads):
            cols = slice(h * WIDTH, (h + 1) * WIDTH)
            scores = jnp.where(same, mul(qd_ref[r, cols], kd_ref[r, cols], NT), 0.0).astype(bf16)
            o_ref[r, cols] = mul(scores, i_ref[r, cols].astype(bf16), NN)

    states.compose(True, state)

    @pl.loop(0, blocks)
    def _(b):
        r = pl.ds(pl.multiple_of(b * WIDTH, WIDTH), WIDTH)
        places = base + b * WIDTH + lax.broadcasted_iota(jnp.int32, (WIDTH, WIDTH), 0)
        valid = jnp.where(places < ends_ref[ends_ref.shape[0] - 1], 1.0, 0.0)
        for h in range(heads):
            cols = slice(h * WIDTH, (h + 1) * WIDTH)
            low = state[h].astype(bf16)
            starts_ref[b, h] = low
            o = o_ref[r, cols] + mul(qe_ref[r, cols], low, NT)
            o_ref[r, cols] = o
            state[h] = decays[b, h : h + 1, :] * state[h] + adds[b, h]
            scale = lax.rsqrt(jnp.mean(o * o, axis=-1, keepdims=True) + epsilon)
            s = s_ref[r, cols]
            z = s * jax.nn.sigmoid(s) * valid
            u_ref[r, cols] = (o * scale * gain_ref[:, cols] * z).astype(bf16)

    states.drain(True)


def scan_forward(size, ends, q, f, i, s, bound, gain):
    rows, c = q.shape
    blocks, heads = rows // WIDTH, c // WIDTH
    low = VM((rows, c), bf16)
    return pl.pallas_call(
        partial(scan_kernel, size),
        out_shape=[
            jax.ShapeDtypeStruct((rows, c), f32),
            jax.ShapeDtypeStruct((rows, c), bf16),
            jax.ShapeDtypeStruct((blocks, heads, WIDTH, WIDTH), bf16),
        ],
        in_specs=[pl.BlockSpec(memory_space=pltpu.SMEM)] + [pl.BlockSpec(memory_space=VM)] * 6,
        out_specs=[pl.BlockSpec(memory_space=VM)] * 3,
        scratch_shapes=[
            low,
            low,
            low,
            VM((blocks, heads, WIDTH, WIDTH), f32),
            VM((blocks, 8, WIDTH), f32),
        ]
        + states_scratch(size, heads),
        compiler_params=pltpu.CompilerParams(collective_id=1, has_side_effects=True, vmem_limit_bytes=48 * MIB),
        cost_estimate=pl.CostEstimate(flops=20 * rows * c * WIDTH, bytes_accessed=14 * MIB, transcendentals=8 * rows * c),
        name="scan_forward",
    )(ends, q, f, i, s, bound, gain)


def scan_back_kernel(size, count, *refs):
    take = taker(refs)
    ends_ref, q_ref, f_ref, i_ref, s_ref, bound_ref, gain_ref, o_ref, starts_ref, ub_ref = take(10)
    grads = take(count)
    dq_ref, df_ref, di_ref, ds_ref, small_ref = take(5)
    grad_outs = take(count)
    qd_ref, kd_ref, qe_ref, kt_ref, do_ref, run_ref, adds, decays = take(8)
    state, out_state, out_decay, land_state, land_decay, sems = take(6)
    sums = group_sums(size, grads, grad_outs, take)
    greet(*group_peers(size, "seq"))
    rows, c = q_ref.shape
    blocks, heads = rows // WIDTH, c // WIDTH
    base = lax.axis_index("seq") * rows
    states = States(size, out_state, out_decay, land_state, land_decay, sems)
    for each in sums:
        each.start()
    state[...] = jnp.zeros_like(state)
    out_decay[...] = jnp.ones_like(out_decay)
    small_ref[...] = jnp.zeros_like(small_ref)

    @pl.loop(0, blocks)
    def _(back):
        b = blocks - 1 - back
        r = pl.ds(pl.multiple_of(b * WIDTH, WIDTH), WIDTH)
        same, carry, tail, keep = block_masks(base + b * WIDTH, ends_ref)
        places = base + b * WIDTH + lax.broadcasted_iota(jnp.int32, (WIDTH, WIDTH), 0)
        valid = jnp.where(places < ends_ref[ends_ref.shape[0] - 1], 1.0, 0.0)
        for h in range(heads):
            cols = slice(h * WIDTH, (h + 1) * WIDTH)
            o, s, ub, gain = o_ref[r, cols], s_ref[r, cols], ub_ref[r, cols], gain_ref[:, cols]
            scale = lax.rsqrt(jnp.mean(o * o, axis=-1, keepdims=True) + epsilon)
            normed = o * scale
            gate = jax.nn.sigmoid(s)
            uz = ub * (s * gate * valid)
            small_ref[heads + h : heads + h + 1, :] += jnp.sum(uz * normed, axis=0, keepdims=True)
            nb = uz * gain
            ds_ref[r, cols] = (ub * normed * gain * valid * (gate * (1.0 + s * (1.0 - gate)))).astype(bf16)
            do = (scale * (nb - normed * jnp.mean(nb * normed, axis=-1, keepdims=True))).astype(bf16)
            do_ref[r, cols] = do
            q = q_ref[r, cols]
            q = q * jax.nn.sigmoid(q)
            key, run, _ = decay_parts(f_ref[r, cols], bound_ref[:, cols])
            middle, last = run[WIDTH // 2 - 1 : WIDTH // 2, :], run[WIDTH - 1 :, :]
            run_ref[r, cols] = run
            qd_ref[r, cols] = (q * jnp.exp(run - middle)).astype(bf16)
            kd_ref[r, cols] = (key * jnp.exp(middle - run)).astype(bf16)
            kt_ref[r, cols] = (key * jnp.exp(last - run) * tail).astype(bf16)
            qe = (q * jnp.exp(run) * carry).astype(bf16)
            qe_ref[r, cols] = qe
            add = mul(do, qe, TN)
            decay = jnp.exp(last) * keep
            adds[b, h] = add
            decays[b, h : h + 1, :] = decay
            state[h] = decay * state[h] + add
            out_decay[h : h + 1, :] = out_decay[h : h + 1, :] * decay

    out_state[...] = state[...].astype(bf16)
    states.start(False)

    for each in sums:
        each.middle()

    states.compose(False, state)

    @pl.loop(0, blocks)
    def _(back):
        b = blocks - 1 - back
        r = pl.ds(pl.multiple_of(b * WIDTH, WIDTH), WIDTH)
        same, carry, tail, keep = block_masks(base + b * WIDTH, ends_ref)
        shape = (WIDTH, WIDTH)
        down, along = lax.broadcasted_iota(jnp.int32, shape, 0), lax.broadcasted_iota(jnp.int32, shape, 1)
        from_here = jnp.where(along >= down, 1.0, 0.0).astype(bf16)
        ahead = jnp.where(along < down, 1.0, 0.0).astype(bf16)
        for h in range(heads):
            cols = slice(h * WIDTH, (h + 1) * WIDTH)
            do, v = do_ref[r, cols], i_ref[r, cols].astype(bf16)
            low, start = state[h].astype(bf16), starts_ref[b, h]
            dq_state = mul(do, start, NN)
            dk_state = mul(v, low, NN)
            kt = kt_ref[r, cols]
            qd, kd = qd_ref[r, cols], kd_ref[r, cols]
            scores = jnp.where(same, mul(qd, kd, NT), 0.0).astype(bf16)
            slopes = jnp.where(same, mul(do, v, NT), 0.0).astype(bf16)
            dq_near = mul(slopes, kd, NN)
            dk_near = mul(slopes, qd, TN)
            di_ref[r, cols] = (mul(scores, do, TN) + mul(kt, low, NT)).astype(bf16)
            run = run_ref[r, cols]
            middle, last = run[WIDTH // 2 - 1 : WIDTH // 2, :], run[WIDTH - 1 :, :]
            q_back = dq_near * jnp.exp(run - middle) + dq_state * (jnp.exp(run) * carry)
            k_back = dk_near * jnp.exp(middle - run) + dk_state * (jnp.exp(last - run) * tail)
            later = (
                qe_ref[r, cols].astype(f32) * dq_state
                + qd.astype(f32) * dq_near
                - kd.astype(f32) * dk_near
            )
            earlier = kt.astype(f32) * dk_state
            decay = decays[b, h : h + 1, :]
            log_back = decay * jnp.sum(low.astype(f32) * start.astype(f32), axis=0, keepdims=True)
            for ones, part in ((from_here, later), (ahead, earlier)):
                high = part.astype(bf16)
                log_back = log_back + mul(ones, high, NN)
                log_back = log_back + mul(ones, (part - high.astype(f32)).astype(bf16), NN)
            f_pre = f_ref[r, cols]
            away, near = jax.nn.sigmoid(-f_pre), jax.nn.sigmoid(f_pre)
            upper = jax.nn.sigmoid(-bound_ref[:, cols])
            lower = jax.nn.sigmoid(bound_ref[:, cols])
            forget_back = log_back / (1.0 - upper * away) - k_back
            slope = forget_back * away * upper
            df_ref[r, cols] = (slope * near).astype(bf16)
            small_ref[h : h + 1, :] += jnp.sum(slope, axis=0, keepdims=True) * lower
            dq_ref[r, cols] = (q_back * silu_slope(q_ref[r, cols])).astype(bf16)
            state[h] = adds[b, h] + decay * state[h]

    for each in sums:
        each.finish()
    states.drain(False)
    for each in sums:
        each.drain()


def scan_backward(size, ends, q, f, i, s, bound, gain, o, starts, ub, grads):
    rows, c = q.shape
    blocks, heads = rows // WIDTH, c // WIDTH
    low, wide = VM((rows, c), bf16), VM((rows, c), f32)
    spec = pl.BlockSpec(memory_space=VM)
    return pl.pallas_call(
        partial(scan_back_kernel, size, len(grads)),
        out_shape=[jax.ShapeDtypeStruct((rows, c), bf16)] * 4
        + [jax.ShapeDtypeStruct((2 * heads, WIDTH), f32)]
        + [jax.ShapeDtypeStruct(grad.shape[1:], f32) for grad in grads],
        in_specs=[pl.BlockSpec(memory_space=pltpu.SMEM)]
        + [spec] * 9
        + [pl.BlockSpec(memory_space=pl.ANY)] * len(grads),
        out_specs=[spec] * (5 + len(grads)),
        scratch_shapes=[low] * 5
        + [wide, VM((blocks, heads, WIDTH, WIDTH), f32), VM((blocks, 8, WIDTH), f32)]
        + states_scratch(size, heads)
        + group_sums_scratch(grads),
        compiler_params=pltpu.CompilerParams(collective_id=2, has_side_effects=True, vmem_limit_bytes=60 * MIB),
        cost_estimate=pl.CostEstimate(flops=40 * rows * c * WIDTH, bytes_accessed=20 * MIB, transcendentals=16 * rows * c),
        name="scan_backward",
    )(ends, q, f, i, s, bound, gain, o, starts, ub, *[in_pairs(grad) for grad in grads])


def middle_kernel(
    size,
    rounds,
    u_ref,
    x_ref,
    cot_ref,
    gain_ref,
    out_w,
    gate_w,
    up_w,
    down_w,
    res_ref,
    back_ref,
    b_ref,
    e_ref,
    ub_ref,
    second_ref,
    hidden_out,
    gate_out,
    up_out,
    part,
    land,
    total,
    hidden,
    gate_back,
    up_back,
    keep_sems,
    s_send,
    s_recv,
    g_send,
    g_recv,
    s_send2,
    s_recv2,
    g_send2,
    g_recv2,
):
    greet(*line_peers(size))
    me = lax.axis_index("tp")
    m, d = x_ref.shape[1:]
    ff = gate_w.shape[1]
    scatter = Scatter(size, s_send, s_recv, part, land, total)
    gather = Gather(size, g_send, g_recv, b_ref)
    scatter_back = Scatter(size, s_send2, s_recv2, part, land, total)
    gather_back = Gather(size, g_send2, g_recv2, e_ref)
    gain = gain_ref[...]
    second_ref[...] = jnp.zeros_like(second_ref)
    tile = min(512, d)

    def project_out(j):
        rows = u_ref[:, j].reshape(size * m, u_ref.shape[3])

        @pl.loop(0, d // tile)
        def _(n):
            cols = pl.ds(pl.multiple_of(n * tile, tile), tile)
            part[j, :, :, cols] = mul(rows, out_w[:, cols], NN).astype(bf16).reshape(size, m, tile)

        scatter.start(j)

    def norm(j):
        @pl.loop(0, m // 16)
        def _(g):
            r = pl.ds(pl.multiple_of(g * 16, 16), 16)
            residual = x_ref[j, r, :].astype(f32) + total[r, :]
            res_ref[j, r, :] = residual
            scale = lax.rsqrt(jnp.mean(residual * residual, axis=-1, keepdims=True) + epsilon)
            b_ref[me, j, r, :] = (residual * scale * gain).astype(bf16)

        gather.start(j)

    def kept(j):
        return [
            pltpu.make_async_copy(src, dst.at[:, j], keep_sems.at[k])
            for k, (src, dst) in enumerate(((hidden, hidden_out), (gate_back, gate_out), (up_back, up_out)))
        ]

    def feed(j):
        @pl.when(j > 0)
        def _():
            for copy in kept(j - 1):
                copy.wait()

        rows = b_ref[:, j].reshape(size * m, d)
        cot = cot_ref[:, j].reshape(size * m, d)
        step = 512
        for low in range(0, ff, step):
            cols = slice(low, min(low + step, ff))
            width = cols.stop - cols.start
            gate = mul(rows, gate_w[:, cols], NN)
            up = mul(rows, up_w[:, cols], NN)
            hb = mul(cot, down_w[cols, :], NT)
            sig = jax.nn.sigmoid(gate)
            act = gate * sig
            shape = (size, m, width)
            hidden[:, :, cols] = (act * up).astype(bf16).reshape(shape)
            up_back[:, :, cols] = (hb * act).astype(bf16).reshape(shape)
            gate_back[:, :, cols] = (hb * up * (sig * (1.0 + gate * (1.0 - sig)))).astype(bf16).reshape(shape)
        for copy in kept(j):
            copy.start()

    def feed_back(j):
        scatter.drain(j)
        gates = gate_back[...].reshape(size * m, ff)
        ups = up_back[...].reshape(size * m, ff)

        @pl.loop(0, d // tile)
        def _(n):
            cols = pl.ds(pl.multiple_of(n * tile, tile), tile)
            sums = mul(gates, gate_w[cols, :], NT) + mul(ups, up_w[cols, :], NT)
            part[j, :, :, cols] = sums.astype(bf16).reshape(size, m, tile)

        scatter_back.start(j)

    def norm_back(j):
        @pl.loop(0, m // 16)
        def _(g):
            r = pl.ds(pl.multiple_of(g * 16, 16), 16)
            b_back, residual = total[r, :], res_ref[j, r, :]
            scale = lax.rsqrt(jnp.mean(residual * residual, axis=-1, keepdims=True) + epsilon)
            normed = residual * scale
            second_ref[...] += jnp.sum(b_back * normed, axis=0, keepdims=True)
            inner = b_back * gain
            back = cot_ref[me, j, r, :].astype(f32) + scale * (
                inner - normed * jnp.mean(inner * normed, axis=-1, keepdims=True)
            )
            back_ref[j, r, :] = back
            e_ref[me, j, r, :] = back.astype(bf16)

        gather_back.start(j)

    def unproject(j):
        rows = e_ref[:, j].reshape(size * m, d)
        ub_ref[:, j] = mul(rows, out_w[...], NT).reshape(size, m, out_w.shape[0])

    @pl.loop(0, rounds + 4)
    def _(i):
        def stage(lag, body):
            @pl.when((i >= lag) & (i < rounds + lag))
            def _():
                body(i - lag)

        stage(0, project_out)
        for t in range(1, size):
            stage(1, lambda j: scatter.step(j, t) if t < size - 1 else scatter.finish(j))
            if t == size - 1:
                stage(1, norm)
            stage(2, lambda j: gather.step(j, t))
            stage(3, lambda j: scatter_back.step(j, t) if t < size - 1 else scatter_back.finish(j))
            if t == size - 1:
                stage(3, norm_back)
            stage(4, lambda j: gather_back.step(j, t))
        stage(2, feed)
        stage(2, feed_back)
        stage(4, unproject)

    for copy in kept(rounds - 1):
        copy.wait()

    @pl.loop(0, rounds)
    def _(j):
        gather.drain(j)
        scatter_back.drain(j)
        gather_back.drain(j)


def middle(size, rounds, u, x, cot, gain, out_w, gate_w, up_w, down_w):
    rows, d = x.shape
    m = rows // rounds
    c, ff = out_w.shape[0], gate_w.shape[1]
    shape = (size, rounds, m)
    sems = DMA((2, rounds, size))
    wide = VM((size, m, ff), bf16)
    outs = pl.pallas_call(
        partial(middle_kernel, size, rounds),
        out_shape=[
            jax.ShapeDtypeStruct((rounds, m, d), f32),
            jax.ShapeDtypeStruct((rounds, m, d), f32),
            jax.ShapeDtypeStruct(shape + (d,), bf16),
            jax.ShapeDtypeStruct(shape + (d,), bf16),
            jax.ShapeDtypeStruct(shape + (c,), f32),
            jax.ShapeDtypeStruct((1, d), f32),
        ]
        + [jax.ShapeDtypeStruct(shape + (ff,), bf16)] * 3,
        in_specs=[pl.BlockSpec(memory_space=VM)] * 8,
        out_specs=[pl.BlockSpec(memory_space=VM)] * 6 + [pl.BlockSpec(memory_space=pl.ANY)] * 3,
        scratch_shapes=[
            VM((rounds, size, m, d), bf16),
            VM((2, rounds, size, m, d), bf16),
            VM((m, d), f32),
            wide,
            wide,
            wide,
            DMA((3,)),
        ]
        + [sems] * 8,
        compiler_params=pltpu.CompilerParams(collective_id=3, has_side_effects=True, vmem_limit_bytes=63 * MIB),
        cost_estimate=pl.CostEstimate(
            flops=2 * size * rows * d * (2 * c + 5 * ff), bytes_accessed=56 * MIB, transcendentals=size * rows * ff
        ),
        name="middle",
    )(
        u.reshape(shape + (c,)),
        x.reshape(rounds, m, d),
        cot.reshape(shape + (d,)),
        gain.reshape(1, d),
        out_w,
        gate_w,
        up_w,
        down_w,
    )
    res, back, b, e, ub, second, hidden, gates, ups = outs
    total = size * rows
    return (
        res.reshape(rows, d),
        back.reshape(rows, d),
        b.reshape(total, d),
        e.reshape(total, d),
        ub.reshape(total, c),
        second,
        hidden.reshape(total, ff),
        gates.reshape(total, ff),
        ups.reshape(total, ff),
    )


class Everyone:
    def __init__(self, size, axis, mine, land, sems):
        self.size, self.axis = size, axis
        self.here = lax.axis_index(axis)
        self.mine, self.land, self.sems = mine, land, sems

    def copy(self, slot, peer):
        return remote(self.mine, self.land.at[slot], self.sems.at[0, peer], self.sems.at[1, slot], self.axis, peer)

    def others(self):
        for k in range(self.size):
            yield k, self.here != k

    def start(self):
        for k, other in self.others():

            @pl.when(other)
            def _():
                self.copy(self.here, k).start()

    def finish(self, out):
        out[...] = self.mine[...]
        for k, other in self.others():

            @pl.when(other)
            def _():
                self.copy(k, k).wait_recv()
                out[...] = out[...] + self.land[k]

    def drain(self):
        for k, other in self.others():

            @pl.when(other)
            def _():
                self.copy(self.here, k).wait_send()


def everyone_scratch(size, rows):
    return [VM((rows, WIDTH), f32), VM((size, rows, WIDTH), f32), DMA((2, size))]


def stack(vector, into, at):
    for k in range(vector.shape[1] // WIDTH):
        into[at + k : at + k + 1, :] = vector[:, k * WIDTH : (k + 1) * WIDTH]


def last_kernel(size, groups, rounds, count, *refs):
    take = taker(refs)
    backs, weights = take(4), take(4)
    x_ref, back_ref, gain_ref, second_ref, small_ref = take(5)
    grads = take(count)
    tokens_out, second_out, first_out, small_out = take(4)
    grad_outs = take(count)
    part, land, total, first, s_send, s_recv = take(6)
    small_seq, gain_seq, second_tp, first_tp = (take(3) for _ in range(4))
    sums = group_sums(groups, grads, grad_outs, take)

    seq, seq_count = group_peers(groups, "seq")
    tp, tp_count = group_peers(size, "tp")
    greet(seq + tp, seq_count + tp_count)

    for each in sums:
        each.start()

    m, d = x_ref.shape[1:]
    scatter = Scatter(size, s_send, s_recv, part, land, total)
    gain = gain_ref[...]
    first[...] = jnp.zeros_like(first)
    tile = min(512, d)

    seq_small = Everyone(groups, "seq", *small_seq)
    seq_first = Everyone(groups, "seq", *gain_seq)
    tp_second = Everyone(size, "tp", *second_tp)
    tp_first = Everyone(size, "tp", *first_tp)
    lines, smalls = d // WIDTH, small_ref.shape[0]
    stack(second_ref[...], small_seq[0], 0)
    small_seq[0][lines : lines + smalls, :] = small_ref[...]
    seq_small.start()

    def products(j):
        @pl.loop(0, d // tile)
        def _(n):
            cols = pl.ds(pl.multiple_of(n * tile, tile), tile)
            acc = None
            for back, weight in zip(backs, weights):
                term = mul(back[:, j].reshape(size * m, back.shape[3]), weight[cols, :], NT)
                acc = term if acc is None else acc + term
            part[j, :, :, cols] = acc.astype(bf16).reshape(size, m, tile)

        scatter.start(j)

    def norm_back(j):
        @pl.loop(0, m // 16)
        def _(g):
            r = pl.ds(pl.multiple_of(g * 16, 16), 16)
            a_back, x = total[r, :], x_ref[j, r, :].astype(f32)
            scale = lax.rsqrt(jnp.mean(x * x, axis=-1, keepdims=True) + epsilon)
            normed = x * scale
            first[...] += jnp.sum(a_back * normed, axis=0, keepdims=True)
            inner = a_back * gain
            tokens_out[j, r, :] = back_ref[j, r, :] + scale * (
                inner - normed * jnp.mean(inner * normed, axis=-1, keepdims=True)
            )

    @pl.loop(0, rounds)
    def _(j):
        products(j)

    for each in sums[: count // 2]:
        each.middle()

    seq_small.finish(small_out)
    second_tp[0][...] = small_out[:lines, :]
    tp_second.start()

    for each in sums[count // 2 :]:
        each.middle()

    @pl.loop(0, rounds)
    def _(j):
        for t in range(1, size):
            if t < size - 1:
                scatter.step(j, t)
            else:
                scatter.finish(j)
        norm_back(j)

    stack(first[...], gain_seq[0], 0)
    seq_first.start()
    tp_second.finish(second_out)
    for each in sums[: count // 2]:
        each.finish()
    seq_first.finish(first_tp[0])
    tp_first.start()
    for each in sums[count // 2 :]:
        each.finish()
    tp_first.finish(first_out)

    for each in sums + [seq_small, seq_first, tp_second, tp_first]:
        each.drain()

    @pl.loop(0, rounds)
    def _(j):
        scatter.drain(j)


def last(size, groups, rounds, backs, weights, x, back, gain, second, small, grads):
    rows, d = x.shape
    m = rows // rounds
    c = weights[0].shape[1]
    shape = (size, rounds, m)
    lines = d // WIDTH
    sems = DMA((2, rounds, size))
    spec = pl.BlockSpec(memory_space=VM)
    small_rows = lines + small.shape[0]
    outs = pl.pallas_call(
        partial(last_kernel, size, groups, rounds, len(grads)),
        out_shape=[
            jax.ShapeDtypeStruct((rounds, m, d), f32),
            jax.ShapeDtypeStruct((lines, WIDTH), f32),
            jax.ShapeDtypeStruct((lines, WIDTH), f32),
            jax.ShapeDtypeStruct((small_rows, WIDTH), f32),
        ]
        + [jax.ShapeDtypeStruct(grad.shape[1:], f32) for grad in grads],
        in_specs=[spec] * 13 + [pl.BlockSpec(memory_space=pl.ANY)] * len(grads),
        out_specs=[spec] * (4 + len(grads)),
        scratch_shapes=[
            VM((rounds, size, m, d), bf16),
            VM((2, rounds, size, m, d), bf16),
            VM((m, d), f32),
            VM((1, d), f32),
            sems,
            sems,
        ]
        + everyone_scratch(groups, small_rows)
        + everyone_scratch(groups, lines)
        + everyone_scratch(size, lines)
        + everyone_scratch(size, lines)
        + group_sums_scratch(grads),
        compiler_params=pltpu.CompilerParams(collective_id=4, has_side_effects=True, vmem_limit_bytes=63 * MIB),
        cost_estimate=pl.CostEstimate(flops=8 * size * rows * d * c, bytes_accessed=56 * MIB, transcendentals=0),
        name="last",
    )(
        *[part.reshape(shape + (c,)) for part in backs],
        *weights,
        x.reshape(rounds, m, d),
        back.reshape(rounds, m, d),
        gain.reshape(1, d),
        second,
        small,
        *[in_pairs(grad) for grad in grads],
    )
    return (outs[0].reshape(rows, d), outs[1], outs[2], outs[3][lines:]) + tuple(outs[4:])


def per_device(
    size,
    groups,
    tokens,
    lengths,
    cotangent,
    first_gain,
    query_weight,
    forget_weight,
    input_weight,
    swish_weight,
    bound_logit,
    group_gain,
    out_weight,
    second_gain,
    gate_weight,
    up_weight,
    down_weight,
):
    weights = (query_weight, forget_weight, input_weight, swish_weight)
    ends = jnp.cumsum(lengths).astype(jnp.int32)
    bound, head_gain = bound_logit.reshape(1, -1), group_gain.reshape(1, -1)
    a, q, f, i, s = project(size, ROUNDS, tokens, first_gain, *weights)
    cot_own, q = lax.optimization_barrier((cotangent, q))
    cot = lax.all_gather(cot_own, "tp", axis=0, tiled=True)
    o, u, starts = scan_forward(groups, ends, q, f, i, s, bound, head_gain)
    residual, back, b, e, ub, second, hidden, gates, ups = middle(
        size, ROUNDS, u, tokens, cot, second_gain, out_weight, gate_weight, up_weight, down_weight
    )
    hidden_2, ub = lax.optimization_barrier((hidden, ub))
    down = jnp.dot(hidden_2, down_weight, preferred_element_type=f32).astype(bf16)
    down = lax.psum_scatter(down, "tp", scatter_dimension=0, tiled=True)
    output = (residual + down.astype(f32)).astype(bf16)
    total, d = b.shape

    def by_rows(left, right):
        grad = lax.dot_general(left, right, TN, preferred_element_type=f32).astype(bf16)
        return grad.reshape(groups, grad.shape[0] // groups, grad.shape[1])

    narrow = d // groups < WIDTH

    def by_cols(left, right):
        if narrow:
            return by_rows(right, left)
        right = right.reshape(total, groups, right.shape[1] // groups)
        return jnp.einsum("tf,tnc->nfc", left, right, preferred_element_type=f32).astype(bf16)

    glu = [by_rows(b, gates), by_rows(b, ups)]
    dq, df, di, ds, small, gate_grad, up_grad = scan_backward(
        groups, ends, q, f, i, s, bound, head_gain, o, starts, ub, glu
    )
    others = [by_cols(hidden, cot), by_cols(u, e)]
    mix = [by_rows(a, part) for part in (dq, df, di, ds)]
    tokens_grad, second_sum, first_sum, small_sum, *sums = last(
        size, groups, ROUNDS, (dq, df, di, ds), weights, tokens, back, first_gain, second, small, others + mix
    )
    heads = bound_logit.shape[0]
    here = lax.axis_index("seq")
    place = here * size + lax.axis_index("tp")
    each = d // (groups * size)
    wide = WIDTH // groups
    first_grad = lax.dynamic_slice_in_dim(first_sum.reshape(-1), place * each, each)
    second_grad = lax.dynamic_slice_in_dim(second_sum.reshape(-1), place * each, each)
    bound_grad = lax.dynamic_slice_in_dim(small_sum[:heads], here * wide, wide, axis=1)
    head_grad = lax.dynamic_slice_in_dim(small_sum[heads:], here * wide, wide, axis=1)
    down_grad, out_grad, query_grad, forget_grad, input_grad, swish_grad = sums
    if narrow:
        down_grad, out_grad = down_grad.T, out_grad.T
    return (
        output,
        tokens_grad,
        first_grad,
        query_grad,
        forget_grad,
        input_grad,
        swish_grad,
        bound_grad,
        head_grad,
        out_grad,
        second_grad,
        gate_grad,
        up_grad,
        down_grad,
    )


def solution(mesh):
    rows, both, cols, lines = P(("seq", "tp"), None), P(("seq", "tp")), P(None, "tp"), P("tp", None)
    in_specs = (rows, P(), rows, P(), cols, cols, cols, cols, lines, lines, lines, P(), cols, cols, lines)
    down, across = P("seq", "tp"), P("tp", "seq")
    out_specs = (rows, rows, both, down, down, down, down, across, across, across, both, down, down, across)
    return jax.shard_map(
        partial(per_device, mesh.shape["tp"], mesh.shape["seq"]),
        mesh=mesh,
        in_specs=in_specs,
        out_specs=out_specs,
        check_vma=False,
    )
```

time: 1740 us -> 750 us (0.43)
  waiting for transfers between devices: 1140 us -> 49.8 us
  Pallas kernels: 0 us -> 574 us
  matrix products: 249 us -> 61.9 us
  other arithmetic: 131 us -> 3.39 us
  local copies, waits for them, and re-layouts: 126 us -> 42.3 us
  blocking collectives: 64.2 us -> 0 us
    reduce_scatter x12 -> x1, waiting for transfers between devices: 866 us -> 0.01 us  [per_device(): down = lax.psum_scatter(down, 'tp', scatter_dimension=0, tiled=True)]
    pallas_call x0 -> x5, Pallas kernels: none -> 574 us  [the longest x1 252 us: middle(): pl.pallas_call(partial(middle_kernel, size, rounds), out_shape=[jax.Shape...]
    all_gather x6 -> x1, waiting for transfers between devices: 275 us -> 49.7 us  [per_device(): cot = lax.all_gather(cot_own, 'tp', axis=0, tiled=True)]
    dot_general x27 -> x9, matrix products: 249 us -> 61.9 us  [the longest x6 37.4 us: by_rows(): lax.dot_general(left, right, TN, preferred_element_type=f32).astype(bf16)]
    unnamed x1 -> x0, blocking collectives: 46.2 us -> none
    reduce_sum x26 -> x0, other arithmetic: 38.6 us -> none  [the longest x16 20.7 us: advance(): return (pieces[0][:, :, None] * state_now + pieces[1], state_now)]
    reshape x9 -> x0, local copies, waits for them, and re-layouts: 27.8 us -> none  [the longest x2 6.11 us: group_out(): normed = (split_heads * inv_scale * group_gain).reshape(recurrent_out.shape)]
    add x19 -> x0, other arithmetic: 23.9 us -> none  [the longest x16 17.9 us: advance(): return (pieces[0][:, :, None] * state_now + pieces[1], state_now)]
  transfers between devices with their start and end apart: 20 -> 2, of which waited for: 16 -> 1; matrix products, arithmetic and copies ran while one was open for 18% -> 7% of each run, Pallas kernels for 0% -> 32%
where the time goes in v2:
time: 750 us; the launch traced here: 746 us
  Pallas kernels  574 us (77%)
  matrix products  61.9 us (8%)
  waiting for transfers between devices  49.8 us (7%)
  local copies, waits for them, and re-layouts  42.3 us (6%)
  between operations  14.4 us (2%)
    pallas_call x1, Pallas kernels, middle(): pl.pallas_call(partial(middle_kernel, size, rounds), out_shape=[jax.Shape...  252 us
    pallas_call x1, Pallas kernels, last(): pl.pallas_call(partial(last_kernel, size, groups, rounds, len(grads)), ou...  117 us
    pallas_call x1, Pallas kernels, scan_backward(): pl.pallas_call(partial(scan_back_kernel, size, len(grads)), out_shape=[ja...  94.9 us
    pallas_call x1, Pallas kernels, project(): pl.pallas_call(partial(project_kernel, size, rounds), out_shape=[jax.Shap...  84 us
    all_gather x1, waiting for transfers between devices, per_device(): cot = lax.all_gather(cot_own, 'tp', axis=0, tiled=True)  49.7 us
    dot_general x6, matrix products, by_rows(): lax.dot_general(left, right, TN, preferred_element_type=f32).astype(bf16)  37.4 us
    pallas_call x1, Pallas kernels, scan_forward(): pl.pallas_call(partial(scan_kernel, size), out_shape=[jax.ShapeDtypeStruc...  26.6 us
    unnamed x66, local copies, waits for them, and re-layouts  21.1 us
  transfers between devices with their start and end apart: 2, of which 1 were waited for; matrix products, arithmetic and copies ran while one was open for 7% of the time, Pallas kernels for 32%

profile of v2, /device:TPU:0, one launch (start us, length us, event | category | flops | bytes accessed | tf_op | source)
XLA Modules:
  0.0 746.1 jit_solution(10081505266002157549)
XLA Ops:
  7.2 0.0 all-gather.2.cloned.1.call-start
  7.2 0.0 copy-start.4
  7.2 1.2 copy-done.4
  8.5 0.7 copy-done.7
  9.2 84.0 %project.1 = (bf16[4,4,64,2048]{3,2,1,0:T(8,128)(2,1)}, f32[4,4,64,512]{3,2,1,0:T(8,128)S(1)}, f32[4,4,64,512]{3,2,1,0:T(8,128)S(1)}, f32[4,4,64,512]{3,2,1,0:T(8,128)}, f32[4,4,64,512]{3,2,1,0:T(8,128)}) custom-call(bf16[4,64,2048]{2,1,0:T(8,128)(2,1)S(1)} %bitcast.79, f32[1,2048]{1,0:T(1,128)S(1)} %bitcast.85, bf16[2048,512]{1,0:T(8,128)(2,1)} %refs_4_.1, ...), custom_call_target="tpu_custom_call" | custom-call | flops 8589934592 | bytes 33554432 | tf_op jit(solution)/shard_map/project/pallas_call | solution.py:358
  93.1 0.0 copy-start
  93.1 1.3 copy-done
  94.5 1.3 copy-done.1
  95.8 0.0 all-gather.2.cloned.1.call-update
  95.8 0.0 reduce-scatter.2.cloned.1.call-start
  95.9 0.0 copy-done.23
  95.9 0.2 reduce-window.9
  96.1 0.0 copy-done.5
  96.1 0.0 copy-done.6
  96.1 26.6 %scan_forward.1 = (f32[1024,512]{1,0:T(8,128)S(1)}, bf16[1024,512]{1,0:T(8,128)(2,1)S(1)}, bf16[8,4,128,128]{3,2,1,0:T(8,128)(2,1)S(1)}) custom-call(s32[7]{0:T(128)S(1)} %bitcast.86, f32[1024,512]{1,0:T(8,128)} %bitcast.73, f32[1024,512]{1,0:T(8,128)} %bitcast.75, f32[1024,512]{1,0:T(8,128)} %bitcast.90, f32[1024,512]{1,0:T(8,128)} %bitcast.92, ...), custom_call_target="tpu_custom_call" | custom-call | flops 1342177280 | bytes 14680064 | tf_op jit(solution)/shard_map/scan_forward/pallas_call | solution.py:559
  122.7 0.0 copy-done.8
  122.7 0.0 copy-start.2
  122.7 1.3 copy-done.2
  124.1 1.0 copy-done.3
  125.0 1.0 copy-done.9
  126.0 49.7 %all-gather.2.cloned.1.call-done = bf16[1024,2048]{1,0:T(8,128)(2,1)} async-done(((bf16[256,2048]{1,0:T(8,128)(2,1)}), bf16[1024,2048]{1,0:T(8,128)(2,1)}) %all-gather.2.cloned.1.call-update) | async-done | bytes 4194320 | tf_op jit(solution)/shard_map/all_gather | solution.py:1169
  175.7 252.0 %middle.1 = (f32[4,64,2048]{2,1,0:T(8,128)}, f32[4,64,2048]{2,1,0:T(8,128)}, bf16[4,4,64,2048]{3,2,1,0:T(8,128)(2,1)}, bf16[4,4,64,2048]{3,2,1,0:T(8,128)(2,1)},...) custom-call(bf16[4,4,64,512]{3,2,1,0:T(8,128)(2,1)} %bitcast.88, ...), custom_call_target="tpu_custom_call" | custom-call | flops 33822867456 | bytes 58720256 | tf_op jit(solution)/shard_map/middle/pallas_call | solution.py:897
  427.8 0.0 copy-start.25
  427.8 6.6 copy.29
  434.3 0.0 copy-done.25
  434.4 10.6 %convert_bitcast_fusion = bf16[8,1408,256]{1,2,0:T(8,128)(2,1)} fusion(bf16[1024,8,256]{0,2,1:T(8,128)(2,1)} %bitcast.100, bf16[1024,1408,1]{1,0,2:T(8,128)(2,1)S(1)} %bitcast.119), kind=kOutput, calls=%fused_computation.2 | convolution fusion | flops 5908463616 | bytes 12845056 | tf_op jit(solution)/shard_map/tf,tnc->nfc/dot_general | solution.py:1190
  445.0 8.2 %copy.30 = bf16[8,1408,256]{2,1,0:T(8,128)(2,1)} copy(bf16[8,1408,256]{1,2,0:T(8,128)(2,1)} %convert_bitcast_fusion) | data formatting | bytes 11534336 | tf_op jit(solution)/shard_map/convert_element_type | solution.py:1190
  453.2 11.2 %convolution_convert_fusion = bf16[1024,2048]{1,0:T(8,128)(2,1)} fusion(bf16[1024,1408]{1,0:T(8,128)(2,1)S(1)} %bitcast.120, bf16[1408,2048]{1,0:T(8,128)(2,1)} %down_w.1), kind=kOutput, calls=%fused_computation.5 | convolution fusion | flops 5907677184 | bytes 12845056 | tf_op jit(solution)/shard_map/dot_general | solution.py:1175
  464.4 0.0 reduce-scatter.2.cloned.1.call-update
  464.4 0.0 copy-start.26
  464.5 0.0 copy-start.27
  464.5 3.9 copy.35
  468.3 0.0 copy-done.26
  468.3 0.7 copy-done.27
  469.0 8.6 %bitcast_convert_fusion.1 = bf16[2048,1408]{1,0:T(8,128)(2,1)} fusion(bf16[4,4,64,2048]{3,2,1,0:T(8,128)(2,1)S(1)} %copy-done.26, bf16[4,4,64,1408]{3,2,1,0:T(8,128)(2,1)S(1)} %copy-done.27), kind=kOutput, calls=%fused_computation.1 | convolution fusion | flops 5908463616 | bytes 12845056 | tf_op jit(solution)/shard_map/dot_general | solution.py:1181
  477.6 0.0 copy-done.10
  477.6 2.6 convert_bitcast_fusion.1
  480.3 2.4 copy.32
  482.7 11.0 %bitcast_convert_fusion = bf16[2048,1408]{1,0:T(8,128)(2,1)} fusion(bf16[4,4,64,2048]{3,2,1,0:T(8,128)(2,1)} %get-tuple-element.66, bf16[4,4,64,1408]{3,2,1,0:T(8,128)(2,1)} %get-tuple-element.68), kind=kOutput, calls=%fused_computation | convolution fusion | flops 5908463616 | bytes 12845056 | tf_op jit(solution)/shard_map/dot_general | solution.py:1181
  493.7 94.9 %scan_backward.1 = (bf16[1024,512]{1,0:T(8,128)(2,1)}, bf16[1024,512]{1,0:T(8,128)(2,1)}, bf16[1024,512]{1,0:T(8,128)(2,1)}, bf16[1024,512]{1,0:T(8,128)(2,1)}, ...) custom-call(s32[7]{0:T(128)} %bitcast.87, f32[1024,512]{1,0:T(8,128)} %bitcast.74, ...), custom_call_target="tpu_custom_call" | custom-call | flops 2684354560 | bytes 20971520 | tf_op jit(solution)/shard_map/scan_backward/pallas_call | solution.py:707
  588.6 0.0 copy-start.15
  588.6 0.0 copy-start.24
  588.6 6.3 convolution_convert_fusion.4
  594.9 0.0 copy-done.15
  594.9 0.0 copy-done.24
  595.0 3.8 convolution_convert_fusion.3
  598.8 0.0 copy-done.16
  598.8 3.8 convolution_convert_fusion.2
  602.5 3.9 convolution_convert_fusion.1
  606.4 116.7 %last.1 = (f32[4,64,2048]{2,1,0:T(8,128)}, f32[16,128]{1,0:T(8,128)}, f32[16,128]{1,0:T(8,128)}, f32[24,128]{1,0:T(8,128)}, f32[1408,256]{1,0:T(8,128)}, /*index...) custom-call(bf16[4,4,64,512]{3,2,1,0:T(8,128)(2,1)} %bitcast.107, ...), custom_call_target="tpu_custom_call" | custom-call | flops 8589934592 | bytes 58720256 | tf_op jit(solution)/shard_map/last/pallas_call | solution.py:1105
  723.2 1.4 dynamic_slice.12
  724.6 1.3 dynamic_slice.15
  725.8 0.8 fusion.6
  726.6 0.7 constant_dynamic-slice_fusion
  727.2 3.2 fusion.2
  730.5 1.3 copy.49
  731.8 0.8 copy.50
  732.6 0.8 copy.51
  733.4 0.8 copy.52
  734.2 0.8 copy.53
  735.0 0.8 copy.54
  735.8 1.1 copy.55
  736.9 1.1 copy.56
  738.0 1.1 copy.57
  (31 shorter events, 0.1 us)
Async XLA Ops:
  7.2 168.5 %all-gather.2.cloned.1.call-start = ((), (), s32[]{:S(2)}) async-start(), calls=%async_computation.1 | async-start | bytes 5242880 | tf_op jit(solution)/shard_map/all_gather | solution.py:1169
  7.2 1.2 copy-start.4
  8.5 0.7 copy-start.7
  9.2 86.7 %copy-start.23 = (s32[7]{0:T(128)S(1)}, s32[7]{0:T(128)}, u32[]{:S(2)}) copy-start(s32[7]{0:T(128)} %param.16) | copy-start | bytes 88
  9.2 86.9 %copy-start.5 = (f32[4,128]{1,0:T(4,128)S(1)}, f32[4,128]{1,0:T(4,128)}, u32[]{:S(2)}) copy-start(f32[4,128]{1,0:T(4,128)} %param.23) | copy-start | bytes 6148
  9.2 86.9 %copy-start.6 = (f32[4,128]{1,0:T(4,128)S(1)}, f32[4,128]{1,0:T(4,128)}, u32[]{:S(2)}) copy-start(f32[4,128]{1,0:T(4,128)} %param.24) | copy-start | bytes 6148
  93.1 1.3 copy-start
  94.5 1.3 copy-start.1
  95.8 631.4 %reduce-scatter.2.cloned.1.call-start = ((), (), s32[]{:S(2)}) async-start(), calls=%async_computation.2 | async-start | bytes 5242880 | tf_op jit(solution)/shard_map/reduce_scatter | solution.py:1176
  96.1 26.6 %copy-start.8 = (s32[7,1]{0,1:T(1,128)}, s32[7,1]{0,1:T(1,128)S(1)}, u32[]{:S(2)}) copy-start(s32[7,1]{0,1:T(1,128)S(1)} %reduce-window.9) | copy-start | bytes 88
  122.7 1.4 copy-start.2
  124.1 1.0 copy-start.3
  125.0 1.0 copy-start.9
  427.8 6.6 copy-start.25
  464.4 3.9 copy-start.26
  464.5 4.6 copy-start.27
  469.0 8.6 %copy-start.10 = (bf16[1024,512]{1,0:T(8,128)(2,1)S(1)}, bf16[1024,512]{1,0:T(8,128)(2,1)}, u32[]{:S(2)}) copy-start(bf16[1024,512]{1,0:T(8,128)(2,1)} %copy-done.9) | copy-start | bytes 3145732
  588.6 6.4 copy-start.15
  588.6 6.4 copy-start.24
  594.9 3.8 copy-start.16
  598.8 3.8 copy-start.17
  723.2 7.3 copy-start.11
  727.2 4.6 copy-start.22
  727.2 5.4 copy-start.21
  730.4 2.9 copy-start.20
  730.5 3.7 copy-start.19
  730.5 4.5 copy-start.18
  730.5 5.3 copy-start.13
  731.8 5.1 copy-start.12
  734.2 3.8 copy-start.14
Sparse Core Ops, SparseCore 0:
  95.9 79.7 all-gather.1
  464.6 74.7 reduce-scatter.1

commit v3 on v2

--- a/solution.py
+++ b/solution.py
@@ -83,7 +83,10 @@
         self.part, self.land, self.total = part, land, total
 
     def copy(self, way, j, to):
-        return self.hop(way, self.part.at[j, to], self.land.at[way, j, to], j, to)
+        return self.hop(way, self.part.at[j, to], self.slot(way, j, to), j, to)
+
+    def slot(self, way, j, to):
+        return self.land.at[way, j, to - 1 + way]
 
     def start(self, j):
         last = self.size - 1
@@ -109,7 +112,7 @@
             def _():
                 copy = self.copy(way, j, to)
                 copy.wait_recv()
-                self.add(self.part.at[j, to], self.land.at[way, j, to])
+                self.add(self.part.at[j, to], self.slot(way, j, to))
                 copy.start()
 
     def add(self, into, more):
@@ -140,7 +143,7 @@
                 self.copy(way, j, me).wait_recv()
 
                 def more(r):
-                    self.total[r, :] = self.total[r, :] + self.land[way, j, me, r, :].astype(f32)
+                    self.total[r, :] = self.total[r, :] + self.land[way, j, me - 1 + way, r, :].astype(f32)
 
                 over(more)
 
@@ -208,99 +211,210 @@
                 self.copy(1, j, source).wait_send()
 
 
+def add_rows(into, left, right):
+    rows = into.shape[0]
+
+    @pl.loop(0, rows // 16)
+    def _(g):
+        r = pl.ds(pl.multiple_of(g * 16, 16), 16)
+        into[r, :] = (left[r, :].astype(f32) + right[r, :].astype(f32)).astype(bf16)
+
+
 class GroupSum:
-    def __init__(self, size, grad, own, got, land, out, sems):
+    refs = 6
+
+    def __init__(self, size, grad, out, own, got, land, *sems):
         self.half = size // 2
         here = lax.axis_index("seq")
         self.side = lax.rem(here, 2)
         self.mine = here // 2
         self.sibling = here + 1 - 2 * self.side
         self.grad, self.own, self.got, self.land, self.out = grad, own, got, land, out
-        self.pair_sems, self.send, self.recv = sems
-
-    def near(self):
-        return remote(
-            self.grad.at[:, 1 - self.side], self.got, self.pair_sems.at[0], self.pair_sems.at[1], "seq", self.sibling
-        )
-
-    def load(self):
-        return pltpu.make_async_copy(self.grad.at[:, self.side], self.own, self.pair_sems.at[2])
+        self.near_sems, *self.sems = sems
+        self.loads = len(grad.shape) == 4
+        self.turned = out.shape != own.shape[1:]
+
+    @staticmethod
+    def scratch(shape):
+        half = shape[0]
+        return [VM(shape, bf16)] * 3 + [DMA((3, half)), DMA((half,)), DMA((half,))]
+
+    def near(self, k):
+        sems = self.near_sems
+        source = self.grad.at[k, 1 - self.side] if self.loads else self.grad.at[k]
+        return remote(source, self.got.at[k], sems.at[0, k], sems.at[1, k], "seq", self.sibling)
+
+    def load(self, k):
+        return pltpu.make_async_copy(self.grad.at[k, self.side], self.own.at[k], self.near_sems.at[2, k])
+
+    def start(self):
+        for k in range(self.half):
+            self.near(k).start()
+            if self.loads:
+                self.load(k).start()
+
+    def pair(self, k, into):
+        if self.loads:
+            self.load(k).wait()
+        self.near(k).wait_recv()
+        add_rows(into, self.own.at[k], self.got.at[k])
 
     def far(self, k):
-        return remote(
-            self.own.at[k], self.land.at[self.mine], self.send.at[k], self.recv.at[self.mine], "seq", 2 * k + self.side
-        )
+        send, recv = self.sems
+        return remote(self.own.at[k], self.land.at[self.mine], send.at[k], recv.at[self.mine], "seq", 2 * k + self.side)
 
     def arrival(self, k):
-        return remote(
-            self.own.at[k], self.land.at[k], self.send.at[k], self.recv.at[k], "seq", 2 * k + self.side
-        )
-
-    def start(self):
-        self.near().start()
-        self.load().start()
-
-    def over(self, body):
-        rows = self.own.shape[1]
-
-        @pl.loop(0, rows // 16)
-        def _(g):
-            body(pl.ds(pl.multiple_of(g * 16, 16), 16))
+        send, recv = self.sems
+        return remote(self.own.at[k], self.land.at[k], send.at[k], recv.at[k], "seq", 2 * k + self.side)
 
     def middle(self):
-        self.load().wait()
-        self.near().wait_recv()
         for k in range(self.half):
 
-            def both(r):
-                self.own[k, r, :] = (self.own[k, r, :].astype(f32) + self.got[k, r, :].astype(f32)).astype(bf16)
-
-            self.over(both)
+            @pl.when(k == self.mine)
+            def _():
+                self.pair(k, self.land.at[k])
 
             @pl.when(k != self.mine)
             def _():
+                self.pair(k, self.own.at[k])
                 self.far(k).start()
 
+    def relay(self):
+        pass
+
+    def arrive(self):
+        for k in range(self.half):
+
+            @pl.when(k != self.mine)
+            def _():
+                self.arrival(k).wait_recv()
+
+    def terms(self):
+        return [self.land.at[k] for k in range(self.half)]
+
     def finish(self):
-        def first(r):
-            self.out[r, :] = self.own[self.mine, r, :].astype(f32)
-
-        self.over(first)
+        self.arrive()
+        rows, cols = self.own.shape[1:]
+
+        def total(r, c):
+            acc = None
+            for term in self.terms():
+                part = term[r, c].astype(f32)
+                acc = part if acc is None else acc + part
+            return acc
+
+        if self.turned:
+
+            @pl.loop(0, cols // WIDTH)
+            def _(g):
+                c = pl.ds(pl.multiple_of(g * WIDTH, WIDTH), WIDTH)
+                self.out[c, :] = total(slice(None), c).T
+
+        else:
+
+            @pl.loop(0, rows // 16)
+            def _(g):
+                r = pl.ds(pl.multiple_of(g * 16, 16), 16)
+                self.out[r, :] = total(r, slice(None))
+
+    def drain(self):
         for k in range(self.half):
+            self.near(k).wait_send()
+        self.drain_far()
+
+    def drain_far(self):
+        for k in range(self.half):
 
             @pl.when(k != self.mine)
             def _():
-                self.arrival(k).wait_recv()
-
-                def more(r):
-                    self.out[r, :] = self.out[r, :] + self.land[k, r, :].astype(f32)
-
-                self.over(more)
-
-    def drain(self):
-        self.near().wait_send()
-        for k in range(self.half):
-
-            @pl.when(k != self.mine)
-            def _():
                 self.far(k).wait_send()
 
 
+class SquareSum(GroupSum):
+    refs = 6
+
+    def __init__(self, *args):
+        super().__init__(*args)
+        self.hop, self.far_sems = self.sems
+        x, y = lax.rem(self.mine, 2), self.mine // 2
+        self.beside = (2 * y + 1 - x, 2 * (1 - y) + x)
+        self.opposite = 2 * (1 - y) + 1 - x
+        rows = self.own.shape[1] // 2
+        self.halves = (pl.ds(0, rows), pl.ds(rows, rows))
+
+    @staticmethod
+    def scratch(shape):
+        half, rows, cols = shape
+        return [
+            VM(shape, bf16),
+            VM(shape, bf16),
+            VM((2, rows, cols), bf16),
+            DMA((3, half)),
+            VM((2, rows // 2, cols), bf16),
+            DMA((2, 6)),
+        ]
+
+    def over(self, way, at, source, target):
+        sems = self.far_sems
+        return remote(source, target, sems.at[0, at], sems.at[1, at], "seq", 2 * self.beside[way] + self.side)
+
+    def pass_on(self, way):
+        return self.over(way, way, self.own.at[self.opposite, self.halves[way]], self.hop.at[way])
+
+    def deliver(self, way, half):
+        source = self.own.at[self.beside[way], self.halves[half]]
+        return self.over(way, 2 + 2 * way + half, source, self.land.at[way, self.halves[half]])
+
+    def middle(self):
+        self.pair(self.opposite, self.own.at[self.opposite])
+        for way in (0, 1):
+            self.pass_on(way).start()
+        for way in (0, 1):
+            self.pair(self.beside[way], self.own.at[self.beside[way]])
+            self.deliver(way, way).start()
+        self.pair(self.mine, self.own.at[self.mine])
+
+    def relay(self):
+        for way in (0, 1):
+            self.pass_on(way).wait_recv()
+            into = self.own.at[self.beside[1 - way], self.halves[way]]
+            add_rows(into, into, self.hop.at[way])
+            self.deliver(1 - way, way).start()
+
+    def arrive(self):
+        for way in (0, 1):
+            for half in (0, 1):
+                self.deliver(way, half).wait_recv()
+
+    def terms(self):
+        return [self.own.at[self.mine], self.land.at[0], self.land.at[1]]
+
+    def drain_far(self):
+        for way in (0, 1):
+            self.pass_on(way).wait_send()
+            for half in (0, 1):
+                self.deliver(way, half).wait_send()
+
+
+def summer(size):
+    return SquareSum if size == 8 else GroupSum
+
+
 def group_sums(size, grads, outs, take):
-    sums = []
-    for grad, out in zip(grads, outs):
-        own, got, land, *sems = take(6)
-        sums.append(GroupSum(size, grad, own, got, land, out, sems))
-    return sums
-
-
-def group_sums_scratch(grads):
+    kind = summer(size)
+    return [kind(size, grad, out, *take(kind.refs)) for grad, out in zip(grads, outs)]
+
+
+def group_sums_scratch(shapes):
     scratch = []
-    for grad in grads:
-        half = grad.shape[0] // 2
-        shape = (half,) + grad.shape[1:]
-        scratch += [VM(shape, bf16), VM(shape, bf16), VM(shape, bf16), DMA((3,)), DMA((half,)), DMA((half,))]
+    for size, rows, cols in shapes:
+        scratch += summer(size).scratch((size // 2, rows, cols))
     return scratch
+
+
+def sum_shapes(shapes, turned):
+    shapes = [shape[:0:-1] if turn else shape[1:] for shape, turn in zip(shapes, turned)]
+    return [jax.ShapeDtypeStruct(shape, f32) for shape in shapes]
 
 
 def in_pairs(grad):
@@ -601,6 +715,16 @@
 
     @pl.loop(0, blocks)
     def _(back):
+        for order, each in enumerate(sums):
+
+            @pl.when(back == min(order + 1, blocks - 1))
+            def _():
+                each.middle()
+
+            @pl.when(back == blocks - 1)
+            def _():
+                each.relay()
+
         b = blocks - 1 - back
         r = pl.ds(pl.multiple_of(b * WIDTH, WIDTH), WIDTH)
         same, carry, tail, keep = block_masks(base + b * WIDTH, ends_ref)
@@ -637,9 +761,6 @@
 
     out_state[...] = state[...].astype(bf16)
     states.start(False)
-
-    for each in sums:
-        each.middle()
 
     states.compose(False, state)
 
@@ -708,7 +829,7 @@
         partial(scan_back_kernel, size, len(grads)),
         out_shape=[jax.ShapeDtypeStruct((rows, c), bf16)] * 4
         + [jax.ShapeDtypeStruct((2 * heads, WIDTH), f32)]
-        + [jax.ShapeDtypeStruct(grad.shape[1:], f32) for grad in grads],
+        + sum_shapes([grad.shape for grad in grads], [False] * len(grads)),
         in_specs=[pl.BlockSpec(memory_space=pltpu.SMEM)]
         + [spec] * 9
         + [pl.BlockSpec(memory_space=pl.ANY)] * len(grads),
@@ -716,63 +837,43 @@
         scratch_shapes=[low] * 5
         + [wide, VM((blocks, heads, WIDTH, WIDTH), f32), VM((blocks, 8, WIDTH), f32)]
         + states_scratch(size, heads)
-        + group_sums_scratch(grads),
+        + group_sums_scratch([grad.shape for grad in grads]),
         compiler_params=pltpu.CompilerParams(collective_id=2, has_side_effects=True, vmem_limit_bytes=60 * MIB),
         cost_estimate=pl.CostEstimate(flops=40 * rows * c * WIDTH, bytes_accessed=20 * MIB, transcendentals=16 * rows * c),
         name="scan_backward",
     )(ends, q, f, i, s, bound, gain, o, starts, ub, *[in_pairs(grad) for grad in grads])
 
 
-def middle_kernel(
-    size,
-    rounds,
-    u_ref,
-    x_ref,
-    cot_ref,
-    gain_ref,
-    out_w,
-    gate_w,
-    up_w,
-    down_w,
-    res_ref,
-    back_ref,
-    b_ref,
-    e_ref,
-    ub_ref,
-    second_ref,
-    hidden_out,
-    gate_out,
-    up_out,
-    part,
-    land,
-    total,
-    hidden,
-    gate_back,
-    up_back,
-    keep_sems,
-    s_send,
-    s_recv,
-    g_send,
-    g_recv,
-    s_send2,
-    s_recv2,
-    g_send2,
-    g_recv2,
-):
-    greet(*line_peers(size))
+def middle_kernel(size, rounds, *refs):
+    take = taker(refs)
+    u_ref, x_ref, gain_ref, out_w, *loaded = take(8)
+    res_out, back_out, e_out, ub_out, second_ref, down_out, *grad_outs = take(9)
+    gate_w, up_w, down_w, cot_ref = weights = take(4)
+    b_ref, e_ref, res_ref, back_ref, ub_ref, part, land, total = take(8)
+    wide = take(3)
+    down_ref, *tiles = take(4)
+    load_sems, res_sems, back_sems, e_sems, ub_sem, down_sem, tile_sems = take(7)
+    lines = [take(2) for _ in range(4)]
+    hidden, gate_back, up_back = wide
     me = lax.axis_index("tp")
     m, d = x_ref.shape[1:]
     ff = gate_w.shape[1]
-    scatter = Scatter(size, s_send, s_recv, part, land, total)
-    gather = Gather(size, g_send, g_recv, b_ref)
-    scatter_back = Scatter(size, s_send2, s_recv2, part, land, total)
-    gather_back = Gather(size, g_send2, g_recv2, e_ref)
+    group = size * m
+    scatter = Scatter(size, *lines[0], part, land, total)
+    gather = Gather(size, *lines[1], b_ref)
+    scatter_back = Scatter(size, *lines[2], part, land, total)
+    gather_back = Gather(size, *lines[3], e_ref)
     gain = gain_ref[...]
+    tile = min(512, d)
+    local = pltpu.make_async_copy
+    loads = [local(src, dst, load_sems.at[k]) for k, (src, dst) in enumerate(zip(loaded, weights))]
+    for load in loads:
+        load.start()
     second_ref[...] = jnp.zeros_like(second_ref)
-    tile = min(512, d)
+    greet(*line_peers(size))
 
     def project_out(j):
-        rows = u_ref[:, j].reshape(size * m, u_ref.shape[3])
+        rows = u_ref[:, j].reshape(group, u_ref.shape[3])
 
         @pl.loop(0, d // tile)
         def _(n):
@@ -780,6 +881,21 @@
             part[j, :, :, cols] = mul(rows, out_w[:, cols], NN).astype(bf16).reshape(size, m, tile)
 
         scatter.start(j)
+
+    def res_copy(j):
+        return local(res_ref.at[j], res_out.at[j], res_sems.at[j])
+
+    def back_copy(j):
+        return local(back_ref.at[j], back_out.at[j], back_sems.at[j])
+
+    def e_copy(j):
+        return local(e_ref.at[:, j], e_out.at[:, j], e_sems.at[j])
+
+    def ub_copy(j):
+        return local(ub_ref, ub_out.at[:, j], ub_sem.at[0])
+
+    def down_copy(j):
+        return local(down_ref, down_out.at[:, j], down_sem.at[0])
 
     def norm(j):
         @pl.loop(0, m // 16)
@@ -791,22 +907,17 @@
             b_ref[me, j, r, :] = (residual * scale * gain).astype(bf16)
 
         gather.start(j)
-
-    def kept(j):
-        return [
-            pltpu.make_async_copy(src, dst.at[:, j], keep_sems.at[k])
-            for k, (src, dst) in enumerate(((hidden, hidden_out), (gate_back, gate_out), (up_back, up_out)))
-        ]
+        res_copy(j).start()
 
     def feed(j):
-        @pl.when(j > 0)
+        @pl.when(j == 0)
         def _():
-            for copy in kept(j - 1):
-                copy.wait()
-
-        rows = b_ref[:, j].reshape(size * m, d)
-        cot = cot_ref[:, j].reshape(size * m, d)
-        step = 512
+            for load in loads:
+                load.wait()
+
+        rows = b_ref[:, j].reshape(group, d)
+        cot = cot_ref[:, j].reshape(group, d)
+        step = 256
         for low in range(0, ff, step):
             cols = slice(low, min(low + step, ff))
             width = cols.stop - cols.start
@@ -816,16 +927,14 @@
             sig = jax.nn.sigmoid(gate)
             act = gate * sig
             shape = (size, m, width)
-            hidden[:, :, cols] = (act * up).astype(bf16).reshape(shape)
-            up_back[:, :, cols] = (hb * act).astype(bf16).reshape(shape)
-            gate_back[:, :, cols] = (hb * up * (sig * (1.0 + gate * (1.0 - sig)))).astype(bf16).reshape(shape)
-        for copy in kept(j):
-            copy.start()
+            hidden[:, j, :, cols] = (act * up).astype(bf16).reshape(shape)
+            up_back[:, j, :, cols] = (hb * act).astype(bf16).reshape(shape)
+            gate_back[:, j, :, cols] = (hb * up * (sig * (1.0 + gate * (1.0 - sig)))).astype(bf16).reshape(shape)
 
     def feed_back(j):
         scatter.drain(j)
-        gates = gate_back[...].reshape(size * m, ff)
-        ups = up_back[...].reshape(size * m, ff)
+        gates = gate_back[:, j].reshape(group, ff)
+        ups = up_back[:, j].reshape(group, ff)
 
         @pl.loop(0, d // tile)
         def _(n):
@@ -834,6 +943,20 @@
             part[j, :, :, cols] = sums.astype(bf16).reshape(size, m, tile)
 
         scatter_back.start(j)
+
+    def feed_out(j):
+        @pl.when(j > 0)
+        def _():
+            down_copy(j - 1).wait()
+
+        rows = hidden[:, j].reshape(group, ff)
+
+        @pl.loop(0, d // tile)
+        def _(n):
+            cols = pl.ds(pl.multiple_of(n * tile, tile), tile)
+            down_ref[:, :, cols] = mul(rows, down_w[:, cols], NN).astype(bf16).reshape(size, m, tile)
+
+        down_copy(j).start()
 
     def norm_back(j):
         @pl.loop(0, m // 16)
@@ -851,12 +974,44 @@
             e_ref[me, j, r, :] = back.astype(bf16)
 
         gather_back.start(j)
-
-    def unproject(j):
-        rows = e_ref[:, j].reshape(size * m, d)
-        ub_ref[:, j] = mul(rows, out_w[...], NT).reshape(size, m, out_w.shape[0])
-
-    @pl.loop(0, rounds + 4)
+        back_copy(j).start()
+
+    def unproject(j, wait):
+        e_copy(j).start()
+
+        @pl.when(wait)
+        def _():
+            ub_copy(j - 1).wait()
+
+        rows = e_ref[:, j].reshape(group, d)
+        ub_ref[...] = mul(rows, out_w[...], NT).reshape(size, m, out_w.shape[0])
+        ub_copy(j).start()
+
+    depth = tiles[0].shape[0]
+    count = d // depth
+
+    def tile_copies(n):
+        rows = pl.ds(pl.multiple_of(n * depth, depth), depth)
+        return [local(src, dst.at[rows, :], tile_sems.at[k]) for k, (src, dst) in enumerate(zip(tiles, grad_outs))]
+
+    def weight_tiles(low, high):
+        @pl.loop(low, high)
+        def _(n):
+            @pl.when(n > 0)
+            def _():
+                for copy in tile_copies(n - 1):
+                    copy.wait()
+
+            cols = pl.ds(pl.multiple_of(n * depth, depth), depth)
+            for left, right, out in zip((b_ref, b_ref, cot_ref), (gate_back, up_back, hidden), tiles):
+                rows = left[:, :, :, cols].reshape(rounds * group, depth)
+                out[...] = mul(rows, right[...].reshape(rounds * group, ff), TN).astype(bf16)
+            for copy in tile_copies(n):
+                copy.start()
+
+    final = rounds - 1
+
+    @pl.loop(0, rounds + 2)
     def _(i):
         def stage(lag, body):
             @pl.when((i >= lag) & (i < rounds + lag))
@@ -875,13 +1030,37 @@
             stage(4, lambda j: gather_back.step(j, t))
         stage(2, feed)
         stage(2, feed_back)
-        stage(4, unproject)
-
-    for copy in kept(rounds - 1):
+        stage(2, feed_out)
+        stage(4, lambda j: unproject(j, j > 0))
+
+    shares = [count * k // 5 for k in range(6)]
+    for t in range(1, size):
+        if t < size - 1:
+            scatter_back.step(final, t)
+        else:
+            scatter_back.finish(final)
+            norm_back(final)
+        gather_back.step(final - 1, t)
+        if t < size - 1:
+            weight_tiles(shares[t - 1], shares[t])
+    unproject(final - 1, True)
+    weight_tiles(shares[2], shares[3])
+    for t in range(1, size):
+        gather_back.step(final, t)
+        if t < size - 1:
+            weight_tiles(shares[t + 2], shares[t + 3])
+    unproject(final, True)
+
+    for copy in tile_copies(count - 1):
         copy.wait()
+    ub_copy(final).wait()
+    down_copy(final).wait()
 
     @pl.loop(0, rounds)
     def _(j):
+        res_copy(j).wait()
+        back_copy(j).wait()
+        e_copy(j).wait()
         gather.drain(j)
         scatter_back.drain(j)
         gather_back.drain(j)
@@ -893,57 +1072,65 @@
     c, ff = out_w.shape[0], gate_w.shape[1]
     shape = (size, rounds, m)
     sems = DMA((2, rounds, size))
-    wide = VM((size, m, ff), bf16)
+    spec, far = pl.BlockSpec(memory_space=VM), pl.BlockSpec(memory_space=pl.ANY)
+    depth = min(256, d)
     outs = pl.pallas_call(
         partial(middle_kernel, size, rounds),
         out_shape=[
             jax.ShapeDtypeStruct((rounds, m, d), f32),
             jax.ShapeDtypeStruct((rounds, m, d), f32),
             jax.ShapeDtypeStruct(shape + (d,), bf16),
-            jax.ShapeDtypeStruct(shape + (d,), bf16),
             jax.ShapeDtypeStruct(shape + (c,), f32),
             jax.ShapeDtypeStruct((1, d), f32),
+            jax.ShapeDtypeStruct(shape + (d,), bf16),
         ]
-        + [jax.ShapeDtypeStruct(shape + (ff,), bf16)] * 3,
-        in_specs=[pl.BlockSpec(memory_space=VM)] * 8,
-        out_specs=[pl.BlockSpec(memory_space=VM)] * 6 + [pl.BlockSpec(memory_space=pl.ANY)] * 3,
+        + [jax.ShapeDtypeStruct((d, ff), bf16)] * 3,
+        in_specs=[spec] * 4 + [far] * 4,
+        out_specs=[far] * 4 + [spec] + [far] * 4,
         scratch_shapes=[
+            VM(gate_w.shape, bf16),
+            VM(up_w.shape, bf16),
+            VM(down_w.shape, bf16),
+            VM(shape + (d,), bf16),
+            VM(shape + (d,), bf16),
+            VM(shape + (d,), bf16),
+            VM((rounds, m, d), f32),
+            VM((rounds, m, d), f32),
+            VM((size, m, c), f32),
             VM((rounds, size, m, d), bf16),
-            VM((2, rounds, size, m, d), bf16),
+            VM((2, rounds, size - 1, m, d), bf16),
             VM((m, d), f32),
-            wide,
-            wide,
-            wide,
-            DMA((3,)),
         ]
+        + [VM(shape + (ff,), bf16)] * 3
+        + [VM((size, m, d), bf16)]
+        + [VM((depth, ff), bf16)] * 3
+        + [DMA((4,)), DMA((rounds,)), DMA((rounds,)), DMA((rounds,)), DMA((1,)), DMA((1,)), DMA((3,))]
         + [sems] * 8,
         compiler_params=pltpu.CompilerParams(collective_id=3, has_side_effects=True, vmem_limit_bytes=63 * MIB),
         cost_estimate=pl.CostEstimate(
-            flops=2 * size * rows * d * (2 * c + 5 * ff), bytes_accessed=56 * MIB, transcendentals=size * rows * ff
+            flops=2 * size * rows * d * (2 * c + 9 * ff), bytes_accessed=56 * MIB, transcendentals=size * rows * ff
         ),
         name="middle",
     )(
         u.reshape(shape + (c,)),
         x.reshape(rounds, m, d),
-        cot.reshape(shape + (d,)),
         gain.reshape(1, d),
         out_w,
         gate_w,
         up_w,
         down_w,
+        cot.reshape(shape + (d,)),
     )
-    res, back, b, e, ub, second, hidden, gates, ups = outs
+    res, back, e, ub, second, down, *grads = outs
     total = size * rows
     return (
         res.reshape(rows, d),
         back.reshape(rows, d),
-        b.reshape(total, d),
         e.reshape(total, d),
         ub.reshape(total, c),
         second,
-        hidden.reshape(total, ff),
-        gates.reshape(total, ff),
-        ups.reshape(total, ff),
+        down.reshape(total, d),
+        *grads,
     )
 
 
@@ -993,25 +1180,36 @@
         into[at + k : at + k + 1, :] = vector[:, k * WIDTH : (k + 1) * WIDTH]
 
 
-def last_kernel(size, groups, rounds, count, *refs):
+def last_kernel(size, groups, rounds, count, mixed, *refs):
     take = taker(refs)
     backs, weights = take(4), take(4)
-    x_ref, back_ref, gain_ref, second_ref, small_ref = take(5)
+    x_ref, gain_ref, second_ref, small_ref, back_in = take(5)
+    a_in = take(1 if mixed else 0)
     grads = take(count)
     tokens_out, second_out, first_out, small_out = take(4)
-    grad_outs = take(count)
+    grad_outs = take(count + (4 if mixed else 0))
     part, land, total, first, s_send, s_recv = take(6)
     small_seq, gain_seq, second_tp, first_tp = (take(3) for _ in range(4))
-    sums = group_sums(groups, grads, grad_outs, take)
+    nears, a_refs = take(4 if mixed else 0), take(1 if mixed else 0)
+    load_sems = take(1)[0]
+    sums = group_sums(groups, grads + nears, grad_outs, take)
+    early, late = sums[:2], sums[2:]
 
     seq, seq_count = group_peers(groups, "seq")
     tp, tp_count = group_peers(size, "tp")
     greet(seq + tp, seq_count + tp_count)
 
-    for each in sums:
+    for each in sums[:count]:
         each.start()
+    loads = [
+        pltpu.make_async_copy(source, target, load_sems.at[k])
+        for k, (source, target) in enumerate(zip([back_in, *a_in], [tokens_out, *a_refs]))
+    ]
+    for load in loads:
+        load.start()
 
     m, d = x_ref.shape[1:]
+    group = size * m
     scatter = Scatter(size, s_send, s_recv, part, land, total)
     gain = gain_ref[...]
     first[...] = jnp.zeros_like(first)
@@ -1032,11 +1230,25 @@
             cols = pl.ds(pl.multiple_of(n * tile, tile), tile)
             acc = None
             for back, weight in zip(backs, weights):
-                term = mul(back[:, j].reshape(size * m, back.shape[3]), weight[cols, :], NT)
+                term = mul(back[:, j].reshape(group, back.shape[3]), weight[cols, :], NT)
                 acc = term if acc is None else acc + term
             part[j, :, :, cols] = acc.astype(bf16).reshape(size, m, tile)
 
         scatter.start(j)
+
+    def mix(back, each):
+        rows = back[...].reshape(rounds * group, back.shape[3])
+        depth = each.own.shape[1]
+        for side, into in ((1 - each.side, each.grad), (each.side, each.own)):
+
+            @pl.loop(0, each.half)
+            def _(k):
+                cols = pl.ds(pl.multiple_of((2 * k + side) * depth, depth), depth)
+                left = a_refs[0][:, :, :, cols].reshape(rounds * group, depth)
+                into[k] = mul(left, rows, TN).astype(bf16)
+
+            if into is each.grad:
+                each.start()
 
     def norm_back(j):
         @pl.loop(0, m // 16)
@@ -1047,41 +1259,57 @@
             normed = x * scale
             first[...] += jnp.sum(a_back * normed, axis=0, keepdims=True)
             inner = a_back * gain
-            tokens_out[j, r, :] = back_ref[j, r, :] + scale * (
+            tokens_out[j, r, :] = tokens_out[j, r, :] + scale * (
                 inner - normed * jnp.mean(inner * normed, axis=-1, keepdims=True)
             )
 
-    @pl.loop(0, rounds)
-    def _(j):
-        products(j)
-
-    for each in sums[: count // 2]:
-        each.middle()
-
-    seq_small.finish(small_out)
-    second_tp[0][...] = small_out[:lines, :]
-    tp_second.start()
-
-    for each in sums[count // 2 :]:
-        each.middle()
-
-    @pl.loop(0, rounds)
-    def _(j):
-        for t in range(1, size):
+    def steps(j, low, high):
+        for t in range(low, high):
             if t < size - 1:
                 scatter.step(j, t)
             else:
                 scatter.finish(j)
-        norm_back(j)
+                norm_back(j)
+
+    for j in range(rounds):
+        products(j)
+        if j < len(early):
+            early[j].middle()
+    for load in loads:
+        load.wait()
+    if mixed:
+        for at, (back, each) in enumerate(zip(backs, late)):
+            mix(back, each)
+            steps(0, 1, 2) if at == 1 else None
+            steps(0, 2, 3) if at == 3 else None
+    else:
+        steps(0, 1, 3)
+    for each in early:
+        each.relay()
+    for each in late:
+        each.middle()
+    seq_small.finish(small_out)
+    second_tp[0][...] = small_out[:lines, :]
+    tp_second.start()
+    steps(0, 3, size)
+    for j in range(1, rounds):
+        steps(j, 1, size)
+        if j == 1:
+            for each in late[:2]:
+                each.relay()
+        if j == 2:
+            for each in late[2:]:
+                each.relay()
+            early[0].finish()
 
     stack(first[...], gain_seq[0], 0)
     seq_first.start()
     tp_second.finish(second_out)
-    for each in sums[: count // 2]:
+    for each in early[1:]:
         each.finish()
     seq_first.finish(first_tp[0])
     tp_first.start()
-    for each in sums[count // 2 :]:
+    for each in late:
         each.finish()
     tp_first.finish(first_out)
 
@@ -1093,7 +1321,7 @@
         scatter.drain(j)
 
 
-def last(size, groups, rounds, backs, weights, x, back, gain, second, small, grads):
+def last(size, groups, rounds, backs, weights, a, x, back, gain, second, small, grads, turned):
     rows, d = x.shape
     m = rows // rounds
     c = weights[0].shape[1]
@@ -1102,20 +1330,22 @@
     sems = DMA((2, rounds, size))
     spec = pl.BlockSpec(memory_space=VM)
     small_rows = lines + small.shape[0]
+    mixed = a is not None
+    shapes = [grad.shape for grad in grads] + ([(groups, d // groups, c)] * 4 if mixed else [])
     outs = pl.pallas_call(
-        partial(last_kernel, size, groups, rounds, len(grads)),
+        partial(last_kernel, size, groups, rounds, len(grads), mixed),
         out_shape=[
             jax.ShapeDtypeStruct((rounds, m, d), f32),
             jax.ShapeDtypeStruct((lines, WIDTH), f32),
             jax.ShapeDtypeStruct((lines, WIDTH), f32),
             jax.ShapeDtypeStruct((small_rows, WIDTH), f32),
         ]
-        + [jax.ShapeDtypeStruct(grad.shape[1:], f32) for grad in grads],
-        in_specs=[spec] * 13 + [pl.BlockSpec(memory_space=pl.ANY)] * len(grads),
-        out_specs=[spec] * (4 + len(grads)),
+        + sum_shapes(shapes, turned),
+        in_specs=[spec] * 12 + [pl.BlockSpec(memory_space=pl.ANY)] * (1 + mixed + len(grads)),
+        out_specs=[spec] * (4 + len(shapes)),
         scratch_shapes=[
             VM((rounds, size, m, d), bf16),
-            VM((2, rounds, size, m, d), bf16),
+            VM((2, rounds, size - 1, m, d), bf16),
             VM((m, d), f32),
             VM((1, d), f32),
             sems,
@@ -1125,18 +1355,21 @@
         + everyone_scratch(groups, lines)
         + everyone_scratch(size, lines)
         + everyone_scratch(size, lines)
-        + group_sums_scratch(grads),
+        + ([VM((groups // 2, d // groups, c), bf16)] * 4 + [VM(shape + (d,), bf16)] if mixed else [])
+        + [DMA((2,))]
+        + group_sums_scratch(shapes),
         compiler_params=pltpu.CompilerParams(collective_id=4, has_side_effects=True, vmem_limit_bytes=63 * MIB),
-        cost_estimate=pl.CostEstimate(flops=8 * size * rows * d * c, bytes_accessed=56 * MIB, transcendentals=0),
+        cost_estimate=pl.CostEstimate(flops=16 * size * rows * d * c, bytes_accessed=56 * MIB, transcendentals=0),
         name="last",
     )(
         *[part.reshape(shape + (c,)) for part in backs],
         *weights,
         x.reshape(rounds, m, d),
-        back.reshape(rounds, m, d),
         gain.reshape(1, d),
         second,
         small,
+        back.reshape(rounds, m, d),
+        *([a.reshape(shape + (d,))] if mixed else []),
         *[in_pairs(grad) for grad in grads],
     )
     return (outs[0].reshape(rows, d), outs[1], outs[2], outs[3][lines:]) + tuple(outs[4:])
@@ -1168,36 +1401,43 @@
     cot_own, q = lax.optimization_barrier((cotangent, q))
     cot = lax.all_gather(cot_own, "tp", axis=0, tiled=True)
     o, u, starts = scan_forward(groups, ends, q, f, i, s, bound, head_gain)
-    residual, back, b, e, ub, second, hidden, gates, ups = middle(
+    residual, back, e, ub, second, down, *glu = middle(
         size, ROUNDS, u, tokens, cot, second_gain, out_weight, gate_weight, up_weight, down_weight
     )
-    hidden_2, ub = lax.optimization_barrier((hidden, ub))
-    down = jnp.dot(hidden_2, down_weight, preferred_element_type=f32).astype(bf16)
+    down, ub = lax.optimization_barrier((down, ub))
     down = lax.psum_scatter(down, "tp", scatter_dimension=0, tiled=True)
     output = (residual + down.astype(f32)).astype(bf16)
-    total, d = b.shape
-
-    def by_rows(left, right):
-        grad = lax.dot_general(left, right, TN, preferred_element_type=f32).astype(bf16)
+    d = tokens.shape[1]
+
+    def chunks(grad):
         return grad.reshape(groups, grad.shape[0] // groups, grad.shape[1])
 
-    narrow = d // groups < WIDTH
-
-    def by_cols(left, right):
-        if narrow:
-            return by_rows(right, left)
-        right = right.reshape(total, groups, right.shape[1] // groups)
-        return jnp.einsum("tf,tnc->nfc", left, right, preferred_element_type=f32).astype(bf16)
-
-    glu = [by_rows(b, gates), by_rows(b, ups)]
+    def grad_of(left, right):
+        return chunks(lax.dot_general(left, right, TN, preferred_element_type=f32).astype(bf16))
+
+    gates, ups, downs = (chunks(grad) for grad in glu)
     dq, df, di, ds, small, gate_grad, up_grad = scan_backward(
-        groups, ends, q, f, i, s, bound, head_gain, o, starts, ub, glu
+        groups, ends, q, f, i, s, bound, head_gain, o, starts, ub, [gates, ups]
     )
-    others = [by_cols(hidden, cot), by_cols(u, e)]
-    mix = [by_rows(a, part) for part in (dq, df, di, ds)]
+    back_rows = (dq, df, di, ds)
+    here_too = groups == 8
+    others = [downs, grad_of(e, u)] + ([] if here_too else [grad_of(a, part) for part in back_rows])
     tokens_grad, second_sum, first_sum, small_sum, *sums = last(
-        size, groups, ROUNDS, (dq, df, di, ds), weights, tokens, back, first_gain, second, small, others + mix
+        size,
+        groups,
+        ROUNDS,
+        back_rows,
+        weights,
+        a if here_too else None,
+        tokens,
+        back,
+        first_gain,
+        second,
+        small,
+        others,
+        [True, True] + [False] * 4,
     )
+    down_grad, out_grad, query_grad, forget_grad, input_grad, swish_grad = sums
     heads = bound_logit.shape[0]
     here = lax.axis_index("seq")
     place = here * size + lax.axis_index("tp")
@@ -1207,9 +1447,6 @@
     second_grad = lax.dynamic_slice_in_dim(second_sum.reshape(-1), place * each, each)
     bound_grad = lax.dynamic_slice_in_dim(small_sum[:heads], here * wide, wide, axis=1)
     head_grad = lax.dynamic_slice_in_dim(small_sum[heads:], here * wide, wide, axis=1)
-    down_grad, out_grad, query_grad, forget_grad, input_grad, swish_grad = sums
-    if narrow:
-        down_grad, out_grad = down_grad.T, out_grad.T
     return (
         output,
         tokens_grad,

time: 750 us -> 659 us (0.88)
  matrix products: 61.9 us -> 5.89 us
  local copies, waits for them, and re-layouts: 42.3 us -> 21.2 us
  Pallas kernels: 574 us -> 557 us
    dot_general x9 -> x1, matrix products: 61.9 us -> 5.89 us  [grad_of(): lax.dot_general(left, right, TN, preferred_element_type=f32).astype(bf16)]
    pallas_call x1, Pallas kernels: 117 us -> 106 us  [last(): pl.pallas_call(partial(last_kernel, size, groups, rounds, len(grads), mix...]
    convert_element_type x2 -> x0, local copies, waits for them, and re-layouts: 10.6 us -> none  [by_cols(): jnp.einsum('tf,tnc->nfc', left, right, preferred_element_type=f32)]
    unnamed x66 -> x51, local copies, waits for them, and re-layouts: 21.1 us -> 17.3 us
  transfers between devices with their start and end apart: 2 -> 2, of which waited for: 1 -> 1; matrix products, arithmetic and copies ran while one was open for 7% -> 2% of each run, Pallas kernels for 32% -> 35%
where the time goes in v3:
time: 659 us; the launch traced here: 652 us
  Pallas kernels  557 us (85%)
  waiting for transfers between devices  49.8 us (8%)
  local copies, waits for them, and re-layouts  21.2 us (3%)
  between operations  14.4 us (2%)
    pallas_call x1, Pallas kernels, middle(): pl.pallas_call(partial(middle_kernel, size, rounds), out_shape=[jax.Shape...  247 us
    pallas_call x1, Pallas kernels, last(): pl.pallas_call(partial(last_kernel, size, groups, rounds, len(grads), mix...  106 us
    pallas_call x1, Pallas kernels, scan_backward(): pl.pallas_call(partial(scan_back_kernel, size, len(grads)), out_shape=[ja...  93.8 us
    pallas_call x1, Pallas kernels, project(): pl.pallas_call(partial(project_kernel, size, rounds), out_shape=[jax.Shap...  84.3 us
    all_gather x1, waiting for transfers between devices, per_device(): cot = lax.all_gather(cot_own, 'tp', axis=0, tiled=True)  49.8 us
    pallas_call x1, Pallas kernels, scan_forward(): pl.pallas_call(partial(scan_kernel, size), out_shape=[jax.ShapeDtypeStruc...  26.6 us
    unnamed x51, local copies, waits for them, and re-layouts  17.3 us
  transfers between devices with their start and end apart: 2, of which 1 were waited for; matrix products, arithmetic and copies ran while one was open for 2% of the time, Pallas kernels for 35%

profile of v3, /device:TPU:0, one launch (start us, length us, event | category | flops | bytes accessed | tf_op | source)
XLA Modules:
  0.0 651.7 jit_solution(9150375134343016292)
XLA Ops:
  7.2 0.0 all-gather.2.cloned.1.call-start
  7.2 0.0 copy-start.7
  7.2 1.2 copy-done.7
  8.5 0.0 copy-start.10
  8.5 0.7 copy-done.10
  9.2 0.0 copy-start.20
  9.2 0.0 copy-start.4
  9.2 84.3 %project.1 = (bf16[4,4,64,2048]{3,2,1,0:T(8,128)(2,1)}, f32[4,4,64,512]{3,2,1,0:T(8,128)S(1)}, f32[4,4,64,512]{3,2,1,0:T(8,128)S(1)}, f32[4,4,64,512]{3,2,1,0:T(8,128)}, f32[4,4,64,512]{3,2,1,0:T(8,128)}) custom-call(bf16[4,64,2048]{2,1,0:T(8,128)(2,1)S(1)} %bitcast.45, f32[1,2048]{1,0:T(1,128)S(1)} %bitcast.48, bf16[2048,512]{1,0:T(8,128)(2,1)} %refs_4_.3, ...), custom_call_target="tpu_custom_call" | custom-call | flops 8589934592 | bytes 33554432 | tf_op jit(solution)/shard_map/project/pallas_call | solution.py:472
  93.4 0.0 copy-start
  93.4 1.3 copy-done
  94.8 0.0 copy-start.1
  94.8 1.3 copy-done.1
  96.1 0.0 all-gather.2.cloned.1.call-update
  96.1 0.0 reduce-scatter.2.cloned.1.call-start
  96.1 0.0 copy-done.20
  96.2 0.2 reduce-window.9
  96.3 0.0 copy-start.6
  96.3 0.0 copy-done.4
  96.3 0.0 copy-done.5
  96.3 26.6 %scan_forward.1 = (f32[1024,512]{1,0:T(8,128)S(1)}, bf16[1024,512]{1,0:T(8,128)(2,1)S(1)}, bf16[8,4,128,128]{3,2,1,0:T(8,128)(2,1)S(1)}) custom-call(s32[7]{0:T(128)S(1)} %bitcast.41, f32[1024,512]{1,0:T(8,128)} %bitcast.33, f32[1024,512]{1,0:T(8,128)} %bitcast.35, f32[1024,512]{1,0:T(8,128)} %bitcast.49, f32[1024,512]{1,0:T(8,128)} %bitcast.51, ...), custom_call_target="tpu_custom_call" | custom-call | flops 1342177280 | bytes 14680064 | tf_op jit(solution)/shard_map/scan_forward/pallas_call | solution.py:673
  123.0 0.0 copy-done.6
  123.0 0.0 copy-start.2
  123.0 1.3 copy-done.2
  124.3 0.0 copy-start.3
  124.3 1.0 copy-done.3
  125.3 0.0 copy-start.8
  125.3 1.0 copy-done.8
  126.3 49.8 %all-gather.2.cloned.1.call-done = bf16[1024,2048]{1,0:T(8,128)(2,1)} async-done(((bf16[256,2048]{1,0:T(8,128)(2,1)}), bf16[1024,2048]{1,0:T(8,128)(2,1)}) %all-gather.2.cloned.1.call-update) | async-done | bytes 4194320 | tf_op jit(solution)/shard_map/all_gather | solution.py:1402
  176.0 246.6 %middle.1 = (f32[4,64,2048]{2,1,0:T(8,128)}, f32[4,64,2048]{2,1,0:T(8,128)}, bf16[4,4,64,2048]{3,2,1,0:T(8,128)(2,1)}, f32[4,4,64,512]{3,2,1,0:T(8,128)}, f32[1,...) custom-call(bf16[4,4,64,512]{3,2,1,0:T(8,128)(2,1)} %bitcast.46, ...), custom_call_target="tpu_custom_call" | custom-call | flops 57445187584 | bytes 58720256 | tf_op jit(solution)/shard_map/middle/pallas_call | solution.py:1077
  422.6 0.0 reduce-scatter.2.cloned.1.call-update
  422.6 0.0 copy-start.9
  422.6 93.8 %scan_backward.1 = (bf16[1024,512]{1,0:T(8,128)(2,1)}, bf16[1024,512]{1,0:T(8,128)(2,1)}, bf16[1024,512]{1,0:T(8,128)(2,1)}, bf16[1024,512]{1,0:T(8,128)(2,1)}, ...) custom-call(s32[7]{0:T(128)} %bitcast.42, f32[1024,512]{1,0:T(8,128)} %bitcast.34, ...), custom_call_target="tpu_custom_call" | custom-call | flops 2684354560 | bytes 20971520 | tf_op jit(solution)/shard_map/scan_backward/pallas_call | solution.py:828
  516.5 0.0 copy-done.9
  516.5 5.9 convolution_convert_fusion
  522.4 105.7 %last.1 = (f32[4,64,2048]{2,1,0:T(8,128)}, f32[16,128]{1,0:T(8,128)}, f32[16,128]{1,0:T(8,128)}, f32[24,128]{1,0:T(8,128)}, f32[1408,256]{1,0:T(8,128)}, /*index...) custom-call(bf16[4,4,64,512]{3,2,1,0:T(8,128)(2,1)} %bitcast.59, ...), custom_call_target="tpu_custom_call" | custom-call | flops 17179869184 | bytes 58720256 | tf_op jit(solution)/shard_map/last/pallas_call | solution.py:1335
  628.0 1.3 dynamic_slice.12
  629.3 1.3 dynamic_slice.15
  630.6 0.8 fusion.1
  631.3 0.7 constant_dynamic-slice_fusion
  632.0 0.0 reduce-scatter.2.cloned.1.call-done
  632.0 0.0 copy-start.11
  632.0 3.3 fusion
  635.2 0.0 copy-done.11
  635.3 0.0 copy-start.19
  635.3 0.0 copy-start.18
  635.3 1.3 copy.38
  636.6 0.1 copy-done.19
  636.6 0.0 copy-start.16
  636.6 0.0 copy-start.15
  636.6 0.8 copy.39
  637.4 0.0 copy-done.18
  637.4 0.8 copy.40
  638.2 0.0 copy-done.17
  638.2 0.8 copy.41
  639.0 0.0 copy-done.16
  639.0 0.8 copy.42
  639.8 0.0 copy-done.15
  639.8 0.8 copy.43
  640.6 0.0 copy-done.13
  640.6 1.1 copy.44
  641.7 0.0 copy-done.12
  641.7 1.1 copy.45
  642.8 0.8 copy-done.14
  643.6 1.1 copy.46
  (5 shorter events, 0.0 us)
Async XLA Ops:
  7.2 168.8 %all-gather.2.cloned.1.call-start = ((), (), s32[]{:S(2)}) async-start(), calls=%async_computation.1 | async-start | bytes 5242880 | tf_op jit(solution)/shard_map/all_gather | solution.py:1402
  7.2 1.2 copy-start.7
  8.5 0.7 copy-start.10
  9.2 87.0 %copy-start.20 = (s32[7]{0:T(128)S(1)}, s32[7]{0:T(128)}, u32[]{:S(2)}) copy-start(s32[7]{0:T(128)} %param.16) | copy-start | bytes 88
  9.2 87.2 %copy-start.4 = (f32[4,128]{1,0:T(4,128)S(1)}, f32[4,128]{1,0:T(4,128)}, u32[]{:S(2)}) copy-start(f32[4,128]{1,0:T(4,128)} %param.23) | copy-start | bytes 6148
  9.2 87.2 %copy-start.5 = (f32[4,128]{1,0:T(4,128)S(1)}, f32[4,128]{1,0:T(4,128)}, u32[]{:S(2)}) copy-start(f32[4,128]{1,0:T(4,128)} %param.24) | copy-start | bytes 6148
  93.4 1.3 copy-start
  94.8 1.3 copy-start.1
  96.1 535.9 %reduce-scatter.2.cloned.1.call-start = ((), (), s32[]{:S(2)}) async-start(), calls=%async_computation.2 | async-start | bytes 5242880 | tf_op jit(solution)/shard_map/reduce_scatter | solution.py:1408
  96.3 26.6 %copy-start.6 = (s32[7,1]{0,1:T(1,128)}, s32[7,1]{0,1:T(1,128)S(1)}, u32[]{:S(2)}) copy-start(s32[7,1]{0,1:T(1,128)S(1)} %reduce-window.9) | copy-start | bytes 88
  123.0 1.3 copy-start.2
  124.3 1.0 copy-start.3
  125.3 1.0 copy-start.8
  422.6 93.8 %copy-start.9 = (bf16[1024,512]{1,0:T(8,128)(2,1)S(1)}, bf16[1024,512]{1,0:T(8,128)(2,1)}, u32[]{:S(2)}) copy-start(bf16[1024,512]{1,0:T(8,128)(2,1)} %copy-done.8) | copy-start | bytes 3145732
  632.0 3.3 copy-start.11
  635.3 1.4 copy-start.19
  635.3 2.2 copy-start.18
  636.6 1.6 copy-start.17
  636.6 2.4 copy-start.16
  636.6 3.2 copy-start.15
  637.4 3.2 copy-start.13
  639.8 1.9 copy-start.12
  641.7 1.9 copy-start.14
Sparse Core Ops, SparseCore 0:
  96.2 79.7 all-gather.1
  422.7 77.1 reduce-scatter.1

commit v4 on v3

--- a/solution.py
+++ b/solution.py
@@ -429,58 +429,6 @@
         return taken
 
     return take
-
-
-def project_kernel(size, rounds, x_ref, gain_ref, wq, wf, wi, ws, a_ref, q_ref, f_ref, i_ref, s_ref, send, recv):
-    greet(*line_peers(size))
-    line = Gather(size, send, recv, a_ref)
-    gain = gain_ref[...]
-    m, d = x_ref.shape[1:]
-
-    @pl.loop(0, rounds)
-    def _(j):
-        @pl.loop(0, m // 16)
-        def _(g):
-            r = pl.ds(pl.multiple_of(g * 16, 16), 16)
-            x = x_ref[j, r, :].astype(f32)
-            scale = lax.rsqrt(jnp.mean(x * x, axis=-1, keepdims=True) + epsilon)
-            a_ref[line.me, j, r, :] = (x * scale * gain).astype(bf16)
-
-        line.start(j)
-
-    def products(j):
-        rows = a_ref[:, j].reshape(size * m, d)
-        for weight, out in ((wq, q_ref), (wf, f_ref), (wi, i_ref), (ws, s_ref)):
-            out[:, j] = mul(rows, weight[...], NN).reshape(size, m, weight.shape[1])
-
-    @pl.loop(0, rounds)
-    def _(j):
-        for t in range(1, size):
-            line.step(j, t)
-        products(j)
-
-    @pl.loop(0, rounds)
-    def _(j):
-        line.drain(j)
-
-
-def project(size, rounds, tokens, first_gain, wq, wf, wi, ws):
-    rows, d = tokens.shape
-    m = rows // rounds
-    c = wq.shape[1]
-    shape = (size, rounds, m)
-    out = pl.pallas_call(
-        partial(project_kernel, size, rounds),
-        out_shape=[jax.ShapeDtypeStruct(shape + (d,), bf16)] + [jax.ShapeDtypeStruct(shape + (c,), f32)] * 4,
-        in_specs=[pl.BlockSpec(memory_space=VM)] * 6,
-        out_specs=[pl.BlockSpec(memory_space=VM)] * 5,
-        scratch_shapes=[DMA((2, rounds, size)), DMA((2, rounds, size))],
-        compiler_params=pltpu.CompilerParams(collective_id=0, has_side_effects=True, vmem_limit_bytes=48 * MIB),
-        cost_estimate=pl.CostEstimate(flops=8 * size * rows * d * c, bytes_accessed=32 * MIB, transcendentals=0),
-        name="project",
-    )(tokens.reshape(rounds, m, d), first_gain.reshape(1, d), wq, wf, wi, ws)
-    total = size * rows
-    return [out[0].reshape(total, d)] + [part.reshape(total, c) for part in out[1:]]
 
 
 def document(rows, ends_ref):
@@ -579,37 +527,81 @@
     ]
 
 
-def scan_kernel(
-    size,
-    ends_ref,
-    q_ref,
-    f_ref,
-    i_ref,
-    s_ref,
-    bound_ref,
-    gain_ref,
-    o_ref,
-    u_ref,
-    starts_ref,
-    qd_ref,
-    kd_ref,
-    qe_ref,
-    adds,
-    decays,
-    state,
-    out_state,
-    out_decay,
-    land_state,
-    land_decay,
-    sems,
-):
-    greet(*group_peers(size, "seq"))
+def front_kernel(size, groups, rounds, *refs):
+    take = taker(refs)
+    ends_ref, x_ref, norm_gain_ref, bound_ref, gain_ref, cot_in, *loaded = take(10)
+    a_out, q_out, f_out, i_out, s_out, cot_out, o_ref, u_ref, starts_ref = take(9)
+    *weights, a_ref, q_ref, f_ref, i_ref, s_ref, cot_ref = take(10)
+    qd_ref, kd_ref, qe_ref, adds, decays = take(5)
+    state, out_state, out_decay, land_state, land_decay, sems = take(6)
+    load_sems, store_sems, a_send, a_recv, c_send, c_recv = take(6)
+    me = lax.axis_index("tp")
+    m, d = x_ref.shape[1:]
+    known = cot_ref.shape[1]
+    local = pltpu.make_async_copy
+    cot_load = local(cot_in.at[:known], cot_ref.at[me], load_sems.at[4])
+    cot_load.start()
+    loads = [local(source, target, load_sems.at[k]) for k, (source, target) in enumerate(zip(loaded, weights))]
+    for load in loads:
+        load.start()
+    line, line_count = line_peers(size)
+    seq, seq_count = group_peers(groups, "seq")
+    greet(line + seq, line_count + seq_count)
+
+    gather = Gather(size, a_send, a_recv, a_ref)
+    gather_cot = Gather(size, c_send, c_recv, cot_ref)
+    norm_gain = norm_gain_ref[...]
+
+    @pl.loop(0, rounds)
+    def _(j):
+        @pl.loop(0, m // 16)
+        def _(g):
+            r = pl.ds(pl.multiple_of(g * 16, 16), 16)
+            x = x_ref[j, r, :].astype(f32)
+            scale = lax.rsqrt(jnp.mean(x * x, axis=-1, keepdims=True) + epsilon)
+            a_ref[me, j, r, :] = (x * scale * norm_gain).astype(bf16)
+
+        gather.start(j)
+
+    for load in loads:
+        load.wait()
+    cot_load.wait()
+    pres = (q_ref, f_ref, i_ref, s_ref)
+
+    @pl.loop(0, rounds)
+    def _(j):
+        for t in range(1, size):
+            gather.step(j, t)
+
+        @pl.when(j >= rounds - known)
+        def _():
+            gather_cot.start(j - (rounds - known))
+
+        rows = a_ref[:, j].reshape(size * m, d)
+        for weight, out in zip(weights, pres):
+            product = mul(rows, weight[...], NN)
+            for z in range(size):
+                at = pl.multiple_of(z * rounds * m + j * m, 16)
+                out[pl.ds(at, m), :] = product[z * m : (z + 1) * m]
+
+    stores = [
+        local(source, target, store_sems.at[k])
+        for k, (source, target) in enumerate(zip((a_ref, *pres), (a_out, q_out, f_out, i_out, s_out)))
+    ]
+    for store in stores:
+        store.start()
+
     rows, c = q_ref.shape
     blocks, heads = rows // WIDTH, c // WIDTH
     base = lax.axis_index("seq") * rows
-    states = States(size, out_state, out_decay, land_state, land_decay, sems)
+    states = States(groups, out_state, out_decay, land_state, land_decay, sems)
     state[...] = jnp.zeros_like(state)
     out_decay[...] = jnp.ones_like(out_decay)
+
+    def cot_steps(t):
+        @pl.loop(0, known)
+        def _(j):
+            gather_cot.step(j, t)
 
     @pl.loop(0, blocks)
     def _(b):
@@ -634,6 +626,7 @@
 
     out_state[...] = state[...].astype(bf16)
     states.start(True)
+    cot_steps(1)
 
     @pl.loop(0, blocks)
     def _(b):
@@ -645,6 +638,8 @@
             o_ref[r, cols] = mul(scores, i_ref[r, cols].astype(bf16), NN)
 
     states.compose(True, state)
+    for t in range(2, size - 1):
+        cot_steps(t)
 
     @pl.loop(0, blocks)
     def _(b):
@@ -663,44 +658,87 @@
             z = s * jax.nn.sigmoid(s) * valid
             u_ref[r, cols] = (o * scale * gain_ref[:, cols] * z).astype(bf16)
 
+    cot_steps(size - 1)
+    cot_store = local(cot_ref, cot_out, load_sems.at[4])
+    cot_store.start()
     states.drain(True)
 
-
-def scan_forward(size, ends, q, f, i, s, bound, gain):
-    rows, c = q.shape
+    @pl.loop(0, rounds)
+    def _(j):
+        gather.drain(j)
+
+    @pl.loop(0, known)
+    def _(j):
+        gather_cot.drain(j)
+
+    for store in stores:
+        store.wait()
+    cot_store.wait()
+
+
+def front(size, groups, rounds, tokens, cot, norm_gain, weights, ends, bound, gain):
+    own, d = tokens.shape
+    m, c = own // rounds, weights[0].shape[1]
+    rows = size * own
     blocks, heads = rows // WIDTH, c // WIDTH
-    low = VM((rows, c), bf16)
-    return pl.pallas_call(
-        partial(scan_kernel, size),
+    known = max(1, rounds // 2)
+    shape, some = (size, rounds, m, d), (size, known, m, d)
+    wide, low = jax.ShapeDtypeStruct((rows, c), f32), VM((rows, c), bf16)
+    spec, far = pl.BlockSpec(memory_space=VM), pl.BlockSpec(memory_space=pl.ANY)
+    sems = DMA((2, rounds, size))
+    outs = pl.pallas_call(
+        partial(front_kernel, size, groups, rounds),
         out_shape=[
-            jax.ShapeDtypeStruct((rows, c), f32),
+            jax.ShapeDtypeStruct(shape, bf16),
+            wide,
+            wide,
+            wide,
+            wide,
+            jax.ShapeDtypeStruct(some, bf16),
+            wide,
             jax.ShapeDtypeStruct((rows, c), bf16),
             jax.ShapeDtypeStruct((blocks, heads, WIDTH, WIDTH), bf16),
         ],
-        in_specs=[pl.BlockSpec(memory_space=pltpu.SMEM)] + [pl.BlockSpec(memory_space=VM)] * 6,
-        out_specs=[pl.BlockSpec(memory_space=VM)] * 3,
-        scratch_shapes=[
-            low,
-            low,
-            low,
-            VM((blocks, heads, WIDTH, WIDTH), f32),
-            VM((blocks, 8, WIDTH), f32),
-        ]
-        + states_scratch(size, heads),
-        compiler_params=pltpu.CompilerParams(collective_id=1, has_side_effects=True, vmem_limit_bytes=48 * MIB),
-        cost_estimate=pl.CostEstimate(flops=20 * rows * c * WIDTH, bytes_accessed=14 * MIB, transcendentals=8 * rows * c),
-        name="scan_forward",
-    )(ends, q, f, i, s, bound, gain)
+        in_specs=[pl.BlockSpec(memory_space=pltpu.SMEM)] + [spec] * 4 + [far] * 5,
+        out_specs=[far] * 6 + [spec] * 3,
+        scratch_shapes=[VM((d, c), bf16)] * 4
+        + [VM(shape, bf16)]
+        + [VM((rows, c), f32)] * 4
+        + [VM(some, bf16)]
+        + [low] * 3
+        + [VM((blocks, heads, WIDTH, WIDTH), f32), VM((blocks, 8, WIDTH), f32)]
+        + states_scratch(groups, heads)
+        + [DMA((5,)), DMA((5,)), sems, sems, sems, sems],
+        compiler_params=pltpu.CompilerParams(collective_id=0, has_side_effects=True, vmem_limit_bytes=60 * MIB),
+        cost_estimate=pl.CostEstimate(flops=8 * rows * d * c, bytes_accessed=36 * MIB, transcendentals=8 * rows * c),
+        name="front",
+    )(
+        ends,
+        tokens.reshape(rounds, m, d),
+        norm_gain.reshape(1, d),
+        bound,
+        gain,
+        cot.reshape(rounds, m, d),
+        *weights,
+    )
+    return [outs[0].reshape(rows, d)] + list(outs[1:])
 
 
 def scan_back_kernel(size, count, *refs):
     take = taker(refs)
-    ends_ref, q_ref, f_ref, i_ref, s_ref, bound_ref, gain_ref, o_ref, starts_ref, ub_ref = take(10)
+    ends_ref, bound_ref, gain_ref, *loaded = take(10)
     grads = take(count)
     dq_ref, df_ref, di_ref, ds_ref, small_ref = take(5)
     grad_outs = take(count)
     qd_ref, kd_ref, qe_ref, kt_ref, do_ref, run_ref, adds, decays = take(8)
     state, out_state, out_decay, land_state, land_decay, sems = take(6)
+    *inputs, load_sems = take(8)
+    q_ref, f_ref, i_ref, s_ref, o_ref, ub_ref, starts_ref = inputs
+    loads = [
+        pltpu.make_async_copy(source, target, load_sems.at[k]) for k, (source, target) in enumerate(zip(loaded, inputs))
+    ]
+    for load in loads:
+        load.start()
     sums = group_sums(size, grads, grad_outs, take)
     greet(*group_peers(size, "seq"))
     rows, c = q_ref.shape
@@ -712,18 +750,16 @@
     state[...] = jnp.zeros_like(state)
     out_decay[...] = jnp.ones_like(out_decay)
     small_ref[...] = jnp.zeros_like(small_ref)
+    for load in loads:
+        load.wait()
 
     @pl.loop(0, blocks)
     def _(back):
-        for order, each in enumerate(sums):
-
-            @pl.when(back == min(order + 1, blocks - 1))
+        for each in sums[:1]:
+
+            @pl.when(back == 1)
             def _():
                 each.middle()
-
-            @pl.when(back == blocks - 1)
-            def _():
-                each.relay()
 
         b = blocks - 1 - back
         r = pl.ds(pl.multiple_of(b * WIDTH, WIDTH), WIDTH)
@@ -761,11 +797,19 @@
 
     out_state[...] = state[...].astype(bf16)
     states.start(False)
-
+    for each in sums[:1]:
+        each.relay()
+    for each in sums[1:]:
+        each.middle()
     states.compose(False, state)
 
     @pl.loop(0, blocks)
     def _(back):
+        for each in sums[1:]:
+
+            @pl.when(back == blocks // 2)
+            def _():
+                each.relay()
         b = blocks - 1 - back
         r = pl.ds(pl.multiple_of(b * WIDTH, WIDTH), WIDTH)
         same, carry, tail, keep = block_masks(base + b * WIDTH, ends_ref)
@@ -820,7 +864,7 @@
         each.drain()
 
 
-def scan_backward(size, ends, q, f, i, s, bound, gain, o, starts, ub, grads):
+def scan_backward(size, ends, bound, gain, q, f, i, s, o, ub, starts, grads):
     rows, c = q.shape
     blocks, heads = rows // WIDTH, c // WIDTH
     low, wide = VM((rows, c), bf16), VM((rows, c), f32)
@@ -831,29 +875,32 @@
         + [jax.ShapeDtypeStruct((2 * heads, WIDTH), f32)]
         + sum_shapes([grad.shape for grad in grads], [False] * len(grads)),
         in_specs=[pl.BlockSpec(memory_space=pltpu.SMEM)]
-        + [spec] * 9
-        + [pl.BlockSpec(memory_space=pl.ANY)] * len(grads),
+        + [spec] * 2
+        + [pl.BlockSpec(memory_space=pl.ANY)] * (7 + len(grads)),
         out_specs=[spec] * (5 + len(grads)),
         scratch_shapes=[low] * 5
         + [wide, VM((blocks, heads, WIDTH, WIDTH), f32), VM((blocks, 8, WIDTH), f32)]
         + states_scratch(size, heads)
+        + [wide] * 6
+        + [VM(starts.shape, bf16), DMA((7,))]
         + group_sums_scratch([grad.shape for grad in grads]),
         compiler_params=pltpu.CompilerParams(collective_id=2, has_side_effects=True, vmem_limit_bytes=60 * MIB),
         cost_estimate=pl.CostEstimate(flops=40 * rows * c * WIDTH, bytes_accessed=20 * MIB, transcendentals=16 * rows * c),
         name="scan_backward",
-    )(ends, q, f, i, s, bound, gain, o, starts, ub, *[in_pairs(grad) for grad in grads])
+    )(ends, bound, gain, q, f, i, s, o, ub, starts, *[in_pairs(grad) for grad in grads])
 
 
 def middle_kernel(size, rounds, *refs):
     take = taker(refs)
-    u_ref, x_ref, gain_ref, out_w, *loaded = take(8)
-    res_out, back_out, e_out, ub_out, second_ref, down_out, *grad_outs = take(9)
-    gate_w, up_w, down_w, cot_ref = weights = take(4)
+    u_ref, x_ref, gain_ref, out_w, *loaded, cot_some, cot_own = take(9)
+    res_out, back_out, e_out, ub_out, second_ref, down_out, out_grad, *grad_outs = take(10)
+    gate_w, up_w, down_w = weights = take(3)
+    cot_ref = take(1)[0]
     b_ref, e_ref, res_ref, back_ref, ub_ref, part, land, total = take(8)
     wide = take(3)
     down_ref, *tiles = take(4)
     load_sems, res_sems, back_sems, e_sems, ub_sem, down_sem, tile_sems = take(7)
-    lines = [take(2) for _ in range(4)]
+    lines = [take(2) for _ in range(5)]
     hidden, gate_back, up_back = wide
     me = lax.axis_index("tp")
     m, d = x_ref.shape[1:]
@@ -863,10 +910,15 @@
     gather = Gather(size, *lines[1], b_ref)
     scatter_back = Scatter(size, *lines[2], part, land, total)
     gather_back = Gather(size, *lines[3], e_ref)
+    gather_cot = Gather(size, *lines[4], cot_ref)
+    known = cot_some.shape[1]
     gain = gain_ref[...]
     tile = min(512, d)
     local = pltpu.make_async_copy
     loads = [local(src, dst, load_sems.at[k]) for k, (src, dst) in enumerate(zip(loaded, weights))]
+    loads.append(local(cot_some, cot_ref.at[:, :known], load_sems.at[3]))
+    cot_load = local(cot_own.at[known:], cot_ref.at[me, known:], load_sems.at[4])
+    cot_load.start()
     for load in loads:
         load.start()
     second_ref[...] = jnp.zeros_like(second_ref)
@@ -886,7 +938,7 @@
         return local(res_ref.at[j], res_out.at[j], res_sems.at[j])
 
     def back_copy(j):
-        return local(back_ref.at[j], back_out.at[j], back_sems.at[j])
+        return local(back_ref, back_out.at[j], back_sems.at[0])
 
     def e_copy(j):
         return local(e_ref.at[:, j], e_out.at[:, j], e_sems.at[j])
@@ -958,7 +1010,11 @@
 
         down_copy(j).start()
 
-    def norm_back(j):
+    def norm_back(j, again):
+        @pl.when(again)
+        def _():
+            back_copy(j - 1).wait()
+
         @pl.loop(0, m // 16)
         def _(g):
             r = pl.ds(pl.multiple_of(g * 16, 16), 16)
@@ -970,7 +1026,7 @@
             back = cot_ref[me, j, r, :].astype(f32) + scale * (
                 inner - normed * jnp.mean(inner * normed, axis=-1, keepdims=True)
             )
-            back_ref[j, r, :] = back
+            back_ref[r, :] = back
             e_ref[me, j, r, :] = back.astype(bf16)
 
         gather_back.start(j)
@@ -1010,6 +1066,7 @@
                 copy.start()
 
     final = rounds - 1
+    cot_load.wait()
 
     @pl.loop(0, rounds + 2)
     def _(i):
@@ -1019,14 +1076,24 @@
                 body(i - lag)
 
         stage(0, project_out)
+
+        @pl.when(i < rounds - known)
+        def _():
+            gather_cot.start(known + i)
+
         for t in range(1, size):
+
+            @pl.when((i > 0) & (i <= rounds - known))
+            def _():
+                gather_cot.step(known + i - 1, t)
+
             stage(1, lambda j: scatter.step(j, t) if t < size - 1 else scatter.finish(j))
             if t == size - 1:
                 stage(1, norm)
             stage(2, lambda j: gather.step(j, t))
             stage(3, lambda j: scatter_back.step(j, t) if t < size - 1 else scatter_back.finish(j))
             if t == size - 1:
-                stage(3, norm_back)
+                stage(3, lambda j: norm_back(j, j > 0))
             stage(4, lambda j: gather_back.step(j, t))
         stage(2, feed)
         stage(2, feed_back)
@@ -1039,7 +1106,7 @@
             scatter_back.step(final, t)
         else:
             scatter_back.finish(final)
-            norm_back(final)
+            norm_back(final, True)
         gather_back.step(final - 1, t)
         if t < size - 1:
             weight_tiles(shares[t - 1], shares[t])
@@ -1050,23 +1117,52 @@
         if t < size - 1:
             weight_tiles(shares[t + 2], shares[t + 3])
     unproject(final, True)
-
     for copy in tile_copies(count - 1):
         copy.wait()
+    width = u_ref.shape[3]
+
+    def out_tile(n, slot):
+        rows = pl.ds(pl.multiple_of(n * depth, depth), depth)
+        source = tiles[slot].at[:, pl.ds(0, width)]
+        return local(source, out_grad.at[rows, :], tile_sems.at[slot])
+
+    slots = len(tiles) - 1
+
+    @pl.loop(0, count // slots)
+    def _(n):
+        for slot in range(slots):
+            at = n * slots + slot
+
+            @pl.when(n > 0)
+            def _():
+                out_tile(at - slots, slot).wait()
+
+            cols = pl.ds(pl.multiple_of(at * depth, depth), depth)
+            rows = e_ref[:, :, :, cols].reshape(rounds * group, depth)
+            tiles[slot][:, :width] = mul(rows, u_ref[...].reshape(rounds * group, width), TN).astype(bf16)
+            out_tile(at, slot).start()
+
+    for slot in range(slots):
+        out_tile(count - slots + slot, slot).wait()
     ub_copy(final).wait()
+    back_copy(final).wait()
     down_copy(final).wait()
 
     @pl.loop(0, rounds)
     def _(j):
         res_copy(j).wait()
-        back_copy(j).wait()
         e_copy(j).wait()
+
+        @pl.when(j >= known)
+        def _():
+            gather_cot.drain(j)
+
         gather.drain(j)
         scatter_back.drain(j)
         gather_back.drain(j)
 
 
-def middle(size, rounds, u, x, cot, gain, out_w, gate_w, up_w, down_w):
+def middle(size, rounds, u, x, cot_some, cot, gain, out_w, gate_w, up_w, down_w):
     rows, d = x.shape
     m = rows // rounds
     c, ff = out_w.shape[0], gate_w.shape[1]
@@ -1083,10 +1179,11 @@
             jax.ShapeDtypeStruct(shape + (c,), f32),
             jax.ShapeDtypeStruct((1, d), f32),
             jax.ShapeDtypeStruct(shape + (d,), bf16),
+            jax.ShapeDtypeStruct((d, c), bf16),
         ]
         + [jax.ShapeDtypeStruct((d, ff), bf16)] * 3,
-        in_specs=[spec] * 4 + [far] * 4,
-        out_specs=[far] * 4 + [spec] + [far] * 4,
+        in_specs=[spec] * 4 + [far] * 5,
+        out_specs=[far] * 4 + [spec] + [far] * 5,
         scratch_shapes=[
             VM(gate_w.shape, bf16),
             VM(up_w.shape, bf16),
@@ -1095,7 +1192,7 @@
             VM(shape + (d,), bf16),
             VM(shape + (d,), bf16),
             VM((rounds, m, d), f32),
-            VM((rounds, m, d), f32),
+            VM((m, d), f32),
             VM((size, m, c), f32),
             VM((rounds, size, m, d), bf16),
             VM((2, rounds, size - 1, m, d), bf16),
@@ -1104,8 +1201,8 @@
         + [VM(shape + (ff,), bf16)] * 3
         + [VM((size, m, d), bf16)]
         + [VM((depth, ff), bf16)] * 3
-        + [DMA((4,)), DMA((rounds,)), DMA((rounds,)), DMA((rounds,)), DMA((1,)), DMA((1,)), DMA((3,))]
-        + [sems] * 8,
+        + [DMA((5,)), DMA((rounds,)), DMA((1,)), DMA((rounds,)), DMA((1,)), DMA((1,)), DMA((3,))]
+        + [sems] * 10,
         compiler_params=pltpu.CompilerParams(collective_id=3, has_side_effects=True, vmem_limit_bytes=63 * MIB),
         cost_estimate=pl.CostEstimate(
             flops=2 * size * rows * d * (2 * c + 9 * ff), bytes_accessed=56 * MIB, transcendentals=size * rows * ff
@@ -1119,14 +1216,14 @@
         gate_w,
         up_w,
         down_w,
-        cot.reshape(shape + (d,)),
+        cot_some,
+        cot.reshape(rounds, m, d),
     )
     res, back, e, ub, second, down, *grads = outs
     total = size * rows
     return (
         res.reshape(rows, d),
         back.reshape(rows, d),
-        e.reshape(total, d),
         ub.reshape(total, c),
         second,
         down.reshape(total, d),
@@ -1397,12 +1494,11 @@
     weights = (query_weight, forget_weight, input_weight, swish_weight)
     ends = jnp.cumsum(lengths).astype(jnp.int32)
     bound, head_gain = bound_logit.reshape(1, -1), group_gain.reshape(1, -1)
-    a, q, f, i, s = project(size, ROUNDS, tokens, first_gain, *weights)
-    cot_own, q = lax.optimization_barrier((cotangent, q))
-    cot = lax.all_gather(cot_own, "tp", axis=0, tiled=True)
-    o, u, starts = scan_forward(groups, ends, q, f, i, s, bound, head_gain)
-    residual, back, e, ub, second, down, *glu = middle(
-        size, ROUNDS, u, tokens, cot, second_gain, out_weight, gate_weight, up_weight, down_weight
+    a, q, f, i, s, cot_some, o, u, starts = front(
+        size, groups, ROUNDS, tokens, cotangent, first_gain, weights, ends, bound, head_gain
+    )
+    residual, back, ub, second, down, *wide = middle(
+        size, ROUNDS, u, tokens, cot_some, cotangent, second_gain, out_weight, gate_weight, up_weight, down_weight
     )
     down, ub = lax.optimization_barrier((down, ub))
     down = lax.psum_scatter(down, "tp", scatter_dimension=0, tiled=True)
@@ -1415,13 +1511,13 @@
     def grad_of(left, right):
         return chunks(lax.dot_general(left, right, TN, preferred_element_type=f32).astype(bf16))
 
-    gates, ups, downs = (chunks(grad) for grad in glu)
+    outs, gates, ups, downs = (chunks(grad) for grad in wide)
     dq, df, di, ds, small, gate_grad, up_grad = scan_backward(
-        groups, ends, q, f, i, s, bound, head_gain, o, starts, ub, [gates, ups]
+        groups, ends, bound, head_gain, q, f, i, s, o, ub, starts, [gates, ups]
     )
     back_rows = (dq, df, di, ds)
     here_too = groups == 8
-    others = [downs, grad_of(e, u)] + ([] if here_too else [grad_of(a, part) for part in back_rows])
+    others = [downs, outs] + ([] if here_too else [grad_of(a, part) for part in back_rows])
     tokens_grad, second_sum, first_sum, small_sum, *sums = last(
         size,
         groups,

time: 659 us -> 591 us (0.90); the launches traced: 652 us -> 591 us
  waiting for transfers between devices: 49.8 us -> 0.02 us
  local copies, waits for them, and re-layouts: 21.2 us -> 13.4 us
    all_gather x1 -> x0, waiting for transfers between devices: 49.8 us -> none  [per_device(): cot = lax.all_gather(cot_own, 'tp', axis=0, tiled=True)]
    pallas_call x1, Pallas kernels: 93.8 us -> 69.5 us  [scan_backward(): pl.pallas_call(partial(scan_back_kernel, size, len(grads)), out_shape=[ja...]
    pallas_call x1, Pallas kernels: 247 us -> 269 us  [middle(): pl.pallas_call(partial(middle_kernel, size, rounds), out_shape=[jax.Shape...]
    unnamed x51 -> x27, local copies, waits for them, and re-layouts: 17.3 us -> 9.44 us
    pallas_call x2 -> x1, Pallas kernels: 111 us -> 116 us  [front(): pl.pallas_call(partial(front_kernel, size, groups, rounds), out_shape=[ja...]
  transfers between devices with their start and end apart: 2 -> 1, of which waited for: 1 -> 0; matrix products, arithmetic and copies ran while one was open for 2% -> 1% of each run, Pallas kernels for 35% -> 29%
where the time goes in v4:
time: 591 us
  Pallas kernels  559 us (95%)
  between operations  14.1 us (2%)
  local copies, waits for them, and re-layouts  13.4 us (2%)
    pallas_call x1, Pallas kernels, middle(): pl.pallas_call(partial(middle_kernel, size, rounds), out_shape=[jax.Shape...  269 us
    pallas_call x1, Pallas kernels, front(): pl.pallas_call(partial(front_kernel, size, groups, rounds), out_shape=[ja...  116 us
    pallas_call x1, Pallas kernels, last(): pl.pallas_call(partial(last_kernel, size, groups, rounds, len(grads), mix...  103 us
    pallas_call x1, Pallas kernels, scan_backward(): pl.pallas_call(partial(scan_back_kernel, size, len(grads)), out_shape=[ja...  69.5 us
  transfers between devices with their start and end apart: 1, of which 0 were waited for; matrix products, arithmetic and copies ran while one was open for 1% of the time, Pallas kernels for 29%

profile of v4, /device:TPU:0, one launch (start us, length us, event | category | flops | bytes accessed | tf_op | source)
XLA Modules:
  0.0 590.7 jit_solution(11417815292316321815)
XLA Ops:
  7.2 0.0 reduce-scatter.2.cloned.1.call-start
  7.2 1.3 reduce-window.9
  8.6 116.4 %front.1 = (bf16[4,4,64,2048]{3,2,1,0:T(8,128)(2,1)}, f32[1024,512]{1,0:T(8,128)}, f32[1024,512]{1,0:T(8,128)}, f32[1024,512]{1,0:T(8,128)}, f32[1024,512]{1,0:T...) custom-call(s32[7]{0:T(128)} %bitcast.35, ...), custom_call_target="tpu_custom_call" | custom-call | flops 8589934592 | bytes 37748736 | tf_op jit(solution)/shard_map/front/pallas_call | solution.py:689
  124.9 269.4 %middle.1 = (f32[4,64,2048]{2,1,0:T(8,128)}, f32[4,64,2048]{2,1,0:T(8,128)}, bf16[4,4,64,2048]{3,2,1,0:T(8,128)(2,1)}, f32[4,4,64,512]{3,2,1,0:T(8,128)}, f32[1,...) custom-call(bf16[4,4,64,512]{3,2,1,0:T(8,128)(2,1)} %bitcast.52, ...), custom_call_target="tpu_custom_call" | custom-call | flops 57445187584 | bytes 58720256 | tf_op jit(solution)/shard_map/middle/pallas_call | solution.py:1173
  394.4 0.0 reduce-scatter.2.cloned.1.call-update
  394.4 69.5 %scan_backward.1 = (bf16[1024,512]{1,0:T(8,128)(2,1)}, bf16[1024,512]{1,0:T(8,128)(2,1)}, bf16[1024,512]{1,0:T(8,128)(2,1)}, bf16[1024,512]{1,0:T(8,128)(2,1)}, ...) custom-call(s32[7]{0:T(128)} %bitcast.36, f32[1,512]{1,0:T(1,128)} %bitcast.32, f32[1,512]{1,0:T(1,128)} %bitcast.34, ...), custom_call_target="tpu_custom_call" | custom-call | flops 2684354560 | bytes 20971520 | tf_op jit(solution)/shard_map/scan_backward/pallas_call | solution.py:872
  463.9 103.3 %last.1 = (f32[4,64,2048]{2,1,0:T(8,128)}, f32[16,128]{1,0:T(8,128)}, f32[16,128]{1,0:T(8,128)}, f32[24,128]{1,0:T(8,128)}, f32[1408,256]{1,0:T(8,128)}, /*index...) custom-call(bf16[4,4,64,512]{3,2,1,0:T(8,128)(2,1)} %bitcast.42, ...), custom_call_target="tpu_custom_call" | custom-call | flops 17179869184 | bytes 58720256 | tf_op jit(solution)/shard_map/last/pallas_call | solution.py:1432
  567.2 1.3 dynamic_slice.12
  568.5 1.3 dynamic_slice.15
  569.8 0.8 fusion.1
  570.5 0.7 constant_dynamic-slice_fusion
  571.2 0.0 reduce-scatter.2.cloned.1.call-done
  571.2 0.0 copy-start
  571.2 3.3 fusion
  574.4 0.0 copy-done
  574.4 0.0 copy-start.8
  574.5 0.0 copy-start.7
  574.5 1.3 copy.38
  575.8 0.1 copy-done.8
  575.8 0.0 copy-start.6
  575.8 0.0 copy-start.5
  575.8 0.0 copy-start.4
  575.8 0.8 copy.39
  576.6 0.0 copy-done.7
  576.6 0.0 copy-start.2
  576.6 0.8 copy.40
  577.4 0.0 copy-done.6
  577.4 0.8 copy.41
  578.2 0.0 copy-done.5
  578.2 0.8 copy.42
  579.0 0.0 copy-done.4
  579.0 0.0 copy-start.1
  579.0 0.8 copy.43
  579.8 0.0 copy-done.2
  579.8 1.1 copy.44
  580.9 0.0 copy-done.1
  580.9 0.0 copy-start.3
  580.9 1.1 copy.45
  582.0 0.8 copy-done.3
  582.8 1.1 copy.46
Async XLA Ops:
  7.2 564.0 %reduce-scatter.2.cloned.1.call-start = ((), (), s32[]{:S(2)}) async-start(), calls=%async_computation.1 | async-start | bytes 5242880 | tf_op jit(solution)/shard_map/reduce_scatter | solution.py:1504
  571.2 3.3 copy-start
  574.4 1.4 copy-start.8
  574.5 2.2 copy-start.7
  575.8 1.6 copy-start.6
  575.8 2.4 copy-start.5
  575.8 3.2 copy-start.4
  576.6 3.2 copy-start.2
  579.0 1.9 copy-start.1
  580.9 1.9 copy-start.3
Sparse Core Ops, SparseCore 0:
  394.5 76.0 reduce-scatter.1

commit v5 on v4

--- a/solution.py
+++ b/solution.py
@@ -9,6 +9,16 @@
 
 WIDTH = 128
 ROUNDS = 4
+KNOWN = 1
+PIECES = 3
+STEPS = (
+    "C10", "C11", "C20", "A0", "C12", "C13", "A1", "C21", "C22", "C23", "S01", "C30", "S11", "S02", "S03", "A2",
+    "A3", "C31", "C32", "C33", "G01", "G02", "S21", "S22", "S12", "S23", "G03", "F00", "F01", "F02", "O0", "S13",
+    "B0", "S31", "G11", "T01", "T02", "G12", "G13", "F10", "F11", "F12", "O1", "G21", "T03", "B1", "S32", "G22",
+    "G23", "F20", "E01", "F21", "F22", "E02", "E03", "S33", "T11", "T12", "T13", "G31", "O2", "E11", "B2", "U0",
+    "T21", "G32", "G33", "F30", "F31", "T22", "F32", "O3", "E12", "T23", "B3", "W0", "E21", "T31", "T32", "E22",
+    "W1", "W2", "T33", "W3", "E23", "W5", "E31", "E13", "U1", "W6", "W4", "U2", "W7", "E32", "E33", "U3",
+)
 MIB = 1 << 20
 epsilon = 1e-05
 
@@ -681,7 +691,7 @@
     m, c = own // rounds, weights[0].shape[1]
     rows = size * own
     blocks, heads = rows // WIDTH, c // WIDTH
-    known = max(1, rounds // 2)
+    known = KNOWN
     shape, some = (size, rounds, m, d), (size, known, m, d)
     wide, low = jax.ShapeDtypeStruct((rows, c), f32), VM((rows, c), bf16)
     spec, far = pl.BlockSpec(memory_space=VM), pl.BlockSpec(memory_space=pl.ANY)
@@ -961,16 +971,12 @@
         gather.start(j)
         res_copy(j).start()
 
-    def feed(j):
-        @pl.when(j == 0)
-        def _():
-            for load in loads:
-                load.wait()
-
+    def feed(j, piece):
         rows = b_ref[:, j].reshape(group, d)
         cot = cot_ref[:, j].reshape(group, d)
         step = 256
-        for low in range(0, ff, step):
+        starts = list(range(0, ff, step))
+        for low in starts[len(starts) * piece // PIECES : len(starts) * (piece + 1) // PIECES]:
             cols = slice(low, min(low + step, ff))
             width = cols.stop - cols.start
             gate = mul(rows, gate_w[:, cols], NN)
@@ -997,10 +1003,6 @@
         scatter_back.start(j)
 
     def feed_out(j):
-        @pl.when(j > 0)
-        def _():
-            down_copy(j - 1).wait()
-
         rows = hidden[:, j].reshape(group, ff)
 
         @pl.loop(0, d // tile)
@@ -1010,11 +1012,7 @@
 
         down_copy(j).start()
 
-    def norm_back(j, again):
-        @pl.when(again)
-        def _():
-            back_copy(j - 1).wait()
-
+    def norm_back(j):
         @pl.loop(0, m // 16)
         def _(g):
             r = pl.ds(pl.multiple_of(g * 16, 16), 16)
@@ -1032,13 +1030,8 @@
         gather_back.start(j)
         back_copy(j).start()
 
-    def unproject(j, wait):
+    def unproject(j):
         e_copy(j).start()
-
-        @pl.when(wait)
-        def _():
-            ub_copy(j - 1).wait()
-
         rows = e_ref[:, j].reshape(group, d)
         ub_ref[...] = mul(rows, out_w[...], NT).reshape(size, m, out_w.shape[0])
         ub_copy(j).start()
@@ -1047,78 +1040,69 @@
     count = d // depth
 
     def tile_copies(n):
-        rows = pl.ds(pl.multiple_of(n * depth, depth), depth)
+        rows = pl.ds(n * depth, depth)
         return [local(src, dst.at[rows, :], tile_sems.at[k]) for k, (src, dst) in enumerate(zip(tiles, grad_outs))]
 
-    def weight_tiles(low, high):
-        @pl.loop(low, high)
-        def _(n):
-            @pl.when(n > 0)
-            def _():
-                for copy in tile_copies(n - 1):
-                    copy.wait()
-
-            cols = pl.ds(pl.multiple_of(n * depth, depth), depth)
-            for left, right, out in zip((b_ref, b_ref, cot_ref), (gate_back, up_back, hidden), tiles):
-                rows = left[:, :, :, cols].reshape(rounds * group, depth)
-                out[...] = mul(rows, right[...].reshape(rounds * group, ff), TN).astype(bf16)
-            for copy in tile_copies(n):
-                copy.start()
-
-    final = rounds - 1
+    def weight_tile(n):
+        cols = pl.ds(n * depth, depth)
+        for left, right, out in zip((b_ref, b_ref, cot_ref), (gate_back, up_back, hidden), tiles):
+            rows = left[:, :, :, cols].reshape(rounds * group, depth)
+            out[...] = mul(rows, right[...].reshape(rounds * group, ff), TN).astype(bf16)
+        for copy in tile_copies(n):
+            copy.start()
+
     cot_load.wait()
-
-    @pl.loop(0, rounds + 2)
-    def _(i):
-        def stage(lag, body):
-            @pl.when((i >= lag) & (i < rounds + lag))
-            def _():
-                body(i - lag)
-
-        stage(0, project_out)
-
-        @pl.when(i < rounds - known)
-        def _():
-            gather_cot.start(known + i)
-
-        for t in range(1, size):
-
-            @pl.when((i > 0) & (i <= rounds - known))
-            def _():
-                gather_cot.step(known + i - 1, t)
-
-            stage(1, lambda j: scatter.step(j, t) if t < size - 1 else scatter.finish(j))
-            if t == size - 1:
-                stage(1, norm)
-            stage(2, lambda j: gather.step(j, t))
-            stage(3, lambda j: scatter_back.step(j, t) if t < size - 1 else scatter_back.finish(j))
-            if t == size - 1:
-                stage(3, lambda j: norm_back(j, j > 0))
-            stage(4, lambda j: gather_back.step(j, t))
-        stage(2, feed)
-        stage(2, feed_back)
-        stage(2, feed_out)
-        stage(4, lambda j: unproject(j, j > 0))
-
-    shares = [count * k // 5 for k in range(6)]
-    for t in range(1, size):
-        if t < size - 1:
-            scatter_back.step(final, t)
-        else:
-            scatter_back.finish(final)
-            norm_back(final, True)
-        gather_back.step(final - 1, t)
-        if t < size - 1:
-            weight_tiles(shares[t - 1], shares[t])
-    unproject(final - 1, True)
-    weight_tiles(shares[2], shares[3])
-    for t in range(1, size):
-        gather_back.step(final, t)
-        if t < size - 1:
-            weight_tiles(shares[t + 2], shares[t + 3])
-    unproject(final, True)
-    for copy in tile_copies(count - 1):
-        copy.wait()
+    held = {}
+
+    def then(kind, copies):
+        for copy in held.get(kind, []):
+            copy.wait()
+        held[kind] = copies
+
+    shares = sum(name[0] == "W" for name in STEPS)
+    for name in STEPS:
+        kind, j, t = name[0], int(name[1]), int(name[2:] or 0)
+        if kind == "A":
+            project_out(j)
+        elif kind == "C":
+            gather_cot.step(j, t) if t else gather_cot.start(j)
+        elif kind == "S" and t < size - 1:
+            scatter.step(j, t)
+        elif kind == "S":
+            scatter.finish(j)
+            norm(j)
+        elif kind == "G":
+            gather.step(j, t)
+        elif kind == "F":
+            then("loads", loads if "loads" not in held else [])
+            then("loads", [])
+            feed(j, t)
+        elif kind == "B":
+            feed_back(j)
+        elif kind == "O":
+            then(kind, [])
+            feed_out(j)
+            then(kind, [down_copy(j)])
+        elif kind == "T" and t < size - 1:
+            scatter_back.step(j, t)
+        elif kind == "T":
+            then(kind, [])
+            scatter_back.finish(j)
+            norm_back(j)
+            then(kind, [back_copy(j)])
+        elif kind == "E":
+            gather_back.step(j, t)
+        elif kind == "U":
+            then(kind, [])
+            unproject(j)
+            then(kind, [ub_copy(j)])
+        elif kind == "W":
+            for n in range(count * j // shares, count * (j + 1) // shares):
+                then(kind, [])
+                weight_tile(n)
+                then(kind, tile_copies(n))
+    for kind in list(held):
+        then(kind, [])
     width = u_ref.shape[3]
 
     def out_tile(n, slot):
@@ -1144,9 +1128,6 @@
 
     for slot in range(slots):
         out_tile(count - slots + slot, slot).wait()
-    ub_copy(final).wait()
-    back_copy(final).wait()
-    down_copy(final).wait()
 
     @pl.loop(0, rounds)
     def _(j):
@@ -1279,16 +1260,15 @@
 
 def last_kernel(size, groups, rounds, count, mixed, *refs):
     take = taker(refs)
-    backs, weights = take(4), take(4)
-    x_ref, gain_ref, second_ref, small_ref, back_in = take(5)
-    a_in = take(1 if mixed else 0)
+    backs = take(4)
+    x_ref, gain_ref, second_ref, small_ref, back_in, a_in, *weights_in = take(10)
     grads = take(count)
-    tokens_out, second_out, first_out, small_out = take(4)
+    tokens_out, sides_out, small_out = take(3)
     grad_outs = take(count + (4 if mixed else 0))
     part, land, total, first, s_send, s_recv = take(6)
-    small_seq, gain_seq, second_tp, first_tp = (take(3) for _ in range(4))
-    nears, a_refs = take(4 if mixed else 0), take(1 if mixed else 0)
-    load_sems = take(1)[0]
+    small_seq, gains_tp = take(3), take(3)
+    nears = take(4 if mixed else 0)
+    a_ref, *weights, load_sems = take(6)
     sums = group_sums(groups, grads + nears, grad_outs, take)
     early, late = sums[:2], sums[2:]
 
@@ -1298,11 +1278,9 @@
 
     for each in sums[:count]:
         each.start()
-    loads = [
-        pltpu.make_async_copy(source, target, load_sems.at[k])
-        for k, (source, target) in enumerate(zip([back_in, *a_in], [tokens_out, *a_refs]))
-    ]
-    for load in loads:
+    pairs = zip([back_in, a_in, *weights_in], [tokens_out, a_ref, *weights])
+    loads = [pltpu.make_async_copy(source, target, load_sems.at[k]) for k, (source, target) in enumerate(pairs)]
+    for load in loads[1:] + loads[:1]:
         load.start()
 
     m, d = x_ref.shape[1:]
@@ -1313,13 +1291,8 @@
     tile = min(512, d)
 
     seq_small = Everyone(groups, "seq", *small_seq)
-    seq_first = Everyone(groups, "seq", *gain_seq)
-    tp_second = Everyone(size, "tp", *second_tp)
-    tp_first = Everyone(size, "tp", *first_tp)
+    tp_gains = Everyone(size, "tp", *gains_tp)
     lines, smalls = d // WIDTH, small_ref.shape[0]
-    stack(second_ref[...], small_seq[0], 0)
-    small_seq[0][lines : lines + smalls, :] = small_ref[...]
-    seq_small.start()
 
     def products(j):
         @pl.loop(0, d // tile)
@@ -1329,6 +1302,7 @@
             for back, weight in zip(backs, weights):
                 term = mul(back[:, j].reshape(group, back.shape[3]), weight[cols, :], NT)
                 acc = term if acc is None else acc + term
+            first[:, cols] += jnp.sum(acc * a_ref[:, j, :, cols].reshape(group, tile).astype(f32), axis=0, keepdims=True)
             part[j, :, :, cols] = acc.astype(bf16).reshape(size, m, tile)
 
         scatter.start(j)
@@ -1341,7 +1315,7 @@
             @pl.loop(0, each.half)
             def _(k):
                 cols = pl.ds(pl.multiple_of((2 * k + side) * depth, depth), depth)
-                left = a_refs[0][:, :, :, cols].reshape(rounds * group, depth)
+                left = a_ref[:, :, :, cols].reshape(rounds * group, depth)
                 into[k] = mul(left, rows, TN).astype(bf16)
 
             if into is each.grad:
@@ -1354,7 +1328,6 @@
             a_back, x = total[r, :], x_ref[j, r, :].astype(f32)
             scale = lax.rsqrt(jnp.mean(x * x, axis=-1, keepdims=True) + epsilon)
             normed = x * scale
-            first[...] += jnp.sum(a_back * normed, axis=0, keepdims=True)
             inner = a_back * gain
             tokens_out[j, r, :] = tokens_out[j, r, :] + scale * (
                 inner - normed * jnp.mean(inner * normed, axis=-1, keepdims=True)
@@ -1368,49 +1341,49 @@
                 scatter.finish(j)
                 norm_back(j)
 
+    for load in loads[1:]:
+        load.wait()
     for j in range(rounds):
         products(j)
         if j < len(early):
             early[j].middle()
-    for load in loads:
-        load.wait()
+    stack(second_ref[...], small_seq[0], 0)
+    stack(first[...] / gain, small_seq[0], lines)
+    small_seq[0][2 * lines : 2 * lines + smalls, :] = small_ref[...]
+    seq_small.start()
+    steps(0, 1, 2)
+    loads[0].wait()
     if mixed:
         for at, (back, each) in enumerate(zip(backs, late)):
             mix(back, each)
-            steps(0, 1, 2) if at == 1 else None
-            steps(0, 2, 3) if at == 3 else None
+            steps(0, 2, 3) if at == 1 else None
     else:
-        steps(0, 1, 3)
+        steps(0, 2, 3)
     for each in early:
         each.relay()
+    steps(0, 3, size)
     for each in late:
         each.middle()
+    steps(1, 1, 3)
     seq_small.finish(small_out)
-    second_tp[0][...] = small_out[:lines, :]
-    tp_second.start()
-    steps(0, 3, size)
-    for j in range(1, rounds):
+    gains_tp[0][...] = small_out[: 2 * lines, :]
+    tp_gains.start()
+    steps(1, 3, size)
+    for each in late[:2]:
+        each.relay()
+    steps(2, 1, 3)
+    for each in late[2:]:
+        each.relay()
+    steps(2, 3, size)
+    for each in early:
+        each.finish()
+    tp_gains.finish(sides_out)
+    for j in range(3, rounds):
         steps(j, 1, size)
-        if j == 1:
-            for each in late[:2]:
-                each.relay()
-        if j == 2:
-            for each in late[2:]:
-                each.relay()
-            early[0].finish()
-
-    stack(first[...], gain_seq[0], 0)
-    seq_first.start()
-    tp_second.finish(second_out)
-    for each in early[1:]:
-        each.finish()
-    seq_first.finish(first_tp[0])
-    tp_first.start()
     for each in late:
         each.finish()
-    tp_first.finish(first_out)
-
-    for each in sums + [seq_small, seq_first, tp_second, tp_first]:
+
+    for each in sums + [seq_small, tp_gains]:
         each.drain()
 
     @pl.loop(0, rounds)
@@ -1419,6 +1392,7 @@
 
 
 def last(size, groups, rounds, backs, weights, a, x, back, gain, second, small, grads, turned):
+    mixed = len(turned) > len(grads)
     rows, d = x.shape
     m = rows // rounds
     c = weights[0].shape[1]
@@ -1426,20 +1400,18 @@
     lines = d // WIDTH
     sems = DMA((2, rounds, size))
     spec = pl.BlockSpec(memory_space=VM)
-    small_rows = lines + small.shape[0]
-    mixed = a is not None
+    small_rows = 2 * lines + small.shape[0]
     shapes = [grad.shape for grad in grads] + ([(groups, d // groups, c)] * 4 if mixed else [])
     outs = pl.pallas_call(
         partial(last_kernel, size, groups, rounds, len(grads), mixed),
         out_shape=[
             jax.ShapeDtypeStruct((rounds, m, d), f32),
-            jax.ShapeDtypeStruct((lines, WIDTH), f32),
-            jax.ShapeDtypeStruct((lines, WIDTH), f32),
+            jax.ShapeDtypeStruct((2 * lines, WIDTH), f32),
             jax.ShapeDtypeStruct((small_rows, WIDTH), f32),
         ]
         + sum_shapes(shapes, turned),
-        in_specs=[spec] * 12 + [pl.BlockSpec(memory_space=pl.ANY)] * (1 + mixed + len(grads)),
-        out_specs=[spec] * (4 + len(shapes)),
+        in_specs=[spec] * 8 + [pl.BlockSpec(memory_space=pl.ANY)] * (6 + len(grads)),
+        out_specs=[spec] * (3 + len(shapes)),
         scratch_shapes=[
             VM((rounds, size, m, d), bf16),
             VM((2, rounds, size - 1, m, d), bf16),
@@ -1449,27 +1421,28 @@
             sems,
         ]
         + everyone_scratch(groups, small_rows)
-        + everyone_scratch(groups, lines)
-        + everyone_scratch(size, lines)
-        + everyone_scratch(size, lines)
-        + ([VM((groups // 2, d // groups, c), bf16)] * 4 + [VM(shape + (d,), bf16)] if mixed else [])
-        + [DMA((2,))]
+        + everyone_scratch(size, 2 * lines)
+        + ([VM((groups // 2, d // groups, c), bf16)] * 4 if mixed else [])
+        + [VM(shape + (d,), bf16)]
+        + [VM((d, c), bf16)] * 4
+        + [DMA((6,))]
         + group_sums_scratch(shapes),
         compiler_params=pltpu.CompilerParams(collective_id=4, has_side_effects=True, vmem_limit_bytes=63 * MIB),
         cost_estimate=pl.CostEstimate(flops=16 * size * rows * d * c, bytes_accessed=56 * MIB, transcendentals=0),
         name="last",
     )(
         *[part.reshape(shape + (c,)) for part in backs],
-        *weights,
         x.reshape(rounds, m, d),
         gain.reshape(1, d),
         second,
         small,
         back.reshape(rounds, m, d),
-        *([a.reshape(shape + (d,))] if mixed else []),
+        a.reshape(shape + (d,)),
+        *weights,
         *[in_pairs(grad) for grad in grads],
     )
-    return (outs[0].reshape(rows, d), outs[1], outs[2], outs[3][lines:]) + tuple(outs[4:])
+    sides = outs[1]
+    return (outs[0].reshape(rows, d), sides[:lines], sides[lines:], outs[2][2 * lines :]) + tuple(outs[3:])
 
 
 def per_device(
@@ -1524,7 +1497,7 @@
         ROUNDS,
         back_rows,
         weights,
-        a if here_too else None,
+        a,
         tokens,
         back,
         first_gain,

time: 591 us -> 591 us (level); the launches traced: 591 us -> 583 us
  Pallas kernels: 559 us -> 551 us
    pallas_call x1, Pallas kernels: 116 us -> 103 us  [front(): pl.pallas_call(partial(front_kernel, size, groups, rounds), out_shape=[ja...]
  transfers between devices with their start and end apart: 1 -> 1, of which waited for: 0 -> 0; matrix products, arithmetic and copies ran while one was open for 1% -> 1% of each run, Pallas kernels for 29% -> 30%
where the time goes in v5:
time: 591 us; the launch traced here: 583 us
  Pallas kernels  551 us (93%)
  between operations  14.3 us (2%)
  local copies, waits for them, and re-layouts  12.7 us (2%)
    pallas_call x1, Pallas kernels, middle(): pl.pallas_call(partial(middle_kernel, size, rounds), out_shape=[jax.Shape...  273 us
    pallas_call x1, Pallas kernels, front(): pl.pallas_call(partial(front_kernel, size, groups, rounds), out_shape=[ja...  103 us
    pallas_call x1, Pallas kernels, last(): pl.pallas_call(partial(last_kernel, size, groups, rounds, len(grads), mix...  102 us
    pallas_call x1, Pallas kernels, scan_backward(): pl.pallas_call(partial(scan_back_kernel, size, len(grads)), out_shape=[ja...  73.5 us
  transfers between devices with their start and end apart: 1, of which 0 were waited for; matrix products, arithmetic and copies ran while one was open for 1% of the time, Pallas kernels for 30%

profile of v5, /device:TPU:0, one launch (start us, length us, event | category | flops | bytes accessed | tf_op | source)
XLA Modules:
  0.0 582.6 jit_solution(8722945145479776791)
XLA Ops:
  7.2 0.0 reduce-scatter.2.cloned.1.call-start
  7.2 1.3 reduce-window.9
  8.6 102.9 %front.1 = (bf16[4,4,64,2048]{3,2,1,0:T(8,128)(2,1)}, f32[1024,512]{1,0:T(8,128)}, f32[1024,512]{1,0:T(8,128)}, f32[1024,512]{1,0:T(8,128)}, f32[1024,512]{1,0:T...) custom-call(s32[7]{0:T(128)} %bitcast.37, ...), custom_call_target="tpu_custom_call" | custom-call | flops 8589934592 | bytes 37748736 | tf_op jit(solution)/shard_map/front/pallas_call | solution.py:699
  111.4 272.7 %middle.1 = (f32[4,64,2048]{2,1,0:T(8,128)}, f32[4,64,2048]{2,1,0:T(8,128)}, bf16[4,4,64,2048]{3,2,1,0:T(8,128)(2,1)}, f32[4,4,64,512]{3,2,1,0:T(8,128)}, f32[1,...) custom-call(bf16[4,4,64,512]{3,2,1,0:T(8,128)(2,1)} %bitcast.54, ...), custom_call_target="tpu_custom_call" | custom-call | flops 57445187584 | bytes 58720256 | tf_op jit(solution)/shard_map/middle/pallas_call | solution.py:1154
  384.1 0.0 reduce-scatter.2.cloned.1.call-update
  384.2 73.5 %scan_backward.1 = (bf16[1024,512]{1,0:T(8,128)(2,1)}, bf16[1024,512]{1,0:T(8,128)(2,1)}, bf16[1024,512]{1,0:T(8,128)(2,1)}, bf16[1024,512]{1,0:T(8,128)(2,1)}, ...) custom-call(s32[7]{0:T(128)} %bitcast.38, f32[1,512]{1,0:T(1,128)} %bitcast.34, f32[1,512]{1,0:T(1,128)} %bitcast.36, ...), custom_call_target="tpu_custom_call" | custom-call | flops 2684354560 | bytes 20971520 | tf_op jit(solution)/shard_map/scan_backward/pallas_call | solution.py:882
  457.6 101.9 %last.1 = (f32[4,64,2048]{2,1,0:T(8,128)}, f32[32,128]{1,0:T(8,128)}, f32[40,128]{1,0:T(8,128)}, f32[1408,256]{1,0:T(8,128)}, f32[512,256]{1,0:T(8,128)}, /*inde...) custom-call(bf16[4,4,64,512]{3,2,1,0:T(8,128)(2,1)} %bitcast.44, ...), custom_call_target="tpu_custom_call" | custom-call | flops 17179869184 | bytes 58720256 | tf_op jit(solution)/shard_map/last/pallas_call | solution.py:1405
  559.5 0.7 slice_bitcast_fusion
  560.3 0.6 dynamic_slice.12
  560.8 0.6 dynamic_slice.15
  561.4 0.8 fusion.1
  562.2 0.7 constant_dynamic-slice_fusion
  562.8 0.0 reduce-scatter.2.cloned.1.call-done
  562.8 0.0 copy-start
  562.8 3.3 fusion
  566.1 0.0 copy-done
  566.1 0.0 copy-start.8
  566.1 0.0 copy-start.7
  566.1 1.3 copy.38
  567.4 0.1 copy-done.8
  567.5 0.0 copy-start.6
  567.5 0.0 copy-start.5
  567.5 0.0 copy-start.4
  567.5 0.8 copy.39
  568.3 0.0 copy-done.7
  568.3 0.0 copy-start.2
  568.3 0.8 copy.40
  569.1 0.0 copy-done.6
  569.1 0.8 copy.41
  569.9 0.0 copy-done.5
  569.9 0.8 copy.42
  570.7 0.0 copy-done.4
  570.7 0.0 copy-start.1
  570.7 0.8 copy.43
  571.5 0.0 copy-done.2
  571.5 1.1 copy.44
  572.6 0.0 copy-done.1
  572.6 0.0 copy-start.3
  572.6 1.1 copy.45
  573.7 0.8 copy-done.3
  574.5 1.1 copy.46
Async XLA Ops:
  7.2 555.7 %reduce-scatter.2.cloned.1.call-start = ((), (), s32[]{:S(2)}) async-start(), calls=%async_computation.1 | async-start | bytes 5242880 | tf_op jit(solution)/shard_map/reduce_scatter | solution.py:1477
  562.8 3.3 copy-start
  566.1 1.4 copy-start.8
  566.1 2.2 copy-start.7
  567.5 1.6 copy-start.6
  567.5 2.4 copy-start.5
  567.5 3.2 copy-start.4
  568.3 3.2 copy-start.2
  570.7 1.9 copy-start.1
  572.6 1.9 copy-start.3
Sparse Core Ops, SparseCore 0:
  384.3 79.0 reduce-scatter.1

commit v6 on v5

--- a/solution.py
+++ b/solution.py
@@ -578,29 +578,6 @@
     cot_load.wait()
     pres = (q_ref, f_ref, i_ref, s_ref)
 
-    @pl.loop(0, rounds)
-    def _(j):
-        for t in range(1, size):
-            gather.step(j, t)
-
-        @pl.when(j >= rounds - known)
-        def _():
-            gather_cot.start(j - (rounds - known))
-
-        rows = a_ref[:, j].reshape(size * m, d)
-        for weight, out in zip(weights, pres):
-            product = mul(rows, weight[...], NN)
-            for z in range(size):
-                at = pl.multiple_of(z * rounds * m + j * m, 16)
-                out[pl.ds(at, m), :] = product[z * m : (z + 1) * m]
-
-    stores = [
-        local(source, target, store_sems.at[k])
-        for k, (source, target) in enumerate(zip((a_ref, *pres), (a_out, q_out, f_out, i_out, s_out)))
-    ]
-    for store in stores:
-        store.start()
-
     rows, c = q_ref.shape
     blocks, heads = rows // WIDTH, c // WIDTH
     base = lax.axis_index("seq") * rows
@@ -613,8 +590,7 @@
         def _(j):
             gather_cot.step(j, t)
 
-    @pl.loop(0, blocks)
-    def _(b):
+    def block(b):
         r = pl.ds(pl.multiple_of(b * WIDTH, WIDTH), WIDTH)
         same, carry, tail, keep = block_masks(base + b * WIDTH, ends_ref)
         for h in range(heads):
@@ -627,25 +603,90 @@
             kd_ref[r, cols] = (key * jnp.exp(middle - run)).astype(bf16)
             qe_ref[r, cols] = (q * jnp.exp(run) * carry).astype(bf16)
             key_tail = (key * jnp.exp(last - run) * tail).astype(bf16)
-            add = mul(i_ref[r, cols].astype(bf16), key_tail, TN)
-            decay = jnp.exp(last) * keep
-            adds[b, h] = add
-            decays[b, h : h + 1, :] = decay
-            state[h] = decay * state[h] + add
-            out_decay[h : h + 1, :] = out_decay[h : h + 1, :] * decay
-
-    out_state[...] = state[...].astype(bf16)
-    states.start(True)
-    cot_steps(1)
-
-    @pl.loop(0, blocks)
-    def _(b):
+            adds[b, h] = mul(i_ref[r, cols].astype(bf16), key_tail, TN)
+            decays[b, h : h + 1, :] = jnp.exp(last) * keep
+
+    def near_part(b):
         r = pl.ds(pl.multiple_of(b * WIDTH, WIDTH), WIDTH)
         same, carry, tail, keep = block_masks(base + b * WIDTH, ends_ref)
         for h in range(heads):
             cols = slice(h * WIDTH, (h + 1) * WIDTH)
             scores = jnp.where(same, mul(qd_ref[r, cols], kd_ref[r, cols], NT), 0.0).astype(bf16)
             o_ref[r, cols] = mul(scores, i_ref[r, cols].astype(bf16), NN)
+
+    own_rows = rounds * m
+    per = own_rows // WIDTH if own_rows % WIDTH == 0 and WIDTH % m == 0 else 0
+    early = [z * per + k for z in range(size) for k in range(per - 1)] if per > 1 else []
+    late = [b for b in range(blocks) if b not in early]
+    ready = (per - 1) * WIDTH // m if early else rounds
+
+    def some_blocks(chosen, body):
+        if chosen is early and early:
+
+            @pl.loop(0, size)
+            def _(z):
+                for k in range(per - 1):
+                    body(z * per + k)
+
+        elif early:
+
+            @pl.loop(0, size)
+            def _(z):
+                body(z * per + per - 1)
+
+        elif chosen is late:
+            pl.loop(0, blocks)(body)
+
+    def project(j):
+        block_rows = a_ref[:, j].reshape(size * m, d)
+        for weight, out in zip(weights, pres):
+            product = mul(block_rows, weight[...], NN)
+            for z in range(size):
+                at = pl.multiple_of(z * own_rows + j * m, 16)
+                out[pl.ds(at, m), :] = product[z * m : (z + 1) * m]
+
+    @pl.loop(0, rounds)
+    def _(j):
+        for t in range(1, size):
+            gather.step(j, t)
+            if early and t == 1:
+
+                @pl.when(j == ready)
+                def _():
+                    some_blocks(early, block)
+
+            if early and t == 2:
+
+                @pl.when(j == ready)
+                def _():
+                    some_blocks(early, near_part)
+
+        @pl.when(j >= rounds - known)
+        def _():
+            gather_cot.start(j - (rounds - known))
+
+        project(j)
+
+    stores = [
+        local(source, target, store_sems.at[k])
+        for k, (source, target) in enumerate(zip((a_ref, *pres), (a_out, q_out, f_out, i_out, s_out)))
+    ]
+    for store in stores:
+        store.start()
+
+    some_blocks(late, block)
+
+    @pl.loop(0, blocks)
+    def _(b):
+        for h in range(heads):
+            decay = decays[b, h : h + 1, :]
+            state[h] = decay * state[h] + adds[b, h]
+            out_decay[h : h + 1, :] = out_decay[h : h + 1, :] * decay
+
+    out_state[...] = state[...].astype(bf16)
+    states.start(True)
+    cot_steps(1)
+    some_blocks(late, near_part)
 
     states.compose(True, state)
     for t in range(2, size - 1):
@@ -734,16 +775,18 @@
     return [outs[0].reshape(rows, d)] + list(outs[1:])
 
 
-def scan_back_kernel(size, count, *refs):
+def scan_back_kernel(size, line, rounds, count, *refs):
     take = taker(refs)
-    ends_ref, bound_ref, gain_ref, *loaded = take(10)
+    ends_ref, bound_ref, gain_ref, norm_gain_ref, *loaded = take(16)
     grads = take(count)
-    dq_ref, df_ref, di_ref, ds_ref, small_ref = take(5)
+    dq_ref, df_ref, di_ref, ds_ref, small_ref, first_ref, part_out = take(7)
     grad_outs = take(count)
     qd_ref, kd_ref, qe_ref, kt_ref, do_ref, run_ref, adds, decays = take(8)
     state, out_state, out_decay, land_state, land_decay, sems = take(6)
-    *inputs, load_sems = take(8)
-    q_ref, f_ref, i_ref, s_ref, o_ref, ub_ref, starts_ref = inputs
+    *inputs, load_sems = take(13)
+    q_ref, f_ref, i_ref, s_ref, o_ref, ub_ref, starts_ref, *weights, a_ref = inputs
+    *loaded, a_in = loaded
+    stage, stage_sems, a_sems = take(3)
     loads = [
         pltpu.make_async_copy(source, target, load_sems.at[k]) for k, (source, target) in enumerate(zip(loaded, inputs))
     ]
@@ -760,7 +803,7 @@
     state[...] = jnp.zeros_like(state)
     out_decay[...] = jnp.ones_like(out_decay)
     small_ref[...] = jnp.zeros_like(small_ref)
-    for load in loads:
+    for load in loads[:7]:
         load.wait()
 
     @pl.loop(0, blocks)
@@ -867,37 +910,106 @@
             dq_ref[r, cols] = (q_back * silu_slope(q_ref[r, cols])).astype(bf16)
             state[h] = adds[b, h] + decay * state[h]
 
+    for load in loads[7:]:
+        load.wait()
+    m, d = a_ref.shape[2:]
+
+    def a_load(j):
+        slot = lax.rem(j, 2)
+        return pltpu.make_async_copy(a_in.at[:, j], a_ref.at[slot], a_sems.at[slot])
+
+    for j in range(min(2, rounds)):
+        a_load(j).start()
+    tile = min(512, d)
+    first_ref[...] = jnp.zeros_like(first_ref)
+
+    def part_copy(j):
+        return pltpu.make_async_copy(stage.at[lax.rem(j, 2)], part_out.at[j], stage_sems.at[lax.rem(j, 2)])
+
+    @pl.loop(0, rounds)
+    def _(j):
+        @pl.when(j > 1)
+        def _():
+            part_copy(j - 2).wait()
+
+        a_load(j).wait()
+
+        def round_rows(ref):
+            places = [pl.multiple_of(z * rounds * m + j * m, 16) for z in range(line)]
+            return jnp.concatenate([ref[pl.ds(at, m), :] for at in places], axis=0)
+
+        @pl.loop(0, d // tile)
+        def _(n):
+            cols = pl.ds(pl.multiple_of(n * tile, tile), tile)
+            acc = None
+            for back, weight in zip((dq_ref, df_ref, di_ref, ds_ref), weights):
+                term = mul(round_rows(back), weight[cols, :], NT)
+                acc = term if acc is None else acc + term
+            normed = a_ref[lax.rem(j, 2), :, :, cols].reshape(line * m, tile).astype(f32)
+            first_ref[:, cols] += jnp.sum(acc * normed, axis=0, keepdims=True)
+            stage[lax.rem(j, 2), :, :, cols] = acc.astype(bf16).reshape(line, m, tile)
+
+        part_copy(j).start()
+
+        @pl.when(j + 2 < rounds)
+        def _():
+            a_load(j + 2).start()
+
+    first_ref[...] = first_ref[...] / norm_gain_ref[...]
     for each in sums:
         each.finish()
+    for j in range(max(0, rounds - 2), rounds):
+        part_copy(j).wait()
     states.drain(False)
     for each in sums:
         each.drain()
 
 
-def scan_backward(size, ends, bound, gain, q, f, i, s, o, ub, starts, grads):
+def scan_backward(size, line, rounds, ends, bound, gain, q, f, i, s, o, ub, starts, norm_gain, a, weights, grads):
     rows, c = q.shape
+    d = a.shape[1]
+    shape = (line, rounds, rows // line // rounds, d)
+    part = (rounds, line) + shape[2:]
     blocks, heads = rows // WIDTH, c // WIDTH
     low, wide = VM((rows, c), bf16), VM((rows, c), f32)
     spec = pl.BlockSpec(memory_space=VM)
     return pl.pallas_call(
-        partial(scan_back_kernel, size, len(grads)),
+        partial(scan_back_kernel, size, line, rounds, len(grads)),
         out_shape=[jax.ShapeDtypeStruct((rows, c), bf16)] * 4
-        + [jax.ShapeDtypeStruct((2 * heads, WIDTH), f32)]
+        + [jax.ShapeDtypeStruct((2 * heads, WIDTH), f32), jax.ShapeDtypeStruct((1, d), f32)]
+        + [jax.ShapeDtypeStruct(part, bf16)]
         + sum_shapes([grad.shape for grad in grads], [False] * len(grads)),
         in_specs=[pl.BlockSpec(memory_space=pltpu.SMEM)]
-        + [spec] * 2
-        + [pl.BlockSpec(memory_space=pl.ANY)] * (7 + len(grads)),
-        out_specs=[spec] * (5 + len(grads)),
+        + [spec] * 3
+        + [pl.BlockSpec(memory_space=pl.ANY)] * (12 + len(grads)),
+        out_specs=[spec] * 6 + [pl.BlockSpec(memory_space=pl.ANY)] + [spec] * len(grads),
         scratch_shapes=[low] * 5
         + [wide, VM((blocks, heads, WIDTH, WIDTH), f32), VM((blocks, 8, WIDTH), f32)]
         + states_scratch(size, heads)
         + [wide] * 6
-        + [VM(starts.shape, bf16), DMA((7,))]
+        + [VM(starts.shape, bf16)]
+        + [VM((d, c), bf16)] * 4
+        + [VM((2,) + part[1:], bf16), DMA((11,)), VM((2,) + part[1:], bf16), DMA((2,)), DMA((2,))]
         + group_sums_scratch([grad.shape for grad in grads]),
-        compiler_params=pltpu.CompilerParams(collective_id=2, has_side_effects=True, vmem_limit_bytes=60 * MIB),
-        cost_estimate=pl.CostEstimate(flops=40 * rows * c * WIDTH, bytes_accessed=20 * MIB, transcendentals=16 * rows * c),
+        compiler_params=pltpu.CompilerParams(collective_id=2, has_side_effects=True, vmem_limit_bytes=63 * MIB),
+        cost_estimate=pl.CostEstimate(flops=8 * rows * c * d, bytes_accessed=40 * MIB, transcendentals=16 * rows * c),
         name="scan_backward",
-    )(ends, bound, gain, q, f, i, s, o, ub, starts, *[in_pairs(grad) for grad in grads])
+    )(
+        ends,
+        bound,
+        gain,
+        norm_gain.reshape(1, d),
+        q,
+        f,
+        i,
+        s,
+        o,
+        ub,
+        starts,
+        *weights,
+        a.reshape(shape),
+        *[in_pairs(grad) for grad in grads],
+    )
 
 
 def middle_kernel(size, rounds, *refs):
@@ -1261,14 +1373,14 @@
 def last_kernel(size, groups, rounds, count, mixed, *refs):
     take = taker(refs)
     backs = take(4)
-    x_ref, gain_ref, second_ref, small_ref, back_in, a_in, *weights_in = take(10)
+    x_ref, gain_ref, second_ref, small_ref, first_ref, back_in, a_in, part_in = take(8)
     grads = take(count)
-    tokens_out, sides_out, small_out = take(3)
+    tokens_far, small_out = take(2)
     grad_outs = take(count + (4 if mixed else 0))
-    part, land, total, first, s_send, s_recv = take(6)
-    small_seq, gains_tp = take(3), take(3)
+    part, land, total, s_send, s_recv = take(5)
+    small_seq, gains_tp, sides = take(3), take(3), take(1)[0]
     nears = take(4 if mixed else 0)
-    a_ref, *weights, load_sems = take(6)
+    a_ref, tokens_out, load_sems, store_sems = take(4)
     sums = group_sums(groups, grads + nears, grad_outs, take)
     early, late = sums[:2], sums[2:]
 
@@ -1278,34 +1390,31 @@
 
     for each in sums[:count]:
         each.start()
-    pairs = zip([back_in, a_in, *weights_in], [tokens_out, a_ref, *weights])
-    loads = [pltpu.make_async_copy(source, target, load_sems.at[k]) for k, (source, target) in enumerate(pairs)]
-    for load in loads[1:] + loads[:1]:
-        load.start()
-
     m, d = x_ref.shape[1:]
+    tile = min(512, d)
+    local = pltpu.make_async_copy
+
+    def part_load(j):
+        return local(part_in.at[j], part.at[j], load_sems.at[2 + j])
+
+    a_load = local(a_in, a_ref, load_sems.at[1])
+    back_load = local(back_in, tokens_out, load_sems.at[0])
+
+    for j in range(rounds):
+        part_load(j).start()
+    a_load.start()
+    back_load.start()
+
+    def store(j):
+        return local(tokens_out.at[j], tokens_far.at[j], store_sems.at[j])
+
     group = size * m
     scatter = Scatter(size, s_send, s_recv, part, land, total)
     gain = gain_ref[...]
-    first[...] = jnp.zeros_like(first)
-    tile = min(512, d)
 
     seq_small = Everyone(groups, "seq", *small_seq)
     tp_gains = Everyone(size, "tp", *gains_tp)
     lines, smalls = d // WIDTH, small_ref.shape[0]
-
-    def products(j):
-        @pl.loop(0, d // tile)
-        def _(n):
-            cols = pl.ds(pl.multiple_of(n * tile, tile), tile)
-            acc = None
-            for back, weight in zip(backs, weights):
-                term = mul(back[:, j].reshape(group, back.shape[3]), weight[cols, :], NT)
-                acc = term if acc is None else acc + term
-            first[:, cols] += jnp.sum(acc * a_ref[:, j, :, cols].reshape(group, tile).astype(f32), axis=0, keepdims=True)
-            part[j, :, :, cols] = acc.astype(bf16).reshape(size, m, tile)
-
-        scatter.start(j)
 
     def mix(back, each):
         rows = back[...].reshape(rounds * group, back.shape[3])
@@ -1340,34 +1449,35 @@
             else:
                 scatter.finish(j)
                 norm_back(j)
-
-    for load in loads[1:]:
-        load.wait()
+                store(j).start()
+
+    stack(second_ref[...], gains_tp[0], 0)
+    stack(first_ref[...], gains_tp[0], lines)
+    tp_gains.start()
     for j in range(rounds):
-        products(j)
-        if j < len(early):
-            early[j].middle()
-    stack(second_ref[...], small_seq[0], 0)
-    stack(first[...] / gain, small_seq[0], lines)
+        part_load(j).wait()
+        scatter.start(j)
+    tp_gains.finish(sides)
+    small_seq[0][: 2 * lines, :] = sides[...]
     small_seq[0][2 * lines : 2 * lines + smalls, :] = small_ref[...]
     seq_small.start()
+    for each in early:
+        each.middle()
+    a_load.wait()
     steps(0, 1, 2)
-    loads[0].wait()
+    back_load.wait()
     if mixed:
         for at, (back, each) in enumerate(zip(backs, late)):
             mix(back, each)
-            steps(0, 2, 3) if at == 1 else None
+            steps(0, 2, 3) if at == 0 else None
+            steps(0, 3, size) if at == 2 else None
     else:
-        steps(0, 2, 3)
+        steps(0, 2, size)
     for each in early:
         each.relay()
-    steps(0, 3, size)
     for each in late:
         each.middle()
     steps(1, 1, 3)
-    seq_small.finish(small_out)
-    gains_tp[0][...] = small_out[: 2 * lines, :]
-    tp_gains.start()
     steps(1, 3, size)
     for each in late[:2]:
         each.relay()
@@ -1377,7 +1487,7 @@
     steps(2, 3, size)
     for each in early:
         each.finish()
-    tp_gains.finish(sides_out)
+    seq_small.finish(small_out)
     for j in range(3, rounds):
         steps(j, 1, size)
     for each in late:
@@ -1389,13 +1499,14 @@
     @pl.loop(0, rounds)
     def _(j):
         scatter.drain(j)
-
-
-def last(size, groups, rounds, backs, weights, a, x, back, gain, second, small, grads, turned):
+        store(j).wait()
+
+
+def last(size, groups, rounds, backs, part, a, x, back, gain, second, first, small, grads, turned):
     mixed = len(turned) > len(grads)
     rows, d = x.shape
     m = rows // rounds
-    c = weights[0].shape[1]
+    c = backs[0].shape[1]
     shape = (size, rounds, m)
     lines = d // WIDTH
     sems = DMA((2, rounds, size))
@@ -1406,26 +1517,24 @@
         partial(last_kernel, size, groups, rounds, len(grads), mixed),
         out_shape=[
             jax.ShapeDtypeStruct((rounds, m, d), f32),
-            jax.ShapeDtypeStruct((2 * lines, WIDTH), f32),
             jax.ShapeDtypeStruct((small_rows, WIDTH), f32),
         ]
         + sum_shapes(shapes, turned),
-        in_specs=[spec] * 8 + [pl.BlockSpec(memory_space=pl.ANY)] * (6 + len(grads)),
-        out_specs=[spec] * (3 + len(shapes)),
+        in_specs=[spec] * 9 + [pl.BlockSpec(memory_space=pl.ANY)] * (3 + len(grads)),
+        out_specs=[pl.BlockSpec(memory_space=pl.ANY)] + [spec] * (1 + len(shapes)),
         scratch_shapes=[
             VM((rounds, size, m, d), bf16),
             VM((2, rounds, size - 1, m, d), bf16),
             VM((m, d), f32),
-            VM((1, d), f32),
             sems,
             sems,
         ]
         + everyone_scratch(groups, small_rows)
         + everyone_scratch(size, 2 * lines)
+        + [VM((2 * lines, WIDTH), f32)]
         + ([VM((groups // 2, d // groups, c), bf16)] * 4 if mixed else [])
         + [VM(shape + (d,), bf16)]
-        + [VM((d, c), bf16)] * 4
-        + [DMA((6,))]
+        + [VM((rounds, m, d), f32), DMA((2 + rounds,)), DMA((rounds,))]
         + group_sums_scratch(shapes),
         compiler_params=pltpu.CompilerParams(collective_id=4, has_side_effects=True, vmem_limit_bytes=63 * MIB),
         cost_estimate=pl.CostEstimate(flops=16 * size * rows * d * c, bytes_accessed=56 * MIB, transcendentals=0),
@@ -1436,13 +1545,14 @@
         gain.reshape(1, d),
         second,
         small,
+        first,
         back.reshape(rounds, m, d),
         a.reshape(shape + (d,)),
-        *weights,
+        part,
         *[in_pairs(grad) for grad in grads],
     )
     sides = outs[1]
-    return (outs[0].reshape(rows, d), sides[:lines], sides[lines:], outs[2][2 * lines :]) + tuple(outs[3:])
+    return (outs[0].reshape(rows, d), sides[:lines], sides[lines : 2 * lines], sides[2 * lines :]) + tuple(outs[2:])
 
 
 def per_device(
@@ -1485,8 +1595,24 @@
         return chunks(lax.dot_general(left, right, TN, preferred_element_type=f32).astype(bf16))
 
     outs, gates, ups, downs = (chunks(grad) for grad in wide)
-    dq, df, di, ds, small, gate_grad, up_grad = scan_backward(
-        groups, ends, bound, head_gain, q, f, i, s, o, ub, starts, [gates, ups]
+    dq, df, di, ds, small, first, part, gate_grad, up_grad = scan_backward(
+        groups,
+        size,
+        ROUNDS,
+        ends,
+        bound,
+        head_gain,
+        q,
+        f,
+        i,
+        s,
+        o,
+        ub,
+        starts,
+        first_gain,
+        a,
+        weights,
+        [gates, ups],
     )
     back_rows = (dq, df, di, ds)
     here_too = groups == 8
@@ -1496,12 +1622,13 @@
         groups,
         ROUNDS,
         back_rows,
-        weights,
+        part,
         a,
         tokens,
         back,
         first_gain,
         second,
+        first,
         small,
         others,
         [True, True] + [False] * 4,

time: 591 us -> 584 us (0.988)
  Pallas kernels: 551 us -> 544 us
    pallas_call x1, Pallas kernels: 102 us -> 89.3 us  [last(): pl.pallas_call(partial(last_kernel, size, groups, rounds, len(grads), mix...]
    pallas_call x1, Pallas kernels: 73.5 us -> 84.7 us  [scan_backward(): pl.pallas_call(partial(scan_back_kernel, size, line, rounds, len(grads)),...]
where the time goes in v6:
time: 584 us; the launch traced here: 576 us
  Pallas kernels  544 us (93%)
  between operations  14.3 us (2%)
  local copies, waits for them, and re-layouts  12.7 us (2%)
    pallas_call x1, Pallas kernels, middle(): pl.pallas_call(partial(middle_kernel, size, rounds), out_shape=[jax.Shape...  270 us
    pallas_call x1, Pallas kernels, front(): pl.pallas_call(partial(front_kernel, size, groups, rounds), out_shape=[ja...  99.8 us
    pallas_call x1, Pallas kernels, last(): pl.pallas_call(partial(last_kernel, size, groups, rounds, len(grads), mix...  89.3 us
    pallas_call x1, Pallas kernels, scan_backward(): pl.pallas_call(partial(scan_back_kernel, size, line, rounds, len(grads)),...  84.7 us
  transfers between devices with their start and end apart: 1, of which 0 were waited for; matrix products, arithmetic and copies ran while one was open for 1% of the time, Pallas kernels for 30%

profile of v6, /device:TPU:0, one launch (start us, length us, event | category | flops | bytes accessed | tf_op | source)
XLA Modules:
  0.0 575.7 jit_solution(4460437416853127807)
XLA Ops:
  7.2 0.0 reduce-scatter.2.cloned.1.call-start
  7.2 1.3 reduce-window.9
  8.6 99.8 %front.1 = (bf16[4,4,64,2048]{3,2,1,0:T(8,128)(2,1)}, f32[1024,512]{1,0:T(8,128)}, f32[1024,512]{1,0:T(8,128)}, f32[1024,512]{1,0:T(8,128)}, f32[1024,512]{1,0:T...) custom-call(s32[7]{0:T(128)} %bitcast.40, ...), custom_call_target="tpu_custom_call" | custom-call | flops 8589934592 | bytes 37748736 | tf_op jit(solution)/shard_map/front/pallas_call | solution.py:740
  108.4 270.2 %middle.1 = (f32[4,64,2048]{2,1,0:T(8,128)}, f32[4,64,2048]{2,1,0:T(8,128)}, bf16[4,4,64,2048]{3,2,1,0:T(8,128)(2,1)}, f32[4,4,64,512]{3,2,1,0:T(8,128)}, f32[1,...) custom-call(bf16[4,4,64,512]{3,2,1,0:T(8,128)(2,1)} %bitcast.55, ...), custom_call_target="tpu_custom_call" | custom-call | flops 57445187584 | bytes 58720256 | tf_op jit(solution)/shard_map/middle/pallas_call | solution.py:1266
  378.6 0.0 reduce-scatter.2.cloned.1.call-update
  378.6 84.7 %scan_backward.1 = (bf16[1024,512]{1,0:T(8,128)(2,1)}, bf16[1024,512]{1,0:T(8,128)(2,1)}, bf16[1024,512]{1,0:T(8,128)(2,1)}, bf16[1024,512]{1,0:T(8,128)(2,1)}, ...) custom-call(s32[7]{0:T(128)} %bitcast.41, ...), custom_call_target="tpu_custom_call" | custom-call | flops 8589934592 | bytes 41943040 | tf_op jit(solution)/shard_map/scan_backward/pallas_call | solution.py:976
  463.3 89.3 %last.1 = (f32[4,64,2048]{2,1,0:T(8,128)}, f32[40,128]{1,0:T(8,128)}, f32[1408,256]{1,0:T(8,128)}, f32[512,256]{1,0:T(8,128)}, f32[256,512]{1,0:T(8,128)}, /*ind...) custom-call(bf16[4,4,64,512]{3,2,1,0:T(8,128)(2,1)} %bitcast.47, bf16[4,4,64,512]{3,2,1,0:T(8,128)(2,1)} %bitcast.48, ...), custom_call_target="tpu_custom_call" | custom-call | flops 17179869184 | bytes 58720256 | tf_op jit(solution)/shard_map/last/pallas_call | solution.py:1516
  552.7 0.7 slice_bitcast_fusion
  553.4 0.6 dynamic_slice.12
  554.0 0.6 dynamic_slice.15
  554.6 0.8 fusion.1
  555.3 0.7 constant_dynamic-slice_fusion
  556.0 0.0 reduce-scatter.2.cloned.1.call-done
  556.0 0.0 copy-start
  556.0 3.3 fusion
  559.3 0.0 copy-done
  559.3 0.0 copy-start.8
  559.3 0.0 copy-start.7
  559.3 1.3 copy.38
  560.6 0.1 copy-done.8
  560.6 0.0 copy-start.6
  560.6 0.0 copy-start.5
  560.6 0.0 copy-start.4
  560.6 0.8 copy.39
  561.4 0.0 copy-done.7
  561.4 0.0 copy-start.2
  561.4 0.8 copy.40
  562.2 0.0 copy-done.6
  562.2 0.8 copy.41
  563.0 0.0 copy-done.5
  563.0 0.8 copy.42
  563.8 0.0 copy-done.4
  563.8 0.0 copy-start.1
  563.8 0.8 copy.43
  564.6 0.0 copy-done.2
  564.6 1.1 copy.44
  565.7 0.0 copy-done.1
  565.7 0.0 copy-start.3
  565.7 1.1 copy.45
  566.8 0.8 copy-done.3
  567.6 1.1 copy.46
Async XLA Ops:
  7.2 548.8 %reduce-scatter.2.cloned.1.call-start = ((), (), s32[]{:S(2)}) async-start(), calls=%async_computation.1 | async-start | bytes 5242880 | tf_op jit(solution)/shard_map/reduce_scatter | solution.py:1587
  556.0 3.3 copy-start
  559.3 1.4 copy-start.8
  559.3 2.2 copy-start.7
  560.6 1.6 copy-start.6
  560.6 2.4 copy-start.5
  560.6 3.2 copy-start.4
  561.4 3.2 copy-start.2
  563.8 1.9 copy-start.1
  565.7 1.9 copy-start.3
Sparse Core Ops, SparseCore 0:
  378.7 80.5 reduce-scatter.1

commit v7 on v6

--- a/solution.py
+++ b/solution.py
@@ -12,12 +12,12 @@
 KNOWN = 1
 PIECES = 3
 STEPS = (
-    "C10", "C11", "C20", "A0", "C12", "C13", "A1", "C21", "C22", "C23", "S01", "C30", "S11", "S02", "S03", "A2",
-    "A3", "C31", "C32", "C33", "G01", "G02", "S21", "S22", "S12", "S23", "G03", "F00", "F01", "F02", "O0", "S13",
-    "B0", "S31", "G11", "T01", "T02", "G12", "G13", "F10", "F11", "F12", "O1", "G21", "T03", "B1", "S32", "G22",
-    "G23", "F20", "E01", "F21", "F22", "E02", "E03", "S33", "T11", "T12", "T13", "G31", "O2", "E11", "B2", "U0",
-    "T21", "G32", "G33", "F30", "F31", "T22", "F32", "O3", "E12", "T23", "B3", "W0", "E21", "T31", "T32", "E22",
-    "W1", "W2", "T33", "W3", "E23", "W5", "E31", "E13", "U1", "W6", "W4", "U2", "W7", "E32", "E33", "U3",
+    "C10", "C11", "C20", "A0", "C12", "A1", "C21", "C22", "C13", "S01", "C30", "S11", "S02", "S03", "C23", "A2",
+    "C31", "A3", "G01", "G02", "S21", "S22", "S12", "S23", "G03", "F00", "F01", "F02", "O0", "S13", "B0", "C32",
+    "C33", "G11", "G12", "G13", "T01", "S31", "F10", "F11", "F12", "O1", "T02", "G21", "T03", "B1", "S32", "G22",
+    "G23", "F20", "E01", "S33", "E02", "E03", "F21", "F22", "T11", "T12", "T13", "G31", "O2", "B2", "E11", "U0",
+    "T21", "G32", "G33", "F30", "F31", "T22", "F32", "O3", "E12", "T23", "B3", "W0", "E21", "E13", "U1", "T31",
+    "T32", "E22", "W1", "W2", "T33", "W3", "E23", "W5", "E31", "W6", "W4", "U2", "W7", "E32", "E33", "U3",
 )
 MIB = 1 << 20
 epsilon = 1e-05
@@ -779,18 +779,20 @@
     take = taker(refs)
     ends_ref, bound_ref, gain_ref, norm_gain_ref, *loaded = take(16)
     grads = take(count)
-    dq_ref, df_ref, di_ref, ds_ref, small_ref, first_ref, part_out = take(7)
+    *back_outs, small_ref, first_ref, part_out = take(7)
     grad_outs = take(count)
     qd_ref, kd_ref, qe_ref, kt_ref, do_ref, run_ref, adds, decays = take(8)
     state, out_state, out_decay, land_state, land_decay, sems = take(6)
     *inputs, load_sems = take(13)
     q_ref, f_ref, i_ref, s_ref, o_ref, ub_ref, starts_ref, *weights, a_ref = inputs
     *loaded, a_in = loaded
-    stage, stage_sems, a_sems = take(3)
+    stage, stage_sems, a_sems, *backs, back_sems = take(8)
+    dq_ref, df_ref, di_ref, ds_ref = backs
     loads = [
         pltpu.make_async_copy(source, target, load_sems.at[k]) for k, (source, target) in enumerate(zip(loaded, inputs))
     ]
-    for load in loads:
+    soon, later = [loads[k] for k in (4, 3, 5, 0, 1)], [loads[k] for k in (2, 6)]
+    for load in soon + later:
         load.start()
     sums = group_sums(size, grads, grad_outs, take)
     greet(*group_peers(size, "seq"))
@@ -803,7 +805,7 @@
     state[...] = jnp.zeros_like(state)
     out_decay[...] = jnp.ones_like(out_decay)
     small_ref[...] = jnp.zeros_like(small_ref)
-    for load in loads[:7]:
+    for load in soon:
         load.wait()
 
     @pl.loop(0, blocks)
@@ -850,6 +852,10 @@
 
     out_state[...] = state[...].astype(bf16)
     states.start(False)
+    for load in later:
+        load.wait()
+    for load in loads[7:]:
+        load.start()
     for each in sums[:1]:
         each.relay()
     for each in sums[1:]:
@@ -910,6 +916,11 @@
             dq_ref[r, cols] = (q_back * silu_slope(q_ref[r, cols])).astype(bf16)
             state[h] = adds[b, h] + decay * state[h]
 
+    stores = [
+        pltpu.make_async_copy(source, target, back_sems.at[k]) for k, (source, target) in enumerate(zip(backs, back_outs))
+    ]
+    for store in stores:
+        store.start()
     for load in loads[7:]:
         load.wait()
     m, d = a_ref.shape[2:]
@@ -960,6 +971,8 @@
         each.finish()
     for j in range(max(0, rounds - 2), rounds):
         part_copy(j).wait()
+    for store in stores:
+        store.wait()
     states.drain(False)
     for each in sums:
         each.drain()
@@ -982,7 +995,10 @@
         in_specs=[pl.BlockSpec(memory_space=pltpu.SMEM)]
         + [spec] * 3
         + [pl.BlockSpec(memory_space=pl.ANY)] * (12 + len(grads)),
-        out_specs=[spec] * 6 + [pl.BlockSpec(memory_space=pl.ANY)] + [spec] * len(grads),
+        out_specs=[pl.BlockSpec(memory_space=pl.ANY)] * 4
+        + [spec] * 2
+        + [pl.BlockSpec(memory_space=pl.ANY)]
+        + [spec] * len(grads),
         scratch_shapes=[low] * 5
         + [wide, VM((blocks, heads, WIDTH, WIDTH), f32), VM((blocks, 8, WIDTH), f32)]
         + states_scratch(size, heads)
@@ -990,6 +1006,8 @@
         + [VM(starts.shape, bf16)]
         + [VM((d, c), bf16)] * 4
         + [VM((2,) + part[1:], bf16), DMA((11,)), VM((2,) + part[1:], bf16), DMA((2,)), DMA((2,))]
+        + [low] * 4
+        + [DMA((4,))]
         + group_sums_scratch([grad.shape for grad in grads]),
         compiler_params=pltpu.CompilerParams(collective_id=2, has_side_effects=True, vmem_limit_bytes=63 * MIB),
         cost_estimate=pl.CostEstimate(flops=8 * rows * c * d, bytes_accessed=40 * MIB, transcendentals=16 * rows * c),
@@ -1373,14 +1391,14 @@
 def last_kernel(size, groups, rounds, count, mixed, *refs):
     take = taker(refs)
     backs = take(4)
-    x_ref, gain_ref, second_ref, small_ref, first_ref, back_in, a_in, part_in = take(8)
+    x_ref, gain_ref, second_ref, small_ref, first_ref, back_in, a_in, part_in, res_in, down_in = take(10)
     grads = take(count)
-    tokens_far, small_out = take(2)
+    tokens_far, small_out, output_ref = take(3)
     grad_outs = take(count + (4 if mixed else 0))
     part, land, total, s_send, s_recv = take(5)
     small_seq, gains_tp, sides = take(3), take(3), take(1)[0]
     nears = take(4 if mixed else 0)
-    a_ref, tokens_out, load_sems, store_sems = take(4)
+    a_ref, tokens_out, res_ref, down_ref, load_sems, store_sems = take(6)
     sums = group_sums(groups, grads + nears, grad_outs, take)
     early, late = sums[:2], sums[2:]
 
@@ -1404,6 +1422,12 @@
         part_load(j).start()
     a_load.start()
     back_load.start()
+    output_loads = [
+        local(source, target, load_sems.at[2 + rounds + k])
+        for k, (source, target) in enumerate(((res_in, res_ref), (down_in, down_ref)))
+    ]
+    for load in output_loads:
+        load.start()
 
     def store(j):
         return local(tokens_out.at[j], tokens_far.at[j], store_sems.at[j])
@@ -1477,6 +1501,14 @@
         each.relay()
     for each in late:
         each.middle()
+    for load in output_loads:
+        load.wait()
+
+    @pl.loop(0, rounds * m // 16)
+    def _(g):
+        r = pl.ds(pl.multiple_of(g * 16, 16), 16)
+        output_ref[r, :] = (res_ref[r, :] + down_ref[r, :].astype(f32)).astype(bf16)
+
     steps(1, 1, 3)
     steps(1, 3, size)
     for each in late[:2]:
@@ -1502,7 +1534,7 @@
         store(j).wait()
 
 
-def last(size, groups, rounds, backs, part, a, x, back, gain, second, first, small, grads, turned):
+def last(size, groups, rounds, backs, part, a, x, back, gain, second, first, small, residual, down, grads, turned):
     mixed = len(turned) > len(grads)
     rows, d = x.shape
     m = rows // rounds
@@ -1518,10 +1550,11 @@
         out_shape=[
             jax.ShapeDtypeStruct((rounds, m, d), f32),
             jax.ShapeDtypeStruct((small_rows, WIDTH), f32),
+            jax.ShapeDtypeStruct((rows, d), bf16),
         ]
         + sum_shapes(shapes, turned),
-        in_specs=[spec] * 9 + [pl.BlockSpec(memory_space=pl.ANY)] * (3 + len(grads)),
-        out_specs=[pl.BlockSpec(memory_space=pl.ANY)] + [spec] * (1 + len(shapes)),
+        in_specs=[spec] * 9 + [pl.BlockSpec(memory_space=pl.ANY)] * (5 + len(grads)),
+        out_specs=[pl.BlockSpec(memory_space=pl.ANY)] + [spec] * (2 + len(shapes)),
         scratch_shapes=[
             VM((rounds, size, m, d), bf16),
             VM((2, rounds, size - 1, m, d), bf16),
@@ -1534,7 +1567,7 @@
         + [VM((2 * lines, WIDTH), f32)]
         + ([VM((groups // 2, d // groups, c), bf16)] * 4 if mixed else [])
         + [VM(shape + (d,), bf16)]
-        + [VM((rounds, m, d), f32), DMA((2 + rounds,)), DMA((rounds,))]
+        + [VM((rounds, m, d), f32), VM((rows, d), f32), VM((rows, d), bf16), DMA((4 + rounds,)), DMA((rounds,))]
         + group_sums_scratch(shapes),
         compiler_params=pltpu.CompilerParams(collective_id=4, has_side_effects=True, vmem_limit_bytes=63 * MIB),
         cost_estimate=pl.CostEstimate(flops=16 * size * rows * d * c, bytes_accessed=56 * MIB, transcendentals=0),
@@ -1549,6 +1582,8 @@
         back.reshape(rounds, m, d),
         a.reshape(shape + (d,)),
         part,
+        residual,
+        down,
         *[in_pairs(grad) for grad in grads],
     )
     sides = outs[1]
@@ -1585,7 +1620,6 @@
     )
     down, ub = lax.optimization_barrier((down, ub))
     down = lax.psum_scatter(down, "tp", scatter_dimension=0, tiled=True)
-    output = (residual + down.astype(f32)).astype(bf16)
     d = tokens.shape[1]
 
     def chunks(grad):
@@ -1617,7 +1651,7 @@
     back_rows = (dq, df, di, ds)
     here_too = groups == 8
     others = [downs, outs] + ([] if here_too else [grad_of(a, part) for part in back_rows])
-    tokens_grad, second_sum, first_sum, small_sum, *sums = last(
+    tokens_grad, second_sum, first_sum, small_sum, output, *sums = last(
         size,
         groups,
         ROUNDS,
@@ -1630,6 +1664,8 @@
         second,
         first,
         small,
+        residual,
+        down,
         others,
         [True, True] + [False] * 4,
     )

time: 584 us -> 579 us (level)
    unnamed x27 -> x28, local copies, waits for them, and re-layouts: 9.44 us -> 11.7 us
  transfers between devices with their start and end apart: 1 -> 1, of which waited for: 0 -> 0; matrix products, arithmetic and copies ran while one was open for 1% -> 0% of each run, Pallas kernels for 30% -> 14%
where the time goes in v7:
time: 579 us; the launch traced here: 571 us
  Pallas kernels  540 us (93%)
  local copies, waits for them, and re-layouts  15.1 us (3%)
  between operations  14.3 us (2%)
    pallas_call x1, Pallas kernels, middle(): pl.pallas_call(partial(middle_kernel, size, rounds), out_shape=[jax.Shape...  268 us
    pallas_call x1, Pallas kernels, front(): pl.pallas_call(partial(front_kernel, size, groups, rounds), out_shape=[ja...  99.8 us
    pallas_call x1, Pallas kernels, last(): pl.pallas_call(partial(last_kernel, size, groups, rounds, len(grads), mix...  91.8 us
    pallas_call x1, Pallas kernels, scan_backward(): pl.pallas_call(partial(scan_back_kernel, size, line, rounds, len(grads)),...  80.4 us
    unnamed x28, local copies, waits for them, and re-layouts  11.7 us
  transfers between devices with their start and end apart: 1, of which 0 were waited for; matrix products, arithmetic and copies ran while one was open for 0% of the time, Pallas kernels for 14%

profile of v7, /device:TPU:0, one launch (start us, length us, event | category | flops | bytes accessed | tf_op | source)
XLA Modules:
  0.0 570.9 jit_solution(11434358883721189402)
XLA Ops:
  7.2 0.0 reduce-scatter.2.cloned.1.call-start
  7.2 1.3 reduce-window.9
  8.6 99.8 %front.1 = (bf16[4,4,64,2048]{3,2,1,0:T(8,128)(2,1)}, f32[1024,512]{1,0:T(8,128)}, f32[1024,512]{1,0:T(8,128)}, f32[1024,512]{1,0:T(8,128)}, f32[1024,512]{1,0:T...) custom-call(s32[7]{0:T(128)} %bitcast.37, ...), custom_call_target="tpu_custom_call" | custom-call | flops 8589934592 | bytes 37748736 | tf_op jit(solution)/shard_map/front/pallas_call | solution.py:740
  108.4 268.1 %middle.1 = (f32[4,64,2048]{2,1,0:T(8,128)}, f32[4,64,2048]{2,1,0:T(8,128)}, bf16[4,4,64,2048]{3,2,1,0:T(8,128)(2,1)}, f32[4,4,64,512]{3,2,1,0:T(8,128)}, f32[1,...) custom-call(bf16[4,4,64,512]{3,2,1,0:T(8,128)(2,1)} %bitcast.53, ...), custom_call_target="tpu_custom_call" | custom-call | flops 57445187584 | bytes 58720256 | tf_op jit(solution)/shard_map/middle/pallas_call | solution.py:1284
  376.5 0.0 reduce-scatter.2.cloned.1.call-update
  376.5 80.4 %scan_backward.1 = (bf16[1024,512]{1,0:T(8,128)(2,1)}, bf16[1024,512]{1,0:T(8,128)(2,1)}, bf16[1024,512]{1,0:T(8,128)(2,1)}, bf16[1024,512]{1,0:T(8,128)(2,1)}, ...) custom-call(s32[7]{0:T(128)} %bitcast.38, ...), custom_call_target="tpu_custom_call" | custom-call | flops 8589934592 | bytes 41943040 | tf_op jit(solution)/shard_map/scan_backward/pallas_call | solution.py:989
  456.9 0.0 reduce-scatter.2.cloned.1.call-done.refs_13_
  457.0 91.8 %last.1 = (f32[4,64,2048]{2,1,0:T(8,128)}, f32[40,128]{1,0:T(8,128)}, bf16[256,2048]{1,0:T(8,128)(2,1)}, f32[1408,256]{1,0:T(8,128)}, f32[512,256]{1,0:T(8,128)}...) custom-call(bf16[4,4,64,512]{3,2,1,0:T(8,128)(2,1)} %bitcast.44, ...), custom_call_target="tpu_custom_call" | custom-call | flops 17179869184 | bytes 58720256 | tf_op jit(solution)/shard_map/last/pallas_call | solution.py:1548
  548.7 0.0 copy-start
  548.7 0.8 fusion
  549.6 0.7 slice_bitcast_fusion
  550.3 0.6 dynamic_slice.12
  550.9 0.6 dynamic_slice.15
  551.5 0.7 constant_dynamic-slice_fusion
  552.1 2.3 copy.39
  554.4 0.0 copy-done
  554.4 0.0 copy-start.8
  554.4 0.0 copy-start.7
  554.4 1.3 copy.40
  555.7 0.1 copy-done.8
  555.8 0.0 copy-start.6
  555.8 0.0 copy-start.5
  555.8 0.0 copy-start.4
  555.8 0.8 copy.41
  556.6 0.0 copy-done.7
  556.6 0.0 copy-start.2
  556.6 0.8 copy.42
  557.4 0.0 copy-done.6
  557.4 0.8 copy.43
  558.2 0.0 copy-done.5
  558.2 0.8 copy.44
  559.0 0.0 copy-done.4
  559.0 0.0 copy-start.1
  559.0 0.8 copy.45
  559.8 0.0 copy-done.2
  559.8 1.1 copy.46
  560.9 0.0 copy-done.1
  560.9 0.0 copy-start.3
  560.9 1.1 copy.47
  562.0 0.8 copy-done.3
  562.8 1.1 copy.48
Async XLA Ops:
  7.2 449.8 %reduce-scatter.2.cloned.1.call-start = ((), (), s32[]{:S(2)}) async-start(), calls=%async_computation.1 | async-start | bytes 5242880 | tf_op jit(solution)/shard_map/reduce_scatter | solution.py:1622
  548.7 5.7 copy-start
  554.4 1.4 copy-start.8
  554.4 2.2 copy-start.7
  555.8 1.6 copy-start.6
  555.8 2.4 copy-start.5
  555.8 3.2 copy-start.4
  556.6 3.2 copy-start.2
  559.0 1.9 copy-start.1
  560.9 1.9 copy-start.3
Sparse Core Ops, SparseCore 0:
  376.6 80.1 reduce-scatter.1

commit v8 on v7

--- a/solution.py
+++ b/solution.py
@@ -1590,6 +1590,58 @@
     return (outs[0].reshape(rows, d), sides[:lines], sides[lines : 2 * lines], sides[2 * lines :]) + tuple(outs[2:])
 
 
+def results_kernel(count, places_ref, first_ref, second_ref, small_ref, *refs):
+    ins, outs = refs[:count], refs[count : 2 * count]
+    first_out, second_out, bound_out, gain_out, *held, sems = refs[2 * count :]
+    loads = [pltpu.make_async_copy(a, b, sems.at[0, k]) for k, (a, b) in enumerate(zip(ins, held))]
+    stores = [pltpu.make_async_copy(a, b, sems.at[1, k]) for k, (a, b) in enumerate(zip(held, outs))]
+    for load in loads:
+        load.start()
+
+    def share(rows, at, width):
+        picked = rows[:, :width]
+        for k in range(1, WIDTH // width):
+            picked = jnp.where(at == k, rows[:, k * width : (k + 1) * width], picked)
+        return picked
+
+    here, place = places_ref[0], places_ref[1]
+    each = first_out.shape[1]
+    per = WIDTH // each
+    lines = lax.broadcasted_iota(jnp.int32, first_ref.shape, 0)
+    for source, target in ((first_ref, first_out), (second_ref, second_out)):
+        line = jnp.sum(jnp.where(lines == place // per, source[...], 0.0), axis=0, keepdims=True)
+        target[...] = share(line, place % per, each)
+    heads, wide = bound_out.shape
+    bound_out[...] = share(small_ref[:heads, :], here, wide)
+    gain_out[...] = share(small_ref[heads:, :], here, wide)
+    for load, store in zip(loads, stores):
+        load.wait()
+        store.start()
+    for store in stores:
+        store.wait()
+
+
+def results(groups, size, first, second, small, arrays):
+    here = lax.axis_index("seq")
+    places = jnp.stack([here, here * size + lax.axis_index("tp")]).astype(jnp.int32)
+    each, heads = first.size // (groups * size), small.shape[0] // 2
+    spec, far = pl.BlockSpec(memory_space=VM), pl.BlockSpec(memory_space=pl.ANY)
+    outs = pl.pallas_call(
+        partial(results_kernel, len(arrays)),
+        out_shape=[jax.ShapeDtypeStruct(part.shape, part.dtype) for part in arrays]
+        + [jax.ShapeDtypeStruct((1, each), f32)] * 2
+        + [jax.ShapeDtypeStruct((heads, WIDTH // groups), f32)] * 2,
+        in_specs=[pl.BlockSpec(memory_space=pltpu.SMEM)] + [spec] * 3 + [far] * len(arrays),
+        out_specs=[far] * len(arrays) + [spec] * 4,
+        scratch_shapes=[VM(part.shape, part.dtype) for part in arrays] + [DMA((2, len(arrays)))],
+        compiler_params=pltpu.CompilerParams(vmem_limit_bytes=60 * MIB),
+        cost_estimate=pl.CostEstimate(flops=0, bytes_accessed=20 * MIB, transcendentals=0),
+        name="results",
+    )(places, first, second, small, *arrays)
+    copied, (first, second, bound, gain) = outs[: len(arrays)], outs[len(arrays) :]
+    return first.reshape(each), second.reshape(each), bound, gain, copied
+
+
 def per_device(
     size,
     groups,
@@ -1669,16 +1721,12 @@
         others,
         [True, True] + [False] * 4,
     )
-    down_grad, out_grad, query_grad, forget_grad, input_grad, swish_grad = sums
-    heads = bound_logit.shape[0]
-    here = lax.axis_index("seq")
-    place = here * size + lax.axis_index("tp")
-    each = d // (groups * size)
-    wide = WIDTH // groups
-    first_grad = lax.dynamic_slice_in_dim(first_sum.reshape(-1), place * each, each)
-    second_grad = lax.dynamic_slice_in_dim(second_sum.reshape(-1), place * each, each)
-    bound_grad = lax.dynamic_slice_in_dim(small_sum[:heads], here * wide, wide, axis=1)
-    head_grad = lax.dynamic_slice_in_dim(small_sum[heads:], here * wide, wide, axis=1)
+    arrays = [output, tokens_grad, gate_grad, up_grad, *sums]
+    first_grad, second_grad, bound_grad, head_grad, copied = results(
+        groups, size, first_sum, second_sum, small_sum, arrays
+    )
+    output, tokens_grad, gate_grad, up_grad, down_grad, out_grad, *mixes = copied
+    query_grad, forget_grad, input_grad, swish_grad = mixes
     return (
         output,
         tokens_grad,

time: 579 us -> 576 us (level)
  local copies, waits for them, and re-layouts: 15.1 us -> 2.6 us
  Pallas kernels: 540 us -> 548 us
    unnamed x28 -> x0, local copies, waits for them, and re-layouts: 11.7 us -> none
    pallas_call x0 -> x1, Pallas kernels: none -> 8.67 us  [results(): pl.pallas_call(partial(results_kernel, len(arrays)), out_shape=[jax.Shape...]
where the time goes in v8:
time: 576 us; the launch traced here: 567 us
  Pallas kernels  548 us (95%)
  between operations  14.3 us (2%)
    pallas_call x1, Pallas kernels, middle(): pl.pallas_call(partial(middle_kernel, size, rounds), out_shape=[jax.Shape...  268 us
    pallas_call x1, Pallas kernels, front(): pl.pallas_call(partial(front_kernel, size, groups, rounds), out_shape=[ja...  99.7 us
    pallas_call x1, Pallas kernels, last(): pl.pallas_call(partial(last_kernel, size, groups, rounds, len(grads), mix...  91.6 us
    pallas_call x1, Pallas kernels, scan_backward(): pl.pallas_call(partial(scan_back_kernel, size, line, rounds, len(grads)),...  80.4 us
  transfers between devices with their start and end apart: 1, of which 0 were waited for; matrix products, arithmetic and copies ran while one was open for 0% of the time, Pallas kernels for 14%

profile of v8, /device:TPU:0, one launch (start us, length us, event | category | flops | bytes accessed | tf_op | source)
XLA Modules:
  0.0 567.3 jit_solution(6827605379721681172)
XLA Ops:
  7.2 0.0 reduce-scatter.2.cloned.1.call-start
  7.2 1.3 reduce-window.9
  8.6 99.7 %front.1 = (bf16[4,4,64,2048]{3,2,1,0:T(8,128)(2,1)}, f32[1024,512]{1,0:T(8,128)}, f32[1024,512]{1,0:T(8,128)}, f32[1024,512]{1,0:T(8,128)}, f32[1024,512]{1,0:T...) custom-call(s32[7]{0:T(128)} %bitcast.37, ...), custom_call_target="tpu_custom_call" | custom-call | flops 8589934592 | bytes 37748736 | tf_op jit(solution)/shard_map/front/pallas_call | solution.py:740
  108.3 268.1 %middle.1 = (f32[4,64,2048]{2,1,0:T(8,128)}, f32[4,64,2048]{2,1,0:T(8,128)}, bf16[4,4,64,2048]{3,2,1,0:T(8,128)(2,1)}, f32[4,4,64,512]{3,2,1,0:T(8,128)}, f32[1,...) custom-call(bf16[4,4,64,512]{3,2,1,0:T(8,128)(2,1)} %bitcast.55, ...), custom_call_target="tpu_custom_call" | custom-call | flops 57445187584 | bytes 58720256 | tf_op jit(solution)/shard_map/middle/pallas_call | solution.py:1284
  376.4 0.0 reduce-scatter.2.cloned.1.call-update
  376.4 0.6 pad_add_fusion.places_ref
  377.0 80.4 %scan_backward.1 = (bf16[1024,512]{1,0:T(8,128)(2,1)}, bf16[1024,512]{1,0:T(8,128)(2,1)}, bf16[1024,512]{1,0:T(8,128)(2,1)}, bf16[1024,512]{1,0:T(8,128)(2,1)}, ...) custom-call(s32[7]{0:T(128)} %bitcast.38, ...), custom_call_target="tpu_custom_call" | custom-call | flops 8589934592 | bytes 41943040 | tf_op jit(solution)/shard_map/scan_backward/pallas_call | solution.py:989
  457.4 0.0 reduce-scatter.2.cloned.1.call-done.refs_13_
  457.4 91.6 %last.1 = (f32[4,64,2048]{2,1,0:T(8,128)}, f32[40,128]{1,0:T(8,128)}, bf16[256,2048]{1,0:T(8,128)(2,1)}, f32[1408,256]{1,0:T(8,128)}, f32[512,256]{1,0:T(8,128)}...) custom-call(bf16[4,4,64,512]{3,2,1,0:T(8,128)(2,1)} %bitcast.44, ...), custom_call_target="tpu_custom_call" | custom-call | flops 17179869184 | bytes 58720256 | tf_op jit(solution)/shard_map/last/pallas_call | solution.py:1548
  549.0 1.3 fusion
  550.3 1.3 slice.11.small_ref
  551.6 8.7 %results.1 = (bf16[256,2048]{1,0:T(8,128)(2,1)}, f32[256,2048]{1,0:T(8,128)}, f32[256,1408]{1,0:T(8,128)}, f32[256,1408]{1,0:T(8,128)}, f32[1408,256]{1,0:T(8,12...) custom-call(s32[2]{0:T(128)} %pad_add_fusion.places_ref, ...), custom_call_target="tpu_custom_call" | custom-call | bytes 20971520 | tf_op jit(solution)/shard_map/results/pallas_call | solution.py:1629
Async XLA Ops:
  7.2 450.2 %reduce-scatter.2.cloned.1.call-start = ((), (), s32[]{:S(2)}) async-start(), calls=%async_computation.1 | async-start | bytes 5242880 | tf_op jit(solution)/shard_map/reduce_scatter | solution.py:1674
Sparse Core Ops, SparseCore 0:
  376.5 80.0 reduce-scatter.1

commit v9 on v8

--- a/solution.py
+++ b/solution.py
@@ -441,21 +441,28 @@
     return take
 
 
-def document(rows, ends_ref):
-    total = jnp.where(rows >= ends_ref[0], 1, 0)
-    for k in range(1, ends_ref.shape[0]):
-        total = total + jnp.where(rows >= ends_ref[k], 1, 0)
+def running_ends(lengths_ref):
+    ends = [lengths_ref[0]]
+    for k in range(1, lengths_ref.shape[0]):
+        ends.append(ends[-1] + lengths_ref[k])
+    return ends
+
+
+def document(rows, ends):
+    total = jnp.where(rows >= ends[0], 1, 0)
+    for end in ends[1:]:
+        total = total + jnp.where(rows >= end, 1, 0)
     return total
 
 
-def block_masks(first, ends_ref):
+def block_masks(first, ends):
     shape = (WIDTH, WIDTH)
     down = lax.broadcasted_iota(jnp.int32, shape, 0)
     along = lax.broadcasted_iota(jnp.int32, shape, 1)
-    docs = document(first + down, ends_ref)
-    same = (docs == document(first + along, ends_ref)) & (down >= along)
-    before = jnp.where(first > 0, document(first - 1, ends_ref), -1)
-    final = document(first + WIDTH - 1, ends_ref)
+    docs = document(first + down, ends)
+    same = (docs == document(first + along, ends)) & (down >= along)
+    before = jnp.where(first > 0, document(first - 1, ends), -1)
+    final = document(first + WIDTH - 1, ends)
     carry = jnp.where(docs == before, 1.0, 0.0)
     tail = jnp.where(docs == final, 1.0, 0.0)
     keep = jnp.where(final == before, 1.0, 0.0)
@@ -539,7 +546,8 @@
 
 def front_kernel(size, groups, rounds, *refs):
     take = taker(refs)
-    ends_ref, x_ref, norm_gain_ref, bound_ref, gain_ref, cot_in, *loaded = take(10)
+    lengths_ref, x_ref, norm_gain_ref, bound_ref, gain_ref, cot_in, *loaded = take(10)
+    ends = running_ends(lengths_ref)
     a_out, q_out, f_out, i_out, s_out, cot_out, o_ref, u_ref, starts_ref = take(9)
     *weights, a_ref, q_ref, f_ref, i_ref, s_ref, cot_ref = take(10)
     qd_ref, kd_ref, qe_ref, adds, decays = take(5)
@@ -592,7 +600,7 @@
 
     def block(b):
         r = pl.ds(pl.multiple_of(b * WIDTH, WIDTH), WIDTH)
-        same, carry, tail, keep = block_masks(base + b * WIDTH, ends_ref)
+        same, carry, tail, keep = block_masks(base + b * WIDTH, ends)
         for h in range(heads):
             cols = slice(h * WIDTH, (h + 1) * WIDTH)
             q = q_ref[r, cols]
@@ -608,7 +616,7 @@
 
     def near_part(b):
         r = pl.ds(pl.multiple_of(b * WIDTH, WIDTH), WIDTH)
-        same, carry, tail, keep = block_masks(base + b * WIDTH, ends_ref)
+        same, carry, tail, keep = block_masks(base + b * WIDTH, ends)
         for h in range(heads):
             cols = slice(h * WIDTH, (h + 1) * WIDTH)
             scores = jnp.where(same, mul(qd_ref[r, cols], kd_ref[r, cols], NT), 0.0).astype(bf16)
@@ -696,7 +704,7 @@
     def _(b):
         r = pl.ds(pl.multiple_of(b * WIDTH, WIDTH), WIDTH)
         places = base + b * WIDTH + lax.broadcasted_iota(jnp.int32, (WIDTH, WIDTH), 0)
-        valid = jnp.where(places < ends_ref[ends_ref.shape[0] - 1], 1.0, 0.0)
+        valid = jnp.where(places < ends[-1], 1.0, 0.0)
         for h in range(heads):
             cols = slice(h * WIDTH, (h + 1) * WIDTH)
             low = state[h].astype(bf16)
@@ -777,7 +785,8 @@
 
 def scan_back_kernel(size, line, rounds, count, *refs):
     take = taker(refs)
-    ends_ref, bound_ref, gain_ref, norm_gain_ref, *loaded = take(16)
+    lengths_ref, bound_ref, gain_ref, norm_gain_ref, *loaded = take(16)
+    ends = running_ends(lengths_ref)
     grads = take(count)
     *back_outs, small_ref, first_ref, part_out = take(7)
     grad_outs = take(count)
@@ -818,9 +827,9 @@
 
         b = blocks - 1 - back
         r = pl.ds(pl.multiple_of(b * WIDTH, WIDTH), WIDTH)
-        same, carry, tail, keep = block_masks(base + b * WIDTH, ends_ref)
+        same, carry, tail, keep = block_masks(base + b * WIDTH, ends)
         places = base + b * WIDTH + lax.broadcasted_iota(jnp.int32, (WIDTH, WIDTH), 0)
-        valid = jnp.where(places < ends_ref[ends_ref.shape[0] - 1], 1.0, 0.0)
+        valid = jnp.where(places < ends[-1], 1.0, 0.0)
         for h in range(heads):
             cols = slice(h * WIDTH, (h + 1) * WIDTH)
             o, s, ub, gain = o_ref[r, cols], s_ref[r, cols], ub_ref[r, cols], gain_ref[:, cols]
@@ -871,7 +880,7 @@
                 each.relay()
         b = blocks - 1 - back
         r = pl.ds(pl.multiple_of(b * WIDTH, WIDTH), WIDTH)
-        same, carry, tail, keep = block_masks(base + b * WIDTH, ends_ref)
+        same, carry, tail, keep = block_masks(base + b * WIDTH, ends)
         shape = (WIDTH, WIDTH)
         down, along = lax.broadcasted_iota(jnp.int32, shape, 0), lax.broadcasted_iota(jnp.int32, shape, 1)
         from_here = jnp.where(along >= down, 1.0, 0.0).astype(bf16)
@@ -1586,11 +1595,10 @@
         down,
         *[in_pairs(grad) for grad in grads],
     )
-    sides = outs[1]
-    return (outs[0].reshape(rows, d), sides[:lines], sides[lines : 2 * lines], sides[2 * lines :]) + tuple(outs[2:])
-
-
-def results_kernel(count, places_ref, first_ref, second_ref, small_ref, *refs):
+    return (outs[0].reshape(rows, d),) + tuple(outs[1:])
+
+
+def results_kernel(count, size, small_ref, *refs):
     ins, outs = refs[:count], refs[count : 2 * count]
     first_out, second_out, bound_out, gain_out, *held, sems = refs[2 * count :]
     loads = [pltpu.make_async_copy(a, b, sems.at[0, k]) for k, (a, b) in enumerate(zip(ins, held))]
@@ -1604,16 +1612,18 @@
             picked = jnp.where(at == k, rows[:, k * width : (k + 1) * width], picked)
         return picked
 
-    here, place = places_ref[0], places_ref[1]
+    here = lax.axis_index("seq")
+    place = here * size + lax.axis_index("tp")
     each = first_out.shape[1]
     per = WIDTH // each
-    lines = lax.broadcasted_iota(jnp.int32, first_ref.shape, 0)
-    for source, target in ((first_ref, first_out), (second_ref, second_out)):
-        line = jnp.sum(jnp.where(lines == place // per, source[...], 0.0), axis=0, keepdims=True)
+    heads, wide = bound_out.shape
+    lines = (small_ref.shape[0] - 2 * heads) // 2
+    at = lax.broadcasted_iota(jnp.int32, (lines, WIDTH), 0)
+    for source, target in ((small_ref[:lines], second_out), (small_ref[lines : 2 * lines], first_out)):
+        line = jnp.sum(jnp.where(at == place // per, source, 0.0), axis=0, keepdims=True)
         target[...] = share(line, place % per, each)
-    heads, wide = bound_out.shape
-    bound_out[...] = share(small_ref[:heads, :], here, wide)
-    gain_out[...] = share(small_ref[heads:, :], here, wide)
+    bound_out[...] = share(small_ref[2 * lines : 2 * lines + heads, :], here, wide)
+    gain_out[...] = share(small_ref[2 * lines + heads :, :], here, wide)
     for load, store in zip(loads, stores):
         load.wait()
         store.start()
@@ -1621,23 +1631,21 @@
         store.wait()
 
 
-def results(groups, size, first, second, small, arrays):
-    here = lax.axis_index("seq")
-    places = jnp.stack([here, here * size + lax.axis_index("tp")]).astype(jnp.int32)
-    each, heads = first.size // (groups * size), small.shape[0] // 2
+def results(groups, size, small, heads, arrays):
+    each = (small.shape[0] - 2 * heads) // 2 * WIDTH // (groups * size)
     spec, far = pl.BlockSpec(memory_space=VM), pl.BlockSpec(memory_space=pl.ANY)
     outs = pl.pallas_call(
-        partial(results_kernel, len(arrays)),
+        partial(results_kernel, len(arrays), size),
         out_shape=[jax.ShapeDtypeStruct(part.shape, part.dtype) for part in arrays]
         + [jax.ShapeDtypeStruct((1, each), f32)] * 2
         + [jax.ShapeDtypeStruct((heads, WIDTH // groups), f32)] * 2,
-        in_specs=[pl.BlockSpec(memory_space=pltpu.SMEM)] + [spec] * 3 + [far] * len(arrays),
+        in_specs=[spec] + [far] * len(arrays),
         out_specs=[far] * len(arrays) + [spec] * 4,
         scratch_shapes=[VM(part.shape, part.dtype) for part in arrays] + [DMA((2, len(arrays)))],
         compiler_params=pltpu.CompilerParams(vmem_limit_bytes=60 * MIB),
         cost_estimate=pl.CostEstimate(flops=0, bytes_accessed=20 * MIB, transcendentals=0),
         name="results",
-    )(places, first, second, small, *arrays)
+    )(small, *arrays)
     copied, (first, second, bound, gain) = outs[: len(arrays)], outs[len(arrays) :]
     return first.reshape(each), second.reshape(each), bound, gain, copied
 
@@ -1662,7 +1670,7 @@
     down_weight,
 ):
     weights = (query_weight, forget_weight, input_weight, swish_weight)
-    ends = jnp.cumsum(lengths).astype(jnp.int32)
+    ends = lengths.astype(jnp.int32)
     bound, head_gain = bound_logit.reshape(1, -1), group_gain.reshape(1, -1)
     a, q, f, i, s, cot_some, o, u, starts = front(
         size, groups, ROUNDS, tokens, cotangent, first_gain, weights, ends, bound, head_gain
@@ -1703,7 +1711,7 @@
     back_rows = (dq, df, di, ds)
     here_too = groups == 8
     others = [downs, outs] + ([] if here_too else [grad_of(a, part) for part in back_rows])
-    tokens_grad, second_sum, first_sum, small_sum, output, *sums = last(
+    tokens_grad, small_sum, output, *sums = last(
         size,
         groups,
         ROUNDS,
@@ -1723,7 +1731,7 @@
     )
     arrays = [output, tokens_grad, gate_grad, up_grad, *sums]
     first_grad, second_grad, bound_grad, head_grad, copied = results(
-        groups, size, first_sum, second_sum, small_sum, arrays
+        groups, size, small_sum, bound_logit.shape[0], arrays
     )
     output, tokens_grad, gate_grad, up_grad, down_grad, out_grad, *mixes = copied
     query_grad, forget_grad, input_grad, swish_grad = mixes

time: 576 us -> 571 us (level)
  no operation moved by 1% of the time
where the time goes in v9:
time: 571 us; the launch traced here: 563 us
  Pallas kernels  548 us (96%)
  between operations  14.3 us (3%)
    pallas_call x1, Pallas kernels, middle(): pl.pallas_call(partial(middle_kernel, size, rounds), out_shape=[jax.Shape...  268 us
    pallas_call x1, Pallas kernels, front(): pl.pallas_call(partial(front_kernel, size, groups, rounds), out_shape=[ja...  99.8 us
    pallas_call x1, Pallas kernels, last(): pl.pallas_call(partial(last_kernel, size, groups, rounds, len(grads), mix...  91.5 us
    pallas_call x1, Pallas kernels, scan_backward(): pl.pallas_call(partial(scan_back_kernel, size, line, rounds, len(grads)),...  80.4 us
  transfers between devices with their start and end apart: 1, of which 0 were waited for; matrix products, arithmetic and copies ran while one was open for 0% of the time, Pallas kernels for 14%

profile of v9, /device:TPU:0, one launch (start us, length us, event | category | flops | bytes accessed | tf_op | source)
XLA Modules:
  0.0 562.7 jit_solution(8479162837321538865)
XLA Ops:
  7.2 0.0 reduce-scatter.2.cloned.1.call-start
  7.2 99.8 %front.1 = (bf16[4,4,64,2048]{3,2,1,0:T(8,128)(2,1)}, f32[1024,512]{1,0:T(8,128)}, f32[1024,512]{1,0:T(8,128)}, f32[1024,512]{1,0:T(8,128)}, f32[1024,512]{1,0:T...) custom-call(s32[7]{0:T(128)} %refs_0_.3, ...), custom_call_target="tpu_custom_call" | custom-call | flops 8589934592 | bytes 37748736 | tf_op jit(solution)/shard_map/front/pallas_call | solution.py:748
  107.0 268.1 %middle.1 = (f32[4,64,2048]{2,1,0:T(8,128)}, f32[4,64,2048]{2,1,0:T(8,128)}, bf16[4,4,64,2048]{3,2,1,0:T(8,128)(2,1)}, f32[4,4,64,512]{3,2,1,0:T(8,128)}, f32[1,...) custom-call(bf16[4,4,64,512]{3,2,1,0:T(8,128)(2,1)} %bitcast.48, ...), custom_call_target="tpu_custom_call" | custom-call | flops 57445187584 | bytes 58720256 | tf_op jit(solution)/shard_map/middle/pallas_call | solution.py:1293
  375.1 0.0 reduce-scatter.2.cloned.1.call-update
  375.1 80.4 %scan_backward.1 = (bf16[1024,512]{1,0:T(8,128)(2,1)}, bf16[1024,512]{1,0:T(8,128)(2,1)}, bf16[1024,512]{1,0:T(8,128)(2,1)}, bf16[1024,512]{1,0:T(8,128)(2,1)}, ...) custom-call(s32[7]{0:T(128)} %refs_0_.3, ...), custom_call_target="tpu_custom_call" | custom-call | flops 8589934592 | bytes 41943040 | tf_op jit(solution)/shard_map/scan_backward/pallas_call | solution.py:998
  455.6 0.0 reduce-scatter.2.cloned.1.call-done.refs_13_
  455.6 91.5 %last.1 = (f32[4,64,2048]{2,1,0:T(8,128)}, f32[40,128]{1,0:T(8,128)}, bf16[256,2048]{1,0:T(8,128)(2,1)}, f32[1408,256]{1,0:T(8,128)}, f32[512,256]{1,0:T(8,128)}...) custom-call(bf16[4,4,64,512]{3,2,1,0:T(8,128)(2,1)} %bitcast.38, ...), custom_call_target="tpu_custom_call" | custom-call | flops 17179869184 | bytes 58720256 | tf_op jit(solution)/shard_map/last/pallas_call | solution.py:1557
  547.1 8.6 %results.1 = (bf16[256,2048]{1,0:T(8,128)(2,1)}, f32[256,2048]{1,0:T(8,128)}, f32[256,1408]{1,0:T(8,128)}, f32[256,1408]{1,0:T(8,128)}, f32[1408,256]{1,0:T(8,12...) custom-call(f32[40,128]{1,0:T(8,128)} %get-tuple-element.93.small_re, ...), custom_call_target="tpu_custom_call" | custom-call | bytes 20971520 | tf_op jit(solution)/shard_map/results/pallas_call | solution.py:1637
Async XLA Ops:
  7.2 448.4 %reduce-scatter.2.cloned.1.call-start = ((), (), s32[]{:S(2)}) async-start(), calls=%async_computation.1 | async-start | bytes 5242880 | tf_op jit(solution)/shard_map/reduce_scatter | solution.py:1682
Sparse Core Ops, SparseCore 0:
  375.3 80.0 reduce-scatter.1

commit v10 on v9

--- a/solution.py
+++ b/solution.py
@@ -1399,7 +1399,7 @@
 
 def last_kernel(size, groups, rounds, count, mixed, *refs):
     take = taker(refs)
-    backs = take(4)
+    backs_in = take(4)
     x_ref, gain_ref, second_ref, small_ref, first_ref, back_in, a_in, part_in, res_in, down_in = take(10)
     grads = take(count)
     tokens_far, small_out, output_ref = take(3)
@@ -1407,7 +1407,7 @@
     part, land, total, s_send, s_recv = take(5)
     small_seq, gains_tp, sides = take(3), take(3), take(1)[0]
     nears = take(4 if mixed else 0)
-    a_ref, tokens_out, res_ref, down_ref, load_sems, store_sems = take(6)
+    a_ref, *backs, tokens_out, res_ref, down_ref, load_sems, store_sems = take(10)
     sums = group_sums(groups, grads + nears, grad_outs, take)
     early, late = sums[:2], sums[2:]
 
@@ -1430,6 +1430,11 @@
     for j in range(rounds):
         part_load(j).start()
     a_load.start()
+    backs_loads = [
+        local(source, target, load_sems.at[4 + rounds + k]) for k, (source, target) in enumerate(zip(backs_in, backs))
+    ]
+    for load in backs_loads:
+        load.start()
     back_load.start()
     output_loads = [
         local(source, target, load_sems.at[2 + rounds + k])
@@ -1497,6 +1502,8 @@
     for each in early:
         each.middle()
     a_load.wait()
+    for load in backs_loads:
+        load.wait()
     steps(0, 1, 2)
     back_load.wait()
     if mixed:
@@ -1562,7 +1569,9 @@
             jax.ShapeDtypeStruct((rows, d), bf16),
         ]
         + sum_shapes(shapes, turned),
-        in_specs=[spec] * 9 + [pl.BlockSpec(memory_space=pl.ANY)] * (5 + len(grads)),
+        in_specs=[pl.BlockSpec(memory_space=pl.ANY)] * 4
+        + [spec] * 5
+        + [pl.BlockSpec(memory_space=pl.ANY)] * (5 + len(grads)),
         out_specs=[pl.BlockSpec(memory_space=pl.ANY)] + [spec] * (2 + len(shapes)),
         scratch_shapes=[
             VM((rounds, size, m, d), bf16),
@@ -1576,7 +1585,8 @@
         + [VM((2 * lines, WIDTH), f32)]
         + ([VM((groups // 2, d // groups, c), bf16)] * 4 if mixed else [])
         + [VM(shape + (d,), bf16)]
-        + [VM((rounds, m, d), f32), VM((rows, d), f32), VM((rows, d), bf16), DMA((4 + rounds,)), DMA((rounds,))]
+        + [VM(shape + (c,), bf16)] * 4
+        + [VM((rounds, m, d), f32), VM((rows, d), f32), VM((rows, d), bf16), DMA((8 + rounds,)), DMA((rounds,))]
         + group_sums_scratch(shapes),
         compiler_params=pltpu.CompilerParams(collective_id=4, has_side_effects=True, vmem_limit_bytes=63 * MIB),
         cost_estimate=pl.CostEstimate(flops=16 * size * rows * d * c, bytes_accessed=56 * MIB, transcendentals=0),

time: 571 us -> 570 us (level)
  no operation moved by 1% of the time
where the time goes in v10:
time: 570 us; the launch traced here: 561 us
  Pallas kernels  547 us (96%)
  between operations  14.3 us (3%)
    pallas_call x1, Pallas kernels, middle(): pl.pallas_call(partial(middle_kernel, size, rounds), out_shape=[jax.Shape...  268 us
    pallas_call x1, Pallas kernels, front(): pl.pallas_call(partial(front_kernel, size, groups, rounds), out_shape=[ja...  99.8 us
    pallas_call x1, Pallas kernels, last(): pl.pallas_call(partial(last_kernel, size, groups, rounds, len(grads), mix...  90.2 us
    pallas_call x1, Pallas kernels, scan_backward(): pl.pallas_call(partial(scan_back_kernel, size, line, rounds, len(grads)),...  80.4 us
  transfers between devices with their start and end apart: 1, of which 0 were waited for; matrix products, arithmetic and copies ran while one was open for 0% of the time, Pallas kernels for 14%

profile of v10, /device:TPU:0, one launch (start us, length us, event | category | flops | bytes accessed | tf_op | source)
XLA Modules:
  0.0 561.5 jit_solution(5891010310613644153)
XLA Ops:
  7.2 0.0 reduce-scatter.2.cloned.1.call-start
  7.2 99.8 %front.1 = (bf16[4,4,64,2048]{3,2,1,0:T(8,128)(2,1)}, f32[1024,512]{1,0:T(8,128)}, f32[1024,512]{1,0:T(8,128)}, f32[1024,512]{1,0:T(8,128)}, f32[1024,512]{1,0:T...) custom-call(s32[7]{0:T(128)} %refs_0_.3, ...), custom_call_target="tpu_custom_call" | custom-call | flops 8589934592 | bytes 37748736 | tf_op jit(solution)/shard_map/front/pallas_call | solution.py:748
  107.0 268.1 %middle.1 = (f32[4,64,2048]{2,1,0:T(8,128)}, f32[4,64,2048]{2,1,0:T(8,128)}, bf16[4,4,64,2048]{3,2,1,0:T(8,128)(2,1)}, f32[4,4,64,512]{3,2,1,0:T(8,128)}, f32[1,...) custom-call(bf16[4,4,64,512]{3,2,1,0:T(8,128)(2,1)} %bitcast.48, ...), custom_call_target="tpu_custom_call" | custom-call | flops 57445187584 | bytes 58720256 | tf_op jit(solution)/shard_map/middle/pallas_call | solution.py:1293
  375.1 0.0 reduce-scatter.2.cloned.1.call-update
  375.1 80.4 %scan_backward.1 = (bf16[1024,512]{1,0:T(8,128)(2,1)}, bf16[1024,512]{1,0:T(8,128)(2,1)}, bf16[1024,512]{1,0:T(8,128)(2,1)}, bf16[1024,512]{1,0:T(8,128)(2,1)}, ...) custom-call(s32[7]{0:T(128)} %refs_0_.3, ...), custom_call_target="tpu_custom_call" | custom-call | flops 8589934592 | bytes 41943040 | tf_op jit(solution)/shard_map/scan_backward/pallas_call | solution.py:998
  455.6 0.0 reduce-scatter.2.cloned.1.call-done.refs_13_
  455.6 90.2 %last.1 = (f32[4,64,2048]{2,1,0:T(8,128)}, f32[40,128]{1,0:T(8,128)}, bf16[256,2048]{1,0:T(8,128)(2,1)}, f32[1408,256]{1,0:T(8,128)}, f32[512,256]{1,0:T(8,128)}...) custom-call(bf16[4,4,64,512]{3,2,1,0:T(8,128)(2,1)} %bitcast.38, ...), custom_call_target="tpu_custom_call" | custom-call | flops 17179869184 | bytes 58720256 | tf_op jit(solution)/shard_map/last/pallas_call | solution.py:1564
  545.8 8.6 %results.1 = (bf16[256,2048]{1,0:T(8,128)(2,1)}, f32[256,2048]{1,0:T(8,128)}, f32[256,1408]{1,0:T(8,128)}, f32[256,1408]{1,0:T(8,128)}, f32[1408,256]{1,0:T(8,12...) custom-call(f32[40,128]{1,0:T(8,128)} %get-tuple-element.93.small_re, ...), custom_call_target="tpu_custom_call" | custom-call | bytes 20971520 | tf_op jit(solution)/shard_map/results/pallas_call | solution.py:1647
Async XLA Ops:
  7.2 448.4 %reduce-scatter.2.cloned.1.call-start = ((), (), s32[]{:S(2)}) async-start(), calls=%async_computation.1 | async-start | bytes 5242880 | tf_op jit(solution)/shard_map/reduce_scatter | solution.py:1692
Sparse Core Ops, SparseCore 0:
  375.3 80.0 reduce-scatter.1
